TPU v7x, 32 devices: a whole 2x2x4 slice. The times are simulated.
32 devices in a mesh: section: 8 (over z, x), dp: 4 (over y, core).
Axes of the slice: x: 2, y: 2, z: 4, core: 2. Of those that a mesh axis runs over, the one named last changes fastest.
Arguments:
- clean_nodes: bfloat16 [8, 64, 512], P('dp'), may hold values from -6 to 6
- noise_nodes: bfloat16 [8, 64, 512], P('dp'), may hold values from -6 to 6
- edge_feats: bfloat16 [8, 64, 60, 192], P('dp'), may hold values from -6 to 6
- neighbours: int32 [8, 64, 60], P('dp'), may hold values from 0 to 63, as said below
- time_bins: int32 [8], P('dp'), may hold values from 0 to 99
- cotangent: bfloat16 [8, 64, 512], P('dp'), may hold values from -6 to 6
- pair_weight: bfloat16 [8, 512, 1024], P('section'), may hold values from -0.25 to 0.25
- message_edge: bfloat16 [8, 192, 512], P('section'), may hold values from -0.4375 to 0.4375
- message_out: bfloat16 [8, 512, 512], P('section'), may hold values from -0.25 to 0.25
- ffn_in: bfloat16 [8, 512, 2048], P('section'), may hold values from -0.25 to 0.25
- ffn_out: bfloat16 [8, 2048, 512], P('section'), may hold values from -0.125 to 0.125
- edge_pair: bfloat16 [8, 512, 384], P('section'), may hold values from -0.25 to 0.25
- edge_self: bfloat16 [8, 192, 192], P('section'), may hold values from -0.4375 to 0.4375
- edge_out: bfloat16 [8, 192, 192], P('section'), may hold values from -0.4375 to 0.4375
- norm_gain: float32 [8, 3, 512], P('section'), may hold values from 0.25 to 1.75
- norm_shift: float32 [8, 3, 512], P('section'), may hold values from -1.8 to 1.8
- node_bias: float32 [8, 3, 512], P('section'), may hold values from -1.8 to 1.8
- ffn_bias: float32 [8, 2048], P('section'), may hold values from -1.8 to 1.8
- edge_bias: float32 [8, 2, 192], P('section'), may hold values from -1.8 to 1.8
Outputs:
- activations: bfloat16 [8, 8, 64, 512], P('section', 'dp')
- input_grads: bfloat16 [8, 8, 64, 512], P('section', 'dp')
- grad_pair_weight: float32 [8, 512, 1024], P('section')
- grad_message_edge: float32 [8, 192, 512], P('section')
- grad_message_out: float32 [8, 512, 512], P('section')
- grad_ffn_in: float32 [8, 512, 2048], P('section')
- grad_ffn_out: float32 [8, 2048, 512], P('section')
- grad_edge_pair: float32 [8, 512, 384], P('section')
- grad_edge_self: float32 [8, 192, 192], P('section')
- grad_edge_out: float32 [8, 192, 192], P('section')
- grad_norm_gain: float32 [8, 3, 512], P('section')
- grad_norm_shift: float32 [8, 3, 512], P('section')
- grad_node_bias: float32 [8, 3, 512], P('section')
- grad_ffn_bias: float32 [8, 2048], P('section')
- grad_edge_bias: float32 [8, 2, 192], P('section')
Inputs may be any that keep to these rules, and one draw needn't show every extreme that they name: Each node's 60 neighbours are distinct nodes of its own protein other than itself.
All inputs are finite; a program needn't handle non-finite values.
Results may differ from a plain program's by a relative error of at most 0.029.
Values may be sent and summed in bfloat16 or wider, within the bound.
A program may use at most 192 MiB of HBM per device.

v0:
```python
import math

import jax
import jax.numpy as jnp
from jax import lax
from jax.sharding import PartitionSpec as P

TBINS = 100


def from_behind(block, axis, distance):
    devices = range(lax.axis_size(axis))
    route = [(i - distance, i) for i in devices if i - distance in devices]
    return lax.ppermute(block, axis, route)


def for_sending(value):
    return jax.tree.map(lambda a: a.astype(jnp.bfloat16) if a.dtype == jnp.float32 else a, value)


def layer_norm(value, gain, shift):
    centre = jnp.mean(value, axis=-1, keepdims=True)
    centred = value - centre
    spread = jnp.mean(centred * centred, axis=-1, keepdims=True)
    return centred * lax.rsqrt(spread + 1e-05) * gain + shift


def forward_layer(weights, hidden, edge_state, nearest):
    (
        pair_w,
        msg_edge,
        msg_out,
        ffn_w_in,
        ffn_w_out,
        edge_pair_w,
        edge_self_w,
        edge_out_w,
        gains,
        shifts,
        node_b,
        ffn_b,
        edge_b,
    ) = weights
    width = msg_out.shape[0]
    edge_width = edge_self_w.shape[0]
    normed_one = layer_norm(hidden, gains[0], shifts[0]).astype(jnp.bfloat16)
    pair_out = jnp.dot(normed_one, pair_w, preferred_element_type=jnp.float32)
    before_act = (
        pair_out[:, None, :width]
        + jnp.take(pair_out[:, width:], nearest, axis=0)
        + jnp.einsum("nkc,cd->nkd", edge_state, msg_edge, preferred_element_type=jnp.float32)
        + node_b[0]
    )
    message_act = jax.nn.gelu(before_act).astype(jnp.bfloat16)
    message_all = jnp.einsum(
        "nkc,cd->nkd", message_act, msg_out, preferred_element_type=jnp.float32
    )
    after_msg = hidden + jnp.mean(message_all, axis=1) + node_b[1]
    normed_two = layer_norm(after_msg, gains[1], shifts[1]).astype(jnp.bfloat16)
    ffn_pre = jnp.dot(normed_two, ffn_w_in, preferred_element_type=jnp.float32) + ffn_b
    ffn_act = jax.nn.gelu(ffn_pre).astype(jnp.bfloat16)
    after_ffn = (
        after_msg + jnp.dot(ffn_act, ffn_w_out, preferred_element_type=jnp.float32) + node_b[2]
    )
    normed_three = layer_norm(after_ffn, gains[2], shifts[2]).astype(jnp.bfloat16)
    edge_pairs = jnp.dot(normed_three, edge_pair_w, preferred_element_type=jnp.float32)
    edge_pre = (
        edge_pairs[:, None, :edge_width]
        + jnp.take(edge_pairs[:, edge_width:], nearest, axis=0)
        + jnp.einsum("nkc,cd->nkd", edge_state, edge_self_w, preferred_element_type=jnp.float32)
        + edge_b[0]
    )
    edge_act = jax.nn.gelu(edge_pre).astype(jnp.bfloat16)
    edge_next = (
        edge_state.astype(jnp.float32)
        + jnp.einsum("nkc,cd->nkd", edge_act, edge_out_w, preferred_element_type=jnp.float32)
        + edge_b[1]
    )
    saved = (
        normed_one,
        before_act,
        message_act,
        after_msg,
        normed_two,
        ffn_pre,
        ffn_act,
        after_ffn,
        normed_three,
        edge_pre,
        edge_act,
    )
    return (after_ffn, edge_next, saved)


def backward_layer(weights, hidden, edge_state, nearest, grad_nodes_out, grad_edges_out):
    (
        pair_w,
        msg_edge,
        msg_out,
        ffn_w_in,
        ffn_w_out,
        edge_pair_w,
        edge_self_w,
        edge_out_w,
        gains,
        shifts,
        node_b,
        ffn_b,
        edge_b,
    ) = weights
    unused_nodes, unused_edges, saved = forward_layer(weights, hidden, edge_state, nearest)
    (
        normed_one,
        before_act,
        message_act,
        after_msg,
        normed_two,
        ffn_pre,
        ffn_act,
        after_ffn,
        normed_three,
        edge_pre,
        edge_act,
    ) = saved
    width = msg_out.shape[0]
    edge_width = edge_self_w.shape[0]
    count = nearest.shape[1]
    node_count = hidden.shape[0]
    one_hot = (
        nearest.reshape(-1)[None, :] == jnp.arange(node_count, dtype=jnp.int32)[:, None]
    ).astype(jnp.bfloat16)
    edge_grad_low = grad_edges_out.astype(jnp.bfloat16)
    grad_edge_b1 = jnp.sum(grad_edges_out, axis=(0, 1))
    grad_edge_out_w = jnp.einsum(
        "nkc,nkd->cd", edge_act, edge_grad_low, preferred_element_type=jnp.float32
    )
    edge_act_grad = jnp.einsum(
        "nkd,cd->nkc", edge_grad_low, edge_out_w, preferred_element_type=jnp.float32
    )
    unused_value, gelu_edge = jax.vjp(jax.nn.gelu, edge_pre)
    edge_pre_grad = gelu_edge(edge_act_grad)[0].astype(jnp.bfloat16)
    grad_edge_b0 = jnp.sum(edge_pre_grad, axis=(0, 1), dtype=jnp.float32)
    grad_edge_self_w = jnp.einsum(
        "nkc,nkd->cd", edge_state, edge_pre_grad, preferred_element_type=jnp.float32
    )
    edge_total = grad_edges_out + jnp.einsum(
        "nkd,cd->nkc", edge_pre_grad, edge_self_w, preferred_element_type=jnp.float32
    )
    own_edge = jnp.sum(edge_pre_grad, axis=1, dtype=jnp.float32)
    other_edge = jnp.dot(
        one_hot, edge_pre_grad.reshape(-1, edge_width), preferred_element_type=jnp.float32
    )
    pairs_grad = jnp.concatenate([own_edge, other_edge], axis=-1).astype(jnp.bfloat16)
    grad_edge_pair_w = jnp.einsum(
        "nc,nd->cd", normed_three, pairs_grad, preferred_element_type=jnp.float32
    )
    normed_three_grad = jnp.einsum(
        "nd,cd->nc", pairs_grad, edge_pair_w, preferred_element_type=jnp.float32
    )
    unused_value, norm_three_back = jax.vjp(layer_norm, after_ffn, gains[2], shifts[2])
    ffn_side, gain_three, shift_three = norm_three_back(normed_three_grad)
    after_ffn_grad = grad_nodes_out + ffn_side
    grad_node_b2 = jnp.sum(after_ffn_grad, axis=0)
    ffn_out_grad = after_ffn_grad.astype(jnp.bfloat16)
    grad_ffn_w_out = jnp.einsum(
        "nc,nd->cd", ffn_act, ffn_out_grad, preferred_element_type=jnp.float32
    )
    ffn_act_grad = jnp.einsum(
        "nd,cd->nc", ffn_out_grad, ffn_w_out, preferred_element_type=jnp.float32
    )
    unused_value, gelu_ffn = jax.vjp(jax.nn.gelu, ffn_pre)
    ffn_pre_grad = gelu_ffn(ffn_act_grad)[0].astype(jnp.bfloat16)
    grad_ffn_b = jnp.sum(ffn_pre_grad, axis=0, dtype=jnp.float32)
    grad_ffn_w_in = jnp.einsum(
        "nc,nd->cd", normed_two, ffn_pre_grad, preferred_element_type=jnp.float32
    )
    normed_two_grad = jnp.einsum(
        "nd,cd->nc", ffn_pre_grad, ffn_w_in, preferred_element_type=jnp.float32
    )
    unused_value, norm_two_back = jax.vjp(layer_norm, after_msg, gains[1], shifts[1])
    msg_side, gain_two, shift_two = norm_two_back(normed_two_grad)
    after_msg_grad = after_ffn_grad + msg_side
    grad_node_b1 = jnp.sum(after_msg_grad, axis=0)
    message_grad = (after_msg_grad / count).astype(jnp.bfloat16)
    grad_msg_out = jnp.einsum(
        "nkc,nd->cd", message_act, message_grad, preferred_element_type=jnp.float32
    )
    message_act_grad = jnp.einsum(
        "nd,cd->nc", message_grad, msg_out, preferred_element_type=jnp.float32
    )
    unused_value, gelu_msg = jax.vjp(jax.nn.gelu, before_act)
    before_grad = gelu_msg(jnp.broadcast_to(message_act_grad[:, None, :], before_act.shape))[
        0
    ].astype(jnp.bfloat16)
    grad_node_b0 = jnp.sum(before_grad, axis=(0, 1), dtype=jnp.float32)
    grad_msg_edge = jnp.einsum(
        "nkc,nkd->cd", edge_state, before_grad, preferred_element_type=jnp.float32
    )
    edge_total = edge_total + jnp.einsum(
        "nkd,cd->nkc", before_grad, msg_edge, preferred_element_type=jnp.float32
    )
    own_node = jnp.sum(before_grad, axis=1, dtype=jnp.float32)
    other_node = jnp.dot(
        one_hot, before_grad.reshape(-1, width), preferred_element_type=jnp.float32
    )
    pair_grad = jnp.concatenate([own_node, other_node], axis=-1).astype(jnp.bfloat16)
    grad_pair_w = jnp.einsum("nc,nd->cd", normed_one, pair_grad, preferred_element_type=jnp.float32)
    normed_one_grad = jnp.einsum("nd,cd->nc", pair_grad, pair_w, preferred_element_type=jnp.float32)
    unused_value, norm_one_back = jax.vjp(layer_norm, hidden, gains[0], shifts[0])
    input_side, gain_one, shift_one = norm_one_back(normed_one_grad)
    hidden_grad = after_msg_grad + input_side
    grads = (
        grad_pair_w,
        grad_msg_edge,
        grad_msg_out,
        grad_ffn_w_in,
        grad_ffn_w_out,
        grad_edge_pair_w,
        grad_edge_self_w,
        grad_edge_out_w,
        jnp.stack([gain_one, gain_two, gain_three]),
        jnp.stack([shift_one, shift_two, shift_three]),
        jnp.stack([grad_node_b0, grad_node_b1, grad_node_b2]),
        grad_ffn_b,
        jnp.stack([grad_edge_b0, grad_edge_b1]),
    )
    return (hidden_grad.astype(jnp.bfloat16), edge_total.astype(jnp.bfloat16), grads)


def on_device(
    clean_nodes,
    noise_nodes,
    edge_feats,
    neighbours,
    time_bins,
    cotangent,
    pair_weight,
    message_edge,
    message_out,
    ffn_in,
    ffn_out,
    edge_pair,
    edge_self,
    edge_out,
    norm_gain,
    norm_shift,
    node_bias,
    ffn_bias,
    edge_bias,
):
    sections = lax.axis_size("section")
    place = lax.axis_index("section")
    weights = tuple(
        (
            item[0]
            for item in (
                pair_weight,
                message_edge,
                message_out,
                ffn_in,
                ffn_out,
                edge_pair,
                edge_self,
                edge_out,
                norm_gain,
                norm_shift,
                node_bias,
                ffn_bias,
                edge_bias,
            )
        )
    )
    batches, node_count, width = clean_nodes.shape
    phase = (time_bins.astype(jnp.float32) + 0.5) * (math.pi * 0.5 / TBINS)
    start = jnp.cos(phase)[:, None, None] * clean_nodes.astype(jnp.float32) + jnp.sin(phase)[
        :, None, None
    ] * noise_nodes.astype(jnp.float32)
    zero_nodes = jnp.zeros((node_count, width), jnp.bfloat16)
    zero_edges = jnp.zeros(edge_feats.shape[1:], jnp.bfloat16)
    is_first = place == 0
    is_last = place == sections - 1

    def forward_step(step_index, carry):
        recv_nodes, recv_edges, back_nodes, kept_nodes, kept_edges, section_outs = carry
        item = step_index - place
        first_pass = (item >= 0) & (item < batches)
        second_pass = (item >= sections) & (item < sections + batches)
        index = jnp.clip(jnp.where(second_pass, item - sections, item), 0, batches - 1)
        predicted = back_nodes
        own_start = lax.dynamic_index_in_dim(start, index, 0, keepdims=False)
        lead_nodes = own_start + jnp.where(second_pass, predicted.astype(jnp.float32), 0.0)
        nodes_in = jnp.where(is_first, lead_nodes, recv_nodes.astype(jnp.float32))
        edges_in = jnp.where(
            is_first, lax.dynamic_index_in_dim(edge_feats, index, 0, keepdims=False), recv_edges
        )
        nearest = lax.dynamic_index_in_dim(neighbours, index, 0, keepdims=False)

        def run_layer(operand):
            after, edge_next, saved = forward_layer(weights, operand[0], operand[1], operand[2])
            return (after.astype(jnp.bfloat16), edge_next.astype(jnp.bfloat16))

        def skip_layer(operand):
            return (zero_nodes, zero_edges)

        out_nodes, out_edges = lax.cond(
            first_pass | second_pass, run_layer, skip_layer, (nodes_in, edges_in, nearest)
        )
        kept_nodes = lax.dynamic_update_index_in_dim(
            kept_nodes, jnp.where(second_pass, nodes_in, kept_nodes[index]), index, 0
        )
        kept_edges = lax.dynamic_update_index_in_dim(
            kept_edges, jnp.where(second_pass, edges_in, kept_edges[index]), index, 0
        )
        section_outs = lax.dynamic_update_index_in_dim(
            section_outs, jnp.where(second_pass, out_nodes, section_outs[index]), index, 0
        )
        recv_nodes, recv_edges = from_behind((out_nodes, out_edges), "section", 1)
        back_nodes = from_behind(out_nodes, "section", 1 - sections)
        return (recv_nodes, recv_edges, back_nodes, kept_nodes, kept_edges, section_outs)

    forward_init = (
        zero_nodes,
        zero_edges,
        zero_nodes,
        jnp.zeros((batches, node_count, width), jnp.float32),
        jnp.zeros_like(edge_feats),
        jnp.zeros((batches, node_count, width), jnp.bfloat16),
    )
    unused_nodes, unused_edges, unused_back, kept_nodes, kept_edges, section_outs = lax.fori_loop(
        0, 2 * sections + batches - 1, forward_step, forward_init
    )
    grads_zero = tuple((jnp.zeros(item.shape, jnp.float32) for item in weights))

    def backward_step(step_index, carry):
        recv_grad_nodes, recv_grad_edges, grads, input_grads = carry
        item = step_index - (sections - 1 - place)
        live = (item >= 0) & (item < batches)
        index = jnp.clip(item, 0, batches - 1)
        nodes_grad_out = jnp.where(
            is_last,
            lax.dynamic_index_in_dim(cotangent, index, 0, keepdims=False).astype(jnp.float32),
            recv_grad_nodes.astype(jnp.float32),
        )
        edges_grad_out = jnp.where(is_last, 0.0, recv_grad_edges.astype(jnp.float32))
        nearest = lax.dynamic_index_in_dim(neighbours, index, 0, keepdims=False)

        def run_back(operand):
            return backward_layer(
                weights, operand[0], operand[1], operand[2], operand[3], operand[4]
            )

        def skip_back(operand):
            return (zero_nodes, zero_edges, grads_zero)

        nodes_grad, edges_grad, terms = lax.cond(
            live,
            run_back,
            skip_back,
            (kept_nodes[index], kept_edges[index], nearest, nodes_grad_out, edges_grad_out),
        )
        grads = tuple((total + term for total, term in zip(grads, terms)))
        input_grads = lax.dynamic_update_index_in_dim(
            input_grads, jnp.where(live, nodes_grad, input_grads[index]), index, 0
        )
        recv_grad_nodes, recv_grad_edges = from_behind((nodes_grad, edges_grad), "section", -1)
        return (recv_grad_nodes, recv_grad_edges, grads, input_grads)

    backward_init = (
        zero_nodes,
        zero_edges,
        grads_zero,
        jnp.zeros((batches, node_count, width), jnp.bfloat16),
    )
    unused_grad_nodes, unused_grad_edges, grads, input_grads = lax.fori_loop(
        0, sections + batches - 1, backward_step, backward_init
    )
    totals = jax.tree.map(lambda part: part.astype(jnp.float32), lax.psum(for_sending(grads), "dp"))
    return (
        section_outs[None],
        input_grads[None],
        totals[0][None],
        totals[1][None],
        totals[2][None],
        totals[3][None],
        totals[4][None],
        totals[5][None],
        totals[6][None],
        totals[7][None],
        totals[8][None],
        totals[9][None],
        totals[10][None],
        totals[11][None],
        totals[12][None],
    )


def solution(mesh):
    placed = (
        P("dp", None, None),
        P("dp", None, None),
        P("dp", None, None, None),
        P("dp", None, None),
        P("dp"),
        P("dp", None, None),
        P("section", None, None),
        P("section", None, None),
        P("section", None, None),
        P("section", None, None),
        P("section", None, None),
        P("section", None, None),
        P("section", None, None),
        P("section", None, None),
        P("section", None, None),
        P("section", None, None),
        P("section", None, None),
        P("section", None),
        P("section", None, None),
    )
    return jax.shard_map(
        on_device,
        mesh=mesh,
        in_specs=placed,
        out_specs=(
            P("section", "dp", None, None),
            P("section", "dp", None, None),
            P("section", None, None),
            P("section", None, None),
            P("section", None, None),
            P("section", None, None),
            P("section", None, None),
            P("section", None, None),
            P("section", None, None),
            P("section", None, None),
            P("section", None, None),
            P("section", None, None),
            P("section", None, None),
            P("section", None),
            P("section", None, None),
        ),
        check_vma=False,
    )
```

profile of v0, /device:TPU:0, one launch (start us, length us, event | category | flops | bytes accessed | tf_op | source)
XLA Modules:
  0.0 4026.3 jit_solution(3147807647702575206)
XLA Ops:
  20.1 2056.8 %while.71 = (s32[]{:T(128)}, bf16[64,512]{1,0:T(8,128)(2,1)}, bf16[64,60,192]{2,0,1:T(8,128)(2,1)}, bf16[64,512]{1,0:T(8,128)(2,1)}, f32[2,64,512]{2,1,0:T(8,128...) while((s32[]{:T(128)}, bf16[64,512]{1,0:T(8,128)(2,1)}, ...), condition=%wide.region_10.13_spmd, body=%wide.region_0.12_spmd.sunk | while | flops 3739331072 | bytes 93114960 | solution.py:329
  29.5 70.5 %conditional.5 = (bf16[64,512]{1,0:T(8,128)(2,1)}, bf16[64,60,192]{2,0,1:T(8,128)(2,1)}) conditional(s32[]{:T(128)} %convert_element_type.400, () %tuple.173, (f32[64,512]{1,0:T(8,128)S(1)}, f32[3,512]{1,0:T(4,128)}, f32[3,512]{1,0:T(4,128)}, bf16[512,1024]{1,0:T(8,128)(2,1)S(1)}, s32[2,64,60]{2,1,0:T(8,128)}, /*index=5*/s32[]{:T(128)}, ...), branch_computations={%region_1.1_spmd, %region_2.11_spmd} | conditional | flops 3737627136 | bytes 70043920 | solution.py:305
  106.7 39.3 collective-permute-done
  156.2 70.5 %conditional.5 = (bf16[64,512]{1,0:T(8,128)(2,1)}, bf16[64,60,192]{2,0,1:T(8,128)(2,1)}) conditional(s32[]{:T(128)} %convert_element_type.400, () %tuple.173, (f32[64,512]{1,0:T(8,128)S(1)}, f32[3,512]{1,0:T(4,128)}, f32[3,512]{1,0:T(4,128)}, bf16[512,1024]{1,0:T(8,128)(2,1)S(1)}, s32[2,64,60]{2,1,0:T(8,128)}, /*index=5*/s32[]{:T(128)}, ...), branch_computations={%region_1.1_spmd, %region_2.11_spmd} | conditional | flops 3737627136 | bytes 70043920 | solution.py:305
  236.9 38.4 collective-permute-done
  287.7 74.5 %collective-permute-start.1 = (bf16[64,60,192]{2,0,1:T(8,128)(2,1)}, bf16[64,60,192]{2,0,1:T(8,128)(2,1)}, u32[]{:S(2)}, u32[]{:S(2)}) collective-permute-start(bf16[64,60,192]{2,0,1:T(8,128)(2,1)} %get-tuple-element.2525), channel_id=1, source_target_pairs={{0,4},{4,8},{8,12},{12,16},{16,20},{20,24},{24,28},{1,5},{5,9},{9,... | collective-permute-start | bytes 4423688 | tf_op jit(solution)/shard_map/while/body/eval_jaxpr/ppermute | solution.py:14
  366.7 37.2 collective-permute-done
  422.4 71.3 %collective-permute-start = (bf16[64,512]{1,0:T(8,128)(2,1)}, bf16[64,512]{1,0:T(8,128)(2,1)S(1)}, u32[]{:S(2)}, u32[]{:S(2)}) collective-permute-start(bf16[64,512]{1,0:T(8,128)(2,1)} %get-tuple-element.2524), channel_id=1, source_target_pairs={{0,4},{4,8},{8,12},{12,16},{16,20},{20,24},{24,28},{1,5},{5,9},{9,... | collective-permute-start | bytes 196616 | tf_op jit(solution)/shard_map/while/body/eval_jaxpr/ppermute | solution.py:14
  515.1 35.4 collective-permute-start.1
  557.2 33.6 collective-permute-done
  603.2 37.3 collective-permute-start.1
  640.5 38.5 collective-permute-start
  700.4 33.9 collective-permute-start.1
  734.3 36.1 collective-permute-start
  791.7 34.4 collective-permute-start.1
  826.1 37.1 collective-permute-start
  866.0 136.8 %collective-permute-done.2 = bf16[64,512]{1,0:T(8,128)(2,1)S(1)} collective-permute-done((bf16[64,512]{1,0:T(8,128)(2,1)}, bf16[64,512]{1,0:T(8,128)(2,1)S(1)}, u32[]{:S(2)}, u32[]{:S(2)}) %collective-permute-start.2) | collective-permute-done | bytes 65568 | tf_op jit(solution)/shard_map/while/body/eval_jaxpr/ppermute | solution.py:14
  1012.9 70.5 %conditional.5 = (bf16[64,512]{1,0:T(8,128)(2,1)}, bf16[64,60,192]{2,0,1:T(8,128)(2,1)}) conditional(s32[]{:T(128)} %convert_element_type.400, () %tuple.173, (f32[64,512]{1,0:T(8,128)S(1)}, f32[3,512]{1,0:T(4,128)}, f32[3,512]{1,0:T(4,128)}, bf16[512,1024]{1,0:T(8,128)(2,1)S(1)}, s32[2,64,60]{2,1,0:T(8,128)}, /*index=5*/s32[]{:T(128)}, ...), branch_computations={%region_1.1_spmd, %region_2.11_spmd} | conditional | flops 3737627136 | bytes 70043920 | solution.py:305
  1090.9 33.9 collective-permute-done
  1139.8 70.5 %conditional.5 = (bf16[64,512]{1,0:T(8,128)(2,1)}, bf16[64,60,192]{2,0,1:T(8,128)(2,1)}) conditional(s32[]{:T(128)} %convert_element_type.400, () %tuple.173, (f32[64,512]{1,0:T(8,128)S(1)}, f32[3,512]{1,0:T(4,128)}, f32[3,512]{1,0:T(4,128)}, bf16[512,1024]{1,0:T(8,128)(2,1)S(1)}, s32[2,64,60]{2,1,0:T(8,128)}, /*index=5*/s32[]{:T(128)}, ...), branch_computations={%region_1.1_spmd, %region_2.11_spmd} | conditional | flops 3737627136 | bytes 70043920 | solution.py:305
  1217.9 33.1 collective-permute-done
  1263.3 74.5 %collective-permute-start.1 = (bf16[64,60,192]{2,0,1:T(8,128)(2,1)}, bf16[64,60,192]{2,0,1:T(8,128)(2,1)}, u32[]{:S(2)}, u32[]{:S(2)}) collective-permute-start(bf16[64,60,192]{2,0,1:T(8,128)(2,1)} %get-tuple-element.2525), channel_id=1, source_target_pairs={{0,4},{4,8},{8,12},{12,16},{16,20},{20,24},{24,28},{1,5},{5,9},{9,... | collective-permute-start | bytes 4423688 | tf_op jit(solution)/shard_map/while/body/eval_jaxpr/ppermute | solution.py:14
  1341.9 33.1 collective-permute-done
  1393.5 70.1 %collective-permute-start = (bf16[64,512]{1,0:T(8,128)(2,1)}, bf16[64,512]{1,0:T(8,128)(2,1)S(1)}, u32[]{:S(2)}, u32[]{:S(2)}) collective-permute-start(bf16[64,512]{1,0:T(8,128)(2,1)} %get-tuple-element.2524), channel_id=1, source_target_pairs={{0,4},{4,8},{8,12},{12,16},{16,20},{20,24},{24,28},{1,5},{5,9},{9,... | collective-permute-start | bytes 196616 | tf_op jit(solution)/shard_map/while/body/eval_jaxpr/ppermute | solution.py:14
  1485.0 30.8 collective-permute-start.1
  1522.5 29.0 collective-permute-done
  1563.9 41.9 %collective-permute-start.1 = (bf16[64,60,192]{2,0,1:T(8,128)(2,1)}, bf16[64,60,192]{2,0,1:T(8,128)(2,1)}, u32[]{:S(2)}, u32[]{:S(2)}) collective-permute-start(bf16[64,60,192]{2,0,1:T(8,128)(2,1)} %get-tuple-element.2525), channel_id=1, source_target_pairs={{0,4},{4,8},{8,12},{12,16},{16,20},{20,24},{24,28},{1,5},{5,9},{9,... | collective-permute-start | bytes 4423688 | tf_op jit(solution)/shard_map/while/body/eval_jaxpr/ppermute | solution.py:14
  1605.8 33.9 collective-permute-start
  1661.0 29.4 collective-permute-start.1
  1690.4 40.4 %collective-permute-start = (bf16[64,512]{1,0:T(8,128)(2,1)}, bf16[64,512]{1,0:T(8,128)(2,1)S(1)}, u32[]{:S(2)}, u32[]{:S(2)}) collective-permute-start(bf16[64,512]{1,0:T(8,128)(2,1)} %get-tuple-element.2524), channel_id=1, source_target_pairs={{0,4},{4,8},{8,12},{12,16},{16,20},{20,24},{24,28},{1,5},{5,9},{9,... | collective-permute-start | bytes 196616 | tf_op jit(solution)/shard_map/while/body/eval_jaxpr/ppermute | solution.py:14
  1752.2 29.8 collective-permute-start.1
  1781.9 32.5 collective-permute-start
  1817.2 136.7 %collective-permute-done.2 = bf16[64,512]{1,0:T(8,128)(2,1)S(1)} collective-permute-done((bf16[64,512]{1,0:T(8,128)(2,1)}, bf16[64,512]{1,0:T(8,128)(2,1)S(1)}, u32[]{:S(2)}, u32[]{:S(2)}) %collective-permute-start.2) | collective-permute-done | bytes 65568 | tf_op jit(solution)/shard_map/while/body/eval_jaxpr/ppermute | solution.py:14
  1972.9 30.1 collective-permute-done
  2003.0 73.2 %collective-permute-done.2 = bf16[64,512]{1,0:T(8,128)(2,1)S(1)} collective-permute-done((bf16[64,512]{1,0:T(8,128)(2,1)}, bf16[64,512]{1,0:T(8,128)(2,1)S(1)}, u32[]{:S(2)}, u32[]{:S(2)}) %collective-permute-start.2) | collective-permute-done | bytes 65568 | tf_op jit(solution)/shard_map/while/body/eval_jaxpr/ppermute | solution.py:14
  2079.6 1792.8 %while.72 = (s32[]{:T(128)}, bf16[64,512]{1,0:T(8,128)(2,1)}, bf16[64,60,192]{2,0,1:T(8,128)(2,1)}, f32[512,1024]{1,0:T(8,128)}, f32[192,512]{1,0:T(8,128)}, /*i...) while((s32[]{:T(128)}, bf16[64,512]{1,0:T(8,128)(2,1)}, ...), condition=%wide.region_42.45_spmd.clone, body=%wide.region_11.44_spmd.clone.sunk | while | flops 7317364736 | bytes 385552448 | solution.py:374
  2103.3 15.9 conditional.6
  2160.0 15.9 conditional.6
  2216.5 15.9 conditional.6
  2273.3 15.9 conditional.6
  2330.0 15.9 conditional.6
  2386.5 15.9 conditional.6
  2436.5 33.4 collective-permute-done.4
  2517.0 931.7 %collective-permute-done.3 = bf16[64,512]{1,0:T(8,128)(2,1)S(1)} collective-permute-done((bf16[64,512]{1,0:T(8,128)(2,1)}, bf16[64,512]{1,0:T(8,128)(2,1)S(1)}, u32[]{:S(2)}, u32[]{:S(2)}) %collective-permute-start.3) | collective-permute-done | bytes 65568 | tf_op jit(solution)/shard_map/while/body/eval_jaxpr/ppermute | solution.py:14
  3448.7 33.4 collective-permute-done.4
  3482.9 152.5 %conditional.6 = (bf16[64,512]{1,0:T(8,128)(2,1)}, bf16[64,60,192]{2,0,1:T(8,128)(2,1)}, f32[512,1024]{1,0:T(8,128)}, f32[192,512]{1,0:T(8,128)}, f32[512,512]{1...) conditional(s32[]{:T(128)} %convert_element_type.401, ...), branch_computations={%region_12.14_spmd, %region_13.43_spmd} | conditional | flops 7310813696 | bytes 300404384 | solution.py:355
  3677.0 152.5 %conditional.6 = (bf16[64,512]{1,0:T(8,128)(2,1)}, bf16[64,60,192]{2,0,1:T(8,128)(2,1)}, f32[512,1024]{1,0:T(8,128)}, f32[192,512]{1,0:T(8,128)}, f32[512,512]{1...) conditional(s32[]{:T(128)} %convert_element_type.401, ...), branch_computations={%region_12.14_spmd, %region_13.43_spmd} | conditional | flops 7310813696 | bytes 300404384 | solution.py:355
  3897.6 108.9 %all-reduce.4.cloned.1.call-done = (bf16[1,512,1024]{2,1,0:T(8,128)(2,1)}, bf16[1,192,512]{2,1,0:T(8,128)(2,1)}, bf16[1,512,512]{2,1,0:T(8,128)(2,1)}, bf16[1,51...) async-done(((bf16[1,512,1024]{2,1,0:T(8,128)(2,1)}, ...) | async-done | bytes 6504464 | tf_op jit(solution)/shard_map/psum | solution.py:377
  (1823 shorter events, 1480.7 us)
Async XLA Ops:
  7.2 3999.3 %all-reduce.4.cloned.1.call-start = ((), (), s32[]{:S(2)}) async-start(), calls=%async_computation | async-start | bytes 13107200 | tf_op jit(solution)/shard_map/psum | solution.py:377
  100.0 46.0 %collective-permute-start.1 = (bf16[64,60,192]{2,0,1:T(8,128)(2,1)}, bf16[64,60,192]{2,0,1:T(8,128)(2,1)}, u32[]{:S(2)}, u32[]{:S(2)}) collective-permute-start(bf16[64,60,192]{2,0,1:T(8,128)(2,1)} %get-tuple-element.2525), channel_id=1, source_target_pairs={{0,4},{4,8},{8,12},{12,16},{16,20},{20,24},{24,28},{1,5},{5,9},{9,... | collective-permute-start | bytes 4423688 | tf_op jit(solution)/shard_map/while/body/eval_jaxpr/ppermute | solution.py:14
  102.6 43.4 %collective-permute-start = (bf16[64,512]{1,0:T(8,128)(2,1)}, bf16[64,512]{1,0:T(8,128)(2,1)S(1)}, u32[]{:S(2)}, u32[]{:S(2)}) collective-permute-start(bf16[64,512]{1,0:T(8,128)(2,1)} %get-tuple-element.2524), channel_id=1, source_target_pairs={{0,4},{4,8},{8,12},{12,16},{16,20},{20,24},{24,28},{1,5},{5,9},{9,... | collective-permute-start | bytes 196616 | tf_op jit(solution)/shard_map/while/body/eval_jaxpr/ppermute | solution.py:14
  103.9 42.1 %collective-permute-start.2 = (bf16[64,512]{1,0:T(8,128)(2,1)}, bf16[64,512]{1,0:T(8,128)(2,1)S(1)}, u32[]{:S(2)}, u32[]{:S(2)}) collective-permute-start(bf16[64,512]{1,0:T(8,128)(2,1)} %get-tuple-element.2524), channel_id=1, source_target_pairs={{28,0},{29,1},{30,2},{31,3}} | collective-permute-start | bytes 196616 | tf_op jit(solution)/shard_map/while/body/eval_jaxpr/ppermute | solution.py:14
  226.7 48.7 %collective-permute-start.1 = (bf16[64,60,192]{2,0,1:T(8,128)(2,1)}, bf16[64,60,192]{2,0,1:T(8,128)(2,1)}, u32[]{:S(2)}, u32[]{:S(2)}) collective-permute-start(bf16[64,60,192]{2,0,1:T(8,128)(2,1)} %get-tuple-element.2525), channel_id=1, source_target_pairs={{0,4},{4,8},{8,12},{12,16},{16,20},{20,24},{24,28},{1,5},{5,9},{9,... | collective-permute-start | bytes 4423688 | tf_op jit(solution)/shard_map/while/body/eval_jaxpr/ppermute | solution.py:14
  232.8 42.5 %collective-permute-start = (bf16[64,512]{1,0:T(8,128)(2,1)}, bf16[64,512]{1,0:T(8,128)(2,1)S(1)}, u32[]{:S(2)}, u32[]{:S(2)}) collective-permute-start(bf16[64,512]{1,0:T(8,128)(2,1)} %get-tuple-element.2524), channel_id=1, source_target_pairs={{0,4},{4,8},{8,12},{12,16},{16,20},{20,24},{24,28},{1,5},{5,9},{9,... | collective-permute-start | bytes 196616 | tf_op jit(solution)/shard_map/while/body/eval_jaxpr/ppermute | solution.py:14
  234.1 41.2 %collective-permute-start.2 = (bf16[64,512]{1,0:T(8,128)(2,1)}, bf16[64,512]{1,0:T(8,128)(2,1)S(1)}, u32[]{:S(2)}, u32[]{:S(2)}) collective-permute-start(bf16[64,512]{1,0:T(8,128)(2,1)} %get-tuple-element.2524), channel_id=1, source_target_pairs={{28,0},{29,1},{30,2},{31,3}} | collective-permute-start | bytes 196616 | tf_op jit(solution)/shard_map/while/body/eval_jaxpr/ppermute | solution.py:14
  287.7 116.3 %collective-permute-start.1 = (bf16[64,60,192]{2,0,1:T(8,128)(2,1)}, bf16[64,60,192]{2,0,1:T(8,128)(2,1)}, u32[]{:S(2)}, u32[]{:S(2)}) collective-permute-start(bf16[64,60,192]{2,0,1:T(8,128)(2,1)} %get-tuple-element.2525), channel_id=1, source_target_pairs={{0,4},{4,8},{8,12},{12,16},{16,20},{20,24},{24,28},{1,5},{5,9},{9,... | collective-permute-start | bytes 4423688 | tf_op jit(solution)/shard_map/while/body/eval_jaxpr/ppermute | solution.py:14
  362.2 41.7 %collective-permute-start = (bf16[64,512]{1,0:T(8,128)(2,1)}, bf16[64,512]{1,0:T(8,128)(2,1)S(1)}, u32[]{:S(2)}, u32[]{:S(2)}) collective-permute-start(bf16[64,512]{1,0:T(8,128)(2,1)} %get-tuple-element.2524), channel_id=1, source_target_pairs={{0,4},{4,8},{8,12},{12,16},{16,20},{20,24},{24,28},{1,5},{5,9},{9,... | collective-permute-start | bytes 196616 | tf_op jit(solution)/shard_map/while/body/eval_jaxpr/ppermute | solution.py:14
  363.9 40.0 collective-permute-start.2
  416.2 86.6 %collective-permute-start.1 = (bf16[64,60,192]{2,0,1:T(8,128)(2,1)}, bf16[64,60,192]{2,0,1:T(8,128)(2,1)}, u32[]{:S(2)}, u32[]{:S(2)}) collective-permute-start(bf16[64,60,192]{2,0,1:T(8,128)(2,1)} %get-tuple-element.2525), channel_id=1, source_target_pairs={{0,4},{4,8},{8,12},{12,16},{16,20},{20,24},{24,28},{1,5},{5,9},{9,... | collective-permute-start | bytes 4423688 | tf_op jit(solution)/shard_map/while/body/eval_jaxpr/ppermute | solution.py:14
  422.4 74.1 %collective-permute-start = (bf16[64,512]{1,0:T(8,128)(2,1)}, bf16[64,512]{1,0:T(8,128)(2,1)S(1)}, u32[]{:S(2)}, u32[]{:S(2)}) collective-permute-start(bf16[64,512]{1,0:T(8,128)(2,1)} %get-tuple-element.2524), channel_id=1, source_target_pairs={{0,4},{4,8},{8,12},{12,16},{16,20},{20,24},{24,28},{1,5},{5,9},{9,... | collective-permute-start | bytes 196616 | tf_op jit(solution)/shard_map/while/body/eval_jaxpr/ppermute | solution.py:14
  515.1 75.8 %collective-permute-start.1 = (bf16[64,60,192]{2,0,1:T(8,128)(2,1)}, bf16[64,60,192]{2,0,1:T(8,128)(2,1)}, u32[]{:S(2)}, u32[]{:S(2)}) collective-permute-start(bf16[64,60,192]{2,0,1:T(8,128)(2,1)} %get-tuple-element.2525), channel_id=1, source_target_pairs={{0,4},{4,8},{8,12},{12,16},{16,20},{20,24},{24,28},{1,5},{5,9},{9,... | collective-permute-start | bytes 4423688 | tf_op jit(solution)/shard_map/while/body/eval_jaxpr/ppermute | solution.py:14
  550.5 40.3 %collective-permute-start = (bf16[64,512]{1,0:T(8,128)(2,1)}, bf16[64,512]{1,0:T(8,128)(2,1)S(1)}, u32[]{:S(2)}, u32[]{:S(2)}) collective-permute-start(bf16[64,512]{1,0:T(8,128)(2,1)} %get-tuple-element.2524), channel_id=1, source_target_pairs={{0,4},{4,8},{8,12},{12,16},{16,20},{20,24},{24,28},{1,5},{5,9},{9,... | collective-permute-start | bytes 196616 | tf_op jit(solution)/shard_map/while/body/eval_jaxpr/ppermute | solution.py:14
  603.2 84.9 %collective-permute-start.1 = (bf16[64,60,192]{2,0,1:T(8,128)(2,1)}, bf16[64,60,192]{2,0,1:T(8,128)(2,1)}, u32[]{:S(2)}, u32[]{:S(2)}) collective-permute-start(bf16[64,60,192]{2,0,1:T(8,128)(2,1)} %get-tuple-element.2525), channel_id=1, source_target_pairs={{0,4},{4,8},{8,12},{12,16},{16,20},{20,24},{24,28},{1,5},{5,9},{9,... | collective-permute-start | bytes 4423688 | tf_op jit(solution)/shard_map/while/body/eval_jaxpr/ppermute | solution.py:14
  640.5 41.3 %collective-permute-start = (bf16[64,512]{1,0:T(8,128)(2,1)}, bf16[64,512]{1,0:T(8,128)(2,1)S(1)}, u32[]{:S(2)}, u32[]{:S(2)}) collective-permute-start(bf16[64,512]{1,0:T(8,128)(2,1)} %get-tuple-element.2524), channel_id=1, source_target_pairs={{0,4},{4,8},{8,12},{12,16},{16,20},{20,24},{24,28},{1,5},{5,9},{9,... | collective-permute-start | bytes 196616 | tf_op jit(solution)/shard_map/while/body/eval_jaxpr/ppermute | solution.py:14
  700.4 79.1 %collective-permute-start.1 = (bf16[64,60,192]{2,0,1:T(8,128)(2,1)}, bf16[64,60,192]{2,0,1:T(8,128)(2,1)}, u32[]{:S(2)}, u32[]{:S(2)}) collective-permute-start(bf16[64,60,192]{2,0,1:T(8,128)(2,1)} %get-tuple-element.2525), channel_id=1, source_target_pairs={{0,4},{4,8},{8,12},{12,16},{16,20},{20,24},{24,28},{1,5},{5,9},{9,... | collective-permute-start | bytes 4423688 | tf_op jit(solution)/shard_map/while/body/eval_jaxpr/ppermute | solution.py:14
  734.3 38.9 collective-permute-start
  791.7 211.0 %collective-permute-start.1 = (bf16[64,60,192]{2,0,1:T(8,128)(2,1)}, bf16[64,60,192]{2,0,1:T(8,128)(2,1)}, u32[]{:S(2)}, u32[]{:S(2)}) collective-permute-start(bf16[64,60,192]{2,0,1:T(8,128)(2,1)} %get-tuple-element.2525), channel_id=1, source_target_pairs={{0,4},{4,8},{8,12},{12,16},{16,20},{20,24},{24,28},{1,5},{5,9},{9,... | collective-permute-start | bytes 4423688 | tf_op jit(solution)/shard_map/while/body/eval_jaxpr/ppermute | solution.py:14
  826.1 39.9 collective-permute-start
  863.2 139.6 %collective-permute-start.2 = (bf16[64,512]{1,0:T(8,128)(2,1)}, bf16[64,512]{1,0:T(8,128)(2,1)S(1)}, u32[]{:S(2)}, u32[]{:S(2)}) collective-permute-start(bf16[64,512]{1,0:T(8,128)(2,1)} %get-tuple-element.2524), channel_id=1, source_target_pairs={{28,0},{29,1},{30,2},{31,3}} | collective-permute-start | bytes 196616 | tf_op jit(solution)/shard_map/while/body/eval_jaxpr/ppermute | solution.py:14
  1083.4 46.3 %collective-permute-start.1 = (bf16[64,60,192]{2,0,1:T(8,128)(2,1)}, bf16[64,60,192]{2,0,1:T(8,128)(2,1)}, u32[]{:S(2)}, u32[]{:S(2)}) collective-permute-start(bf16[64,60,192]{2,0,1:T(8,128)(2,1)} %get-tuple-element.2525), channel_id=1, source_target_pairs={{0,4},{4,8},{8,12},{12,16},{16,20},{20,24},{24,28},{1,5},{5,9},{9,... | collective-permute-start | bytes 4423688 | tf_op jit(solution)/shard_map/while/body/eval_jaxpr/ppermute | solution.py:14
  1086.0 38.8 collective-permute-start
  1087.3 42.4 %collective-permute-start.2 = (bf16[64,512]{1,0:T(8,128)(2,1)}, bf16[64,512]{1,0:T(8,128)(2,1)S(1)}, u32[]{:S(2)}, u32[]{:S(2)}) collective-permute-start(bf16[64,512]{1,0:T(8,128)(2,1)} %get-tuple-element.2524), channel_id=1, source_target_pairs={{28,0},{29,1},{30,2},{31,3}} | collective-permute-start | bytes 196616 | tf_op jit(solution)/shard_map/while/body/eval_jaxpr/ppermute | solution.py:14
  1210.3 40.6 %collective-permute-start.1 = (bf16[64,60,192]{2,0,1:T(8,128)(2,1)}, bf16[64,60,192]{2,0,1:T(8,128)(2,1)}, u32[]{:S(2)}, u32[]{:S(2)}) collective-permute-start(bf16[64,60,192]{2,0,1:T(8,128)(2,1)} %get-tuple-element.2525), channel_id=1, source_target_pairs={{0,4},{4,8},{8,12},{12,16},{16,20},{20,24},{24,28},{1,5},{5,9},{9,... | collective-permute-start | bytes 4423688 | tf_op jit(solution)/shard_map/while/body/eval_jaxpr/ppermute | solution.py:14
  1212.9 38.0 collective-permute-start
  1263.3 111.7 %collective-permute-start.1 = (bf16[64,60,192]{2,0,1:T(8,128)(2,1)}, bf16[64,60,192]{2,0,1:T(8,128)(2,1)}, u32[]{:S(2)}, u32[]{:S(2)}) collective-permute-start(bf16[64,60,192]{2,0,1:T(8,128)(2,1)} %get-tuple-element.2525), channel_id=1, source_target_pairs={{0,4},{4,8},{8,12},{12,16},{16,20},{20,24},{24,28},{1,5},{5,9},{9,... | collective-permute-start | bytes 4423688 | tf_op jit(solution)/shard_map/while/body/eval_jaxpr/ppermute | solution.py:14
  1337.8 37.2 collective-permute-start
  1387.3 85.4 %collective-permute-start.1 = (bf16[64,60,192]{2,0,1:T(8,128)(2,1)}, bf16[64,60,192]{2,0,1:T(8,128)(2,1)}, u32[]{:S(2)}, u32[]{:S(2)}) collective-permute-start(bf16[64,60,192]{2,0,1:T(8,128)(2,1)} %get-tuple-element.2525), channel_id=1, source_target_pairs={{0,4},{4,8},{8,12},{12,16},{16,20},{20,24},{24,28},{1,5},{5,9},{9,... | collective-permute-start | bytes 4423688 | tf_op jit(solution)/shard_map/while/body/eval_jaxpr/ppermute | solution.py:14
  1393.5 72.9 %collective-permute-start = (bf16[64,512]{1,0:T(8,128)(2,1)}, bf16[64,512]{1,0:T(8,128)(2,1)S(1)}, u32[]{:S(2)}, u32[]{:S(2)}) collective-permute-start(bf16[64,512]{1,0:T(8,128)(2,1)} %get-tuple-element.2524), channel_id=1, source_target_pairs={{0,4},{4,8},{8,12},{12,16},{16,20},{20,24},{24,28},{1,5},{5,9},{9,... | collective-permute-start | bytes 196616 | tf_op jit(solution)/shard_map/while/body/eval_jaxpr/ppermute | solution.py:14
  1485.0 66.5 %collective-permute-start.1 = (bf16[64,60,192]{2,0,1:T(8,128)(2,1)}, bf16[64,60,192]{2,0,1:T(8,128)(2,1)}, u32[]{:S(2)}, u32[]{:S(2)}) collective-permute-start(bf16[64,60,192]{2,0,1:T(8,128)(2,1)} %get-tuple-element.2525), channel_id=1, source_target_pairs={{0,4},{4,8},{8,12},{12,16},{16,20},{20,24},{24,28},{1,5},{5,9},{9,... | collective-permute-start | bytes 4423688 | tf_op jit(solution)/shard_map/while/body/eval_jaxpr/ppermute | solution.py:14
  1563.9 84.9 %collective-permute-start.1 = (bf16[64,60,192]{2,0,1:T(8,128)(2,1)}, bf16[64,60,192]{2,0,1:T(8,128)(2,1)}, u32[]{:S(2)}, u32[]{:S(2)}) collective-permute-start(bf16[64,60,192]{2,0,1:T(8,128)(2,1)} %get-tuple-element.2525), channel_id=1, source_target_pairs={{0,4},{4,8},{8,12},{12,16},{16,20},{20,24},{24,28},{1,5},{5,9},{9,... | collective-permute-start | bytes 4423688 | tf_op jit(solution)/shard_map/while/body/eval_jaxpr/ppermute | solution.py:14
  1661.0 78.8 %collective-permute-start.1 = (bf16[64,60,192]{2,0,1:T(8,128)(2,1)}, bf16[64,60,192]{2,0,1:T(8,128)(2,1)}, u32[]{:S(2)}, u32[]{:S(2)}) collective-permute-start(bf16[64,60,192]{2,0,1:T(8,128)(2,1)} %get-tuple-element.2525), channel_id=1, source_target_pairs={{0,4},{4,8},{8,12},{12,16},{16,20},{20,24},{24,28},{1,5},{5,9},{9,... | collective-permute-start | bytes 4423688 | tf_op jit(solution)/shard_map/while/body/eval_jaxpr/ppermute | solution.py:14
  1690.4 43.2 %collective-permute-start = (bf16[64,512]{1,0:T(8,128)(2,1)}, bf16[64,512]{1,0:T(8,128)(2,1)S(1)}, u32[]{:S(2)}, u32[]{:S(2)}) collective-permute-start(bf16[64,512]{1,0:T(8,128)(2,1)} %get-tuple-element.2524), channel_id=1, source_target_pairs={{0,4},{4,8},{8,12},{12,16},{16,20},{20,24},{24,28},{1,5},{5,9},{9,... | collective-permute-start | bytes 196616 | tf_op jit(solution)/shard_map/while/body/eval_jaxpr/ppermute | solution.py:14
  1752.2 201.8 %collective-permute-start.1 = (bf16[64,60,192]{2,0,1:T(8,128)(2,1)}, bf16[64,60,192]{2,0,1:T(8,128)(2,1)}, u32[]{:S(2)}, u32[]{:S(2)}) collective-permute-start(bf16[64,60,192]{2,0,1:T(8,128)(2,1)} %get-tuple-element.2525), channel_id=1, source_target_pairs={{0,4},{4,8},{8,12},{12,16},{16,20},{20,24},{24,28},{1,5},{5,9},{9,... | collective-permute-start | bytes 4423688 | tf_op jit(solution)/shard_map/while/body/eval_jaxpr/ppermute | solution.py:14
  1814.4 139.5 %collective-permute-start.2 = (bf16[64,512]{1,0:T(8,128)(2,1)}, bf16[64,512]{1,0:T(8,128)(2,1)S(1)}, u32[]{:S(2)}, u32[]{:S(2)}) collective-permute-start(bf16[64,512]{1,0:T(8,128)(2,1)} %get-tuple-element.2524), channel_id=1, source_target_pairs={{28,0},{29,1},{30,2},{31,3}} | collective-permute-start | bytes 196616 | tf_op jit(solution)/shard_map/while/body/eval_jaxpr/ppermute | solution.py:14
  1966.2 110.0 %collective-permute-start.1 = (bf16[64,60,192]{2,0,1:T(8,128)(2,1)}, bf16[64,60,192]{2,0,1:T(8,128)(2,1)}, u32[]{:S(2)}, u32[]{:S(2)}) collective-permute-start(bf16[64,60,192]{2,0,1:T(8,128)(2,1)} %get-tuple-element.2525), channel_id=1, source_target_pairs={{0,4},{4,8},{8,12},{12,16},{16,20},{20,24},{24,28},{1,5},{5,9},{9,... | collective-permute-start | bytes 4423688 | tf_op jit(solution)/shard_map/while/body/eval_jaxpr/ppermute | solution.py:14
  1970.1 106.1 %collective-permute-start.2 = (bf16[64,512]{1,0:T(8,128)(2,1)}, bf16[64,512]{1,0:T(8,128)(2,1)S(1)}, u32[]{:S(2)}, u32[]{:S(2)}) collective-permute-start(bf16[64,512]{1,0:T(8,128)(2,1)} %get-tuple-element.2524), channel_id=1, source_target_pairs={{28,0},{29,1},{30,2},{31,3}} | collective-permute-start | bytes 196616 | tf_op jit(solution)/shard_map/while/body/eval_jaxpr/ppermute | solution.py:14
  2120.5 38.7 collective-permute-start.4
  2177.2 38.5 collective-permute-start.4
  2233.7 38.9 collective-permute-start.4
  2290.6 38.7 collective-permute-start.4
  2347.2 38.5 collective-permute-start.4
  2403.7 66.2 %collective-permute-start.4 = (bf16[64,60,192]{2,0,1:T(8,128)(2,1)}, bf16[64,60,192]{2,0,1:T(8,128)(2,1)}, u32[]{:S(2)}, u32[]{:S(2)}) collective-permute-start(bf16[64,60,192]{2,0,1:T(8,128)(2,1)} %get-tuple-element.2565), channel_id=1, source_target_pairs={{4,0},{8,4},{12,8},{16,12},{20,16},{24,20},{28,24},{5,1},{9,5},{13... | collective-permute-start | bytes 4423688 | tf_op jit(solution)/shard_map/while/body/eval_jaxpr/ppermute | solution.py:14
  2486.6 962.1 %collective-permute-start.3 = (bf16[64,512]{1,0:T(8,128)(2,1)}, bf16[64,512]{1,0:T(8,128)(2,1)S(1)}, u32[]{:S(2)}, u32[]{:S(2)}) collective-permute-start(bf16[64,512]{1,0:T(8,128)(2,1)} %get-tuple-element.2564), channel_id=1, source_target_pairs={{4,0},{8,4},{12,8},{16,12},{20,16},{24,20},{28,24},{5,1},{9,5},{13... | collective-permute-start | bytes 196616 | tf_op jit(solution)/shard_map/while/body/eval_jaxpr/ppermute | solution.py:14
  2487.9 994.2 %collective-permute-start.4 = (bf16[64,60,192]{2,0,1:T(8,128)(2,1)}, bf16[64,60,192]{2,0,1:T(8,128)(2,1)}, u32[]{:S(2)}, u32[]{:S(2)}) collective-permute-start(bf16[64,60,192]{2,0,1:T(8,128)(2,1)} %get-tuple-element.2565), channel_id=1, source_target_pairs={{4,0},{8,4},{12,8},{16,12},{20,16},{24,20},{28,24},{5,1},{9,5},{13... | collective-permute-start | bytes 4423688 | tf_op jit(solution)/shard_map/while/body/eval_jaxpr/ppermute | solution.py:14
  3636.7 39.6 collective-permute-start.4
  3830.8 38.7 collective-permute-start.4
  (536 other events, 5950.9 us)
Sparse Core Ops, SparseCore 0:
  3883.7 122.7 all-reduce.3
where the time goes:
time: 4050 us; the launch traced here: 4030 us
  waiting for transfers between devices  1880 us (46%)
  starting transfers between devices  873 us (22%)
  local copies, waits for them, and re-layouts  551 us (14%)
  other arithmetic  436 us (11%)
  matrix products  232 us (6%)
    ppermute x69, waiting for transfers between devices, from_behind(): return lax.ppermute(block, axis, route)  1770 us
    ppermute x69, starting transfers between devices, from_behind(): return lax.ppermute(block, axis, route)  873 us
    add x99, other arithmetic, backward_step(): grads = tuple((total + term for total, term in zip(grads, terms)))  219 us
    gather x12, local copies, waits for them, and re-layouts, forward_layer(): jnp.take(pair_out[:, width:], nearest, axis=0)  116 us
    psum x1, waiting for transfers between devices, on_device(): lax.psum(for_sending(grads), 'dp')  109 us
    dynamic_update_slice x17, other arithmetic, forward_step(): lax.dynamic_update_index_in_dim(kept_edges, jnp.where(second_pass, edges_...  97 us
    gather x12, local copies, waits for them, and re-layouts, forward_layer(): jnp.take(edge_pairs[:, edge_width:], nearest, axis=0)  89.8 us
  transfers between devices with their start and end apart: 70, of which 31 were waited for; matrix products, arithmetic and copies ran while one was open for 7% of the time, Pallas kernels for 0%

commit v1 on v0

--- a/solution.py
+++ b/solution.py
@@ -1,8 +1,11 @@
+import functools
 import math
 
 import jax
 import jax.numpy as jnp
 from jax import lax
+from jax.experimental import pallas as pl
+from jax.experimental.pallas import tpu as pltpu
 from jax.sharding import PartitionSpec as P
 
 TBINS = 100
@@ -394,7 +397,1030 @@
     )
 
 
+BF16 = jnp.bfloat16
+F32 = jnp.float32
+MESH = pl.DeviceIdType.MESH
+GELU_A = 0.7978845608028654
+GELU_B = 0.044715
+
+
+def gelu(x):
+    return 0.5 * x * (1.0 + jnp.tanh(x * (GELU_A + (GELU_A * GELU_B) * (x * x))))
+
+
+def gelu_both(x):
+    square = x * x
+    t = jnp.tanh(x * (GELU_A + (GELU_A * GELU_B) * square))
+    half = 0.5 * (1.0 + t)
+    slope = half + (0.5 * x) * (1.0 - t * t) * (GELU_A + (3.0 * GELU_A * GELU_B) * square)
+    return x * half, slope
+
+
+def mm(a, b):
+    return jnp.dot(a, b, preferred_element_type=F32)
+
+
+def mm_bt(a, b):
+    return lax.dot_general(a, b, (((1,), (1,)), ((), ())), preferred_element_type=F32)
+
+
+def mm_at(a, b):
+    return lax.dot_general(a, b, (((0,), (0,)), ((), ())), preferred_element_type=F32)
+
+
+def stacked(blocks):
+    return jnp.concatenate(blocks, axis=0)
+
+
+def row_mean(x):
+    return jnp.mean(x, axis=-1, keepdims=True)
+
+
+def normed(x):
+    centred = x - row_mean(x)
+    scale = lax.rsqrt(row_mean(centred * centred) + 1e-05)
+    return centred * scale, scale
+
+
+def norm_back(grad, unit, scale, gain):
+    t = grad * gain
+    return scale * (t - row_mean(t) - unit * row_mean(t * unit))
+
+
+def col_sum(x):
+    return jnp.sum(x, axis=0, keepdims=True)
+
+
+def relay_kernel(
+    dims,
+    ecat0, oht, mix, clean, noise, cot, pw, mo, fi, fo, ep, gains, shifts, node_b, fb, edge_b, we_own, ws_own, wo_own,
+    act, ig, g_fwd, g_bwd, g_dpq, g_small, g_edge,
+    start, par, eb0, wall, fwd, bwd, sg, eg, eg_r, eg_b, eg_o, eg_f, wo, eb1,
+    ecat, wcat, scat, pwn, parn, hin_r, hst, mb_s, mb_r, pq_s, pq_r, rq_s, rq_r,
+    un0, un1, un2, hi_s, sc0, sc1, sc2, sci, u_s, slope_s, de, dacc, gp, gpe, dcat, act_t, edge_t,
+    x_s, x_r, row_s, row_r, dpqo_r, dmb_s, dmb_r, dh1_s, dh1_r, dh1_f, dh2_s, dn3_s, da2_s, h1_s, a1_s,
+    ld_sem, nx_ss, nx_rs, hop_ss, hop_rs,
+    pq_ss, pq_rs, ag_ss, ag_rs, rq_ss, rq_rs, ag2_ss, ag2_rs,
+    mb_ss, mb_rs, x_ss, x_rs, row_ss, row_rs, dpqo_rs, fw_ss, dmb_ss, dmb_rs, dh_ss, dh_rs,
+    e1_ss, e1_rs, e2_ss, e2_rs, g_ss, g_rs, ring_ss, ring_rs, sib_ss, sib_rs,
+):
+    S, B, N, K, Q, D, DE, EP, FF, C = dims
+    BN = B * N
+    RB = 16
+    top = DE + N
+    me_s = lax.axis_index("section")
+    me_d = lax.axis_index("dp")
+    core = lax.rem(me_d, 2)
+    pair = me_d - core
+    w = lax.div(me_s, 2)
+    q = 2 * lax.rem(me_s, 2) + core
+    owner_d = pair + lax.div(w, B)
+    slot = lax.rem(w, B)
+    my_row = pl.multiple_of(slot * N + q * Q, Q)
+    own_rows = pl.ds(top, Q)
+
+    def quarter(j):
+        return pl.ds(pl.multiple_of(DE + j * Q, Q), Q)
+
+    def is_me(sec, dpi):
+        return (sec == me_s) & (dpi == me_d)
+
+    def far(src, dst, ssem, rsem, sec, dpi):
+        return pltpu.make_async_remote_copy(
+            src_ref=src, dst_ref=dst, send_sem=ssem, recv_sem=rsem,
+            device_id={"section": sec, "dp": dpi}, device_id_type=MESH,
+        )
+
+    def push(src, dst, ssem, rsem, sec, dpi):
+        lax.cond(
+            is_me(sec, dpi),
+            lambda: pltpu.make_async_copy(src, dst, rsem).start(),
+            lambda: far(src, dst, ssem, rsem, sec, dpi).start(),
+        )
+
+    def arrive(ref, sem):
+        pltpu.make_async_copy(ref, ref, sem).wait()
+
+    def drain(ref, sem, sec, dpi):
+        @pl.when(jnp.logical_not(is_me(sec, dpi)))
+        def _():
+            arrive(ref, sem)
+
+    def worker_of(p, j):
+        return 2 * (core * B + p) + j // 2, pair + j % 2
+
+    def peer(k):
+        j = lax.rem(q + k, 4)
+        return j, 2 * w + lax.div(j, 2), pair + lax.rem(j, 2)
+
+    works_here = lax.div(w, B) == core
+
+    pairs = [(p, j) for p in range(B) for j in range(4)]
+
+    load = pltpu.make_async_copy(ecat0, ecat.at[0], ld_sem)
+    load.start()
+    barrier = pltpu.get_barrier_semaphore()
+    for sec in range(S):
+        for c in range(C):
+            near = (c == pair) | (c == pair + 1) | (w == sec // 2)
+
+            @pl.when(near & jnp.logical_not(is_me(sec, c)))
+            def _():
+                pl.semaphore_signal(
+                    barrier, inc=1, device_id={"section": sec, "dp": c}, device_id_type=MESH
+                )
+    W = D + 2 * EP
+    H = wall.shape[1] // 2
+    wall[me_s] = jnp.zeros((2 * H, W), BF16)
+    wall[me_s, pl.ds(0, DE), pl.ds(0, D)] = we_own[...]
+    wall[me_s, pl.ds(0, DE), pl.ds(D, DE)] = ws_own[...]
+    wall[me_s, pl.ds(0, DE), pl.ds(D + EP, DE)] = wo_own[...]
+    bias = edge_b[pl.ds(1, 1), :]
+    high = bias.astype(BF16).astype(F32)
+    row = lax.broadcasted_iota(jnp.int32, (16, DE), 0)
+    wall[me_s, pl.ds(DE, 16), pl.ds(0, DE)] = jnp.where(
+        row == 0, high, jnp.where(row == 1, bias - high, 0.0)
+    ).astype(BF16)
+    eb0[...] = jnp.zeros_like(eb0)
+    eb0[:, pl.ds(0, DE)] = edge_b[pl.ds(0, 1), :]
+    par[pl.ds(0, 1), :] = gains[0]
+    par[pl.ds(1, 1), :] = shifts[0]
+    par[pl.ds(2, 1), :] = node_b[0]
+    par[pl.ds(3, 5), :] = jnp.zeros((5, D), F32)
+    pl.semaphore_wait(barrier, 2 * S - 1 + 2 * (C - 2))
+
+    def section_at(i):
+        i = lax.rem(i + S, S)
+        return jnp.where(i < S // 2, 2 * i, 2 * (S - i) - 1)
+
+    place = jnp.where(lax.rem(me_s, 2) == 0, w, S - 1 - w)
+    mine = pl.ds(pl.multiple_of(core * H, H), H)
+    theirs = pl.ds(pl.multiple_of((1 - core) * H, H), H)
+    sides = ((section_at(place + 1), S // 2), (section_at(place - 1), S // 2 - 1))
+
+    def ring_send(layer, side, hop):
+        sec, reach = sides[side]
+        if hop < reach:
+            half = wall.at[layer, mine]
+            far(half, half, ring_ss.at[side, hop], ring_rs.at[layer], sec, me_d).start()
+
+    for side in range(2):
+        ring_send(me_s, side, 0)
+    before = lax.rem(me_s + S - 1, S)
+    far(pw, pwn, nx_ss.at[0], nx_rs.at[0], before, me_d).start()
+    far(par, parn, nx_ss.at[1], nx_rs.at[1], before, me_d).start()
+
+    for p in range(B):
+        rows = pl.ds(p * N, N)
+        start[rows, :] = mix[0, p] * clean[rows, :].astype(F32) + mix[1, p] * noise[rows, :].astype(F32)
+
+    def ring():
+        for hop in range(1, S // 2 + 1):
+            for side in range(2):
+                if hop <= sides[side][1]:
+                    layer = section_at(place - hop if side == 0 else place + hop)
+                    half = wall.at[layer, mine]
+                    arrive(half, ring_rs.at[layer])
+                    ring_send(layer, side, hop)
+                    far(half, half, sib_ss.at[layer], sib_rs.at[layer], me_s, pair + 1 - core).start()
+
+    def ring_drain():
+        for side in range(2):
+            for hop in range(sides[side][1]):
+                arrive(wall.at[me_s, mine], ring_ss.at[side, hop])
+        for layer in range(S):
+            @pl.when(layer != me_s)
+            def _():
+                arrive(wall.at[layer, mine], sib_ss.at[layer])
+
+    def unpack(t):
+        @pl.when(t != me_s)
+        def _():
+            arrive(wall.at[t, theirs], sib_rs.at[t])
+
+        wcat[t, pl.ds(0, DE), :] = wall[t, pl.ds(0, DE), pl.ds(0, D)]
+        scat[t, pl.ds(0, DE), :] = wall[t, pl.ds(0, DE), pl.ds(D, EP)]
+        wo[t, pl.ds(0, DE), :] = wall[t, pl.ds(0, DE), pl.ds(D + EP, EP)]
+        wo[t, pl.ds(DE, N), :] = jnp.zeros((N, EP), BF16)
+        eb1[t] = wall[t, pl.ds(DE, 16), pl.ds(0, EP)]
+
+    def rows_out(src, dst, ssem, rsem):
+        for p, j in pairs:
+            sec, dpi = worker_of(p, j)
+            push(src.at[pl.ds(p * N + j * Q, Q)], dst, ssem, rsem, sec, dpi)
+
+    def rows_drain(src, ssem):
+        lax.cond(
+            works_here,
+            lambda: arrive(src.at[pl.ds(0, B * N - Q)], ssem),
+            lambda: arrive(src, ssem),
+        )
+
+    def spread(rows, half, ref, layer, ssem, rsem, rows_sem):
+        arrive(rows, rows_sem)
+        for k in range(1, 4):
+            _, sec, dpi = peer(k)
+            far(rows.at[:, pl.ds(half, half)], ref.at[layer, quarter(q)], ssem, rsem, sec, dpi).start()
+        ref[layer, own_rows, :] = rows[:, pl.ds(0, half)]
+        ref[layer, quarter(q), :] = rows[:, pl.ds(half, half)]
+
+    def spread_wait(ref, layer, sem):
+        arrive(ref.at[layer, pl.ds(DE, 3 * Q)], sem)
+
+    def share(group, src, dst):
+        for c in range(C):
+            push(src, dst.at[me_d], g_ss.at[group, c], g_rs.at[group, me_d], me_s, c)
+
+    def share_wait(group, src, dst):
+        for c in range(C):
+            arrive(dst.at[c], g_rs.at[group, c])
+            drain(src, g_ss.at[group, c], me_s, c)
+
+    steps = 4
+    KC = K // steps
+    RC = KC * Q
+
+    def messages(t):
+        own = wcat[t, own_rows, :].astype(F32)
+        total = jnp.zeros((Q, D), F32)
+        for i in range(steps):
+            pre = mm(ecat[t, pl.ds(i * RC, RC), :], wcat[t, pl.ds(0, top), :])
+            for k in range(KC):
+                total = total + gelu(pre[k * Q : (k + 1) * Q] + own)
+        mb_s[...] = (total * (1.0 / K)).astype(BF16)
+
+    def edge_update(t):
+        own = scat[t, own_rows, :].astype(F32)
+        bias = eb1[t, pl.ds(0, 1), :].astype(F32) + eb1[t, pl.ds(1, 1), :].astype(F32)
+        for i in range(steps):
+            pe = mm(ecat[t, pl.ds(i * RC, RC), :], scat[t, pl.ds(0, top), :])
+            act_e = stacked([gelu(pe[k * Q : (k + 1) * Q] + own).astype(BF16) for k in range(KC)])
+            z = mm(act_e, wo[t])
+            for k in range(KC):
+                rows = pl.ds(i * RC + k * Q, Q)
+                ecat[t + 1, rows, :] = (ecat[t, rows, :].astype(F32) + z[k * Q : (k + 1) * Q] + bias).astype(BF16)
+
+    chunks = 4
+    FC = FF // chunks
+
+    def node_forward(step):
+        @pl.when(step < S)
+        def _():
+            arrive(pwn, nx_rs.at[0])
+            arrive(parn, nx_rs.at[1])
+            arrive(pw, nx_ss.at[0])
+            arrive(par, nx_ss.at[1])
+
+        @pl.when(step == 0)
+        def _():
+            hi_s[...] = start[...]
+
+        @pl.when(step > 0)
+        def _():
+            arrive(hin_r, hop_rs)
+            first = jnp.where(me_s == 0, 1.0, 0.0)
+            for i in range(0, BN, RB):
+                rows = pl.ds(i, RB)
+                hi_s[rows, :] = hin_r[rows, :].astype(F32) + first * start[rows, :]
+
+        arrive(mb_r, mb_rs)
+        mean = mm(mb_r[...], mo[...])
+        for i in range(0, BN, RB):
+            rows = pl.ds(i, RB)
+            h1 = hi_s[rows, :] + mean[i : i + RB] + node_b[1]
+            h1_s[rows, :] = h1
+            unit, scale = normed(h1)
+            un1[rows, :] = unit
+            sc1[rows, :] = scale
+            fwd[rows, pl.ds(2 * D, D)] = (unit * gains[1] + shifts[1]).astype(BF16)
+            fwd[rows, pl.ds(D, D)] = mb_r[rows, :]
+        a2 = fwd[:, pl.ds(2 * D, D)]
+        y = jnp.zeros((BN, D), F32)
+        for c in range(chunks):
+            cols = pl.ds(c * FC, FC)
+            u = mm(a2, fi[:, cols])
+            v = []
+            for i in range(0, BN, RB):
+                rows = pl.ds(i, RB)
+                block = u[i : i + RB] + fb[:, cols]
+                u_s[rows, cols] = block
+                v.append(gelu(block).astype(BF16))
+            y = y + mm(stacked(v), fo[cols, :])
+        last = jnp.where(me_s == S - 1, 1.0, 0.0)
+        for i in range(0, BN, RB):
+            rows = pl.ds(i, RB)
+            h2 = h1_s[rows, :] + y[i : i + RB] + node_b[2]
+            rounded = h2.astype(BF16)
+            hst[rows, :] = rounded
+            unit, scale = normed(h2)
+            un2[rows, :] = unit
+            sc2[rows, :] = scale
+            fwd[rows, pl.ds(3 * D, D)] = (unit * gains[2] + shifts[2]).astype(BF16)
+            pair_norm(rows, rounded.astype(F32) + last * start[rows, :], parn)
+        rq = mm(fwd[:, pl.ds(3 * D, D)], ep[...])
+        for i in range(0, BN, RB):
+            rows = pl.ds(i, RB)
+            rq_s[rows, pl.ds(0, EP)] = (rq[i : i + RB, :EP] + eb0[...]).astype(BF16)
+            rq_s[rows, pl.ds(EP, EP)] = rq[i : i + RB, EP:].astype(BF16)
+        pair_rows(pwn, parn)
+        later = lax.rem(me_s + 1, S)
+
+        @pl.when(me_s < S - 1)
+        def _():
+            rows_out(rq_s, rq_r, rq_ss, rq_rs)
+
+        @pl.when(step < 2 * S - 1)
+        def _():
+            rows_out(pq_s, pq_r, pq_ss, pq_rs)
+            far(hst, hin_r, hop_ss, hop_rs, later, me_d).start()
+
+        @pl.when(step >= S)
+        def _():
+            act[...] = hst[...]
+            for i in range(0, BN, RB):
+                rows = pl.ds(i, RB)
+                unit, scale = normed(hi_s[rows, :])
+                hi_s[rows, :] = unit
+                sci[rows, :] = scale
+                fwd[rows, pl.ds(0, D)] = (unit * gains[0] + shifts[0]).astype(BF16)
+                for c in range(chunks):
+                    cols = pl.ds(c * FC, FC)
+                    slope_s[rows, cols] = gelu_both(u_s[rows, cols])[1].astype(BF16)
+            share(0, fwd, g_fwd)
+
+    def pair_norm(rows, hidden, first):
+        unit, scale = normed(hidden)
+        un0[rows, :] = unit
+        sc0[rows, :] = scale
+        a1_s[rows, :] = (unit * first[pl.ds(0, 1), :] + first[pl.ds(1, 1), :]).astype(BF16)
+
+    def pair_rows(weight, first):
+        for half in range(2):
+            cols = pl.ds(half * D, D)
+            value = mm(a1_s[...], weight[:, cols])
+            if half == 0:
+                value = value + first[pl.ds(2, 1), :]
+            pq_s[:, cols] = value.astype(BF16)
+
+    def node_forward_drain():
+        arrive(hst, hop_ss)
+        rows_drain(pq_s, pq_ss)
+
+        @pl.when(me_s < S - 1)
+        def _():
+            rows_drain(rq_s, rq_ss)
+
+    @pl.when(me_s == 0)
+    def _():
+        for i in range(0, BN, RB):
+            rows = pl.ds(i, RB)
+            pair_norm(rows, start[rows, :], par)
+        pair_rows(pw, par)
+        rows_out(pq_s, pq_r, pq_ss, pq_rs)
+
+    def message_slope(t):
+        own = wcat[t, own_rows, :].astype(F32)
+        for i in range(steps):
+            pre = mm(ecat[t, pl.ds(i * RC, RC), :], wcat[t, pl.ds(0, top), :])
+            for k in range(KC):
+                gp[t, pl.ds(i * RC + k * Q, Q), :] = gelu_both(pre[k * Q : (k + 1) * Q] + own)[1].astype(BF16)
+
+    def edge_slope(t):
+        own = scat[t, own_rows, :].astype(F32)
+        values = []
+        for i in range(steps):
+            pe = mm(ecat[t, pl.ds(i * RC, RC), :], scat[t, pl.ds(0, top), :])
+            for k in range(KC):
+                value, slope = gelu_both(pe[k * Q : (k + 1) * Q] + own)
+                values.append(value.astype(BF16))
+                gpe[t, pl.ds(i * RC + k * Q, Q), :] = slope.astype(BF16)
+        act_t[t] = stacked(values).T
+
+    def prepare(t):
+        message_slope(t)
+        edge_t[t] = ecat[t].T
+
+        @pl.when(t > 0)
+        def _():
+            edge_slope(t - 1)
+
+    def forward_step(step, carry):
+        t = lax.rem(step, S)
+
+        @pl.when(step < S)
+        def _():
+            unpack(t)
+
+        spread_wait(wcat, t, ag_rs)
+        messages(t)
+        spread_wait(wcat, t, ag_ss)
+        push(mb_s, mb_r.at[pl.ds(my_row, Q)], mb_ss, mb_rs, t, owner_d)
+
+        @pl.when((step == 0) & (me_s == 0))
+        def _():
+            rows_drain(pq_s, pq_ss)
+
+        @pl.when((step > 0) & (me_s == lax.rem(step + S - 1, S)))
+        def _():
+            node_forward_drain()
+
+        @pl.when(me_s == t)
+        def _():
+            node_forward(step)
+
+        @pl.when((me_s != t) & (step >= S))
+        def _():
+            prepare(t)
+
+        @pl.when(t < S - 1)
+        def _():
+            spread(rq_r, EP, scat, t, ag2_ss, ag2_rs, rq_rs)
+
+        @pl.when(step < 2 * S - 1)
+        def _():
+            spread(pq_r, D, wcat, lax.rem(step + 1, S), ag_ss, ag_rs, pq_rs)
+
+        @pl.when(t < S - 1)
+        def _():
+            spread_wait(scat, t, ag2_rs)
+            edge_update(t)
+            spread_wait(scat, t, ag2_ss)
+
+        drain(mb_s, mb_ss, t, owner_d)
+        return carry
+
+    ring()
+    load.wait()
+    spread(pq_r, D, wcat, 0, ag_ss, ag_rs, pq_rs)
+    lax.fori_loop(0, 2 * S, forward_step, 0)
+    ring_drain()
+
+    def edge_back(t):
+        b2, n2 = lax.rem(t, 2), lax.rem(t + 1, 2)
+        total = jnp.zeros((Q, EP), F32)
+        for i in range(steps):
+            chunk = pl.ds(i * RC, RC)
+            carry = mm_bt(dcat[b2, chunk, pl.ds(0, D)], wcat[t, pl.ds(0, top), :])
+            low = []
+            for k in range(KC):
+                rows = pl.ds(i * RC + k * Q, Q)
+                low.append((dacc[rows, :] + carry[k * Q : (k + 1) * Q]).astype(BF16))
+                de[n2, rows, :] = low[-1]
+            dw = mm_bt(stacked(low), wo[t - 1])
+            for k in range(KC):
+                rows = pl.ds(i * RC + k * Q, Q)
+                d = (gpe[t - 1, rows, :].astype(F32) * dw[k * Q : (k + 1) * Q]).astype(BF16)
+                total = total + d.astype(F32)
+                dcat[n2, rows, pl.ds(D, EP)] = d
+        row_s[:, pl.ds(2 * D, EP)] = total.astype(BF16)
+        x_s[:, pl.ds(D, EP)] = mm(oht[...], dcat[n2, :, pl.ds(D, EP)]).astype(BF16)
+
+    def edge_pass(t):
+        b3 = lax.rem(t, 2)
+        for i in range(steps):
+            rows = pl.ds(i * RC, RC)
+            d = dcat[b3, rows, pl.ds(D, EP)]
+            dacc[rows, :] = de[b3, rows, :].astype(F32) + mm_bt(d, scat[t, pl.ds(0, top), :])
+
+    blocks = 2 * C
+    BW = (D + 2 * EP) // blocks
+    my_block = lax.rem(me_s, 2) * C + me_d
+    my_cols = pl.ds(pl.multiple_of(my_block * BW, BW), BW)
+
+    def edge_grads(t):
+        b3 = lax.rem(t, 2)
+
+        @pl.when(t < S - 1)
+        def _():
+            eg[t, pl.ds(0, DE), pl.ds(0, D + EP)] = mm(edge_t[t, pl.ds(0, DE), :], dcat[b3]).astype(BF16)
+            eg[t, pl.ds(0, DE), pl.ds(D + EP, EP)] = mm(act_t[t, pl.ds(0, DE), :], de[b3]).astype(BF16)
+            bias = jnp.sum(de[b3].astype(F32), axis=0, keepdims=True)
+            eg[t, pl.ds(DE, 16), pl.ds(0, EP)] = jnp.broadcast_to(bias, (16, EP)).astype(BF16)
+
+        @pl.when(t == S - 1)
+        def _():
+            eg[t, pl.ds(0, DE), pl.ds(0, D)] = mm(edge_t[t, pl.ds(0, DE), :], dcat[b3, :, pl.ds(0, D)]).astype(BF16)
+            eg[t, pl.ds(0, DE), pl.ds(D, 2 * EP)] = jnp.zeros((DE, 2 * EP), BF16)
+            eg[t, pl.ds(DE, 16), pl.ds(0, EP)] = jnp.zeros((16, EP), BF16)
+
+        eg[t, pl.ds(DE, 16), pl.ds(EP, D + EP)] = jnp.zeros((16, D + EP), BF16)
+        for k in range(blocks):
+            @pl.when(k != my_block)
+            def _():
+                far(
+                    eg.at[t, :, pl.ds(k * BW, BW)], eg_r.at[t, my_block], e1_ss.at[t, k], e1_rs.at[t, my_block],
+                    2 * w + k // C, k % C,
+                ).start()
+
+    def edge_grads_sum(t):
+        eg_r[t, my_block] = eg[t, :, my_cols]
+        for k in range(blocks):
+            @pl.when(k != my_block)
+            def _():
+                arrive(eg_r.at[t, k], e1_rs.at[t, k])
+                arrive(eg.at[t, :, pl.ds(k * BW, BW)], e1_ss.at[t, k])
+        total = eg_r[t, 0].astype(F32)
+        for k in range(1, blocks):
+            total = total + eg_r[t, k].astype(F32)
+        eg_b[t] = total.astype(BF16)
+        push(eg_b.at[t], eg_o.at[me_s], e2_ss.at[t], e2_rs.at[me_s], t, me_d)
+
+    def gather_blocks():
+        for k in range(1, 4):
+            j, sec, dpi = peer(k)
+            rows = pl.ds(pl.multiple_of(j * Q, Q), Q)
+            far(x_s.at[rows], x_r.at[q], x_ss, x_rs, sec, dpi).start()
+        x_r[q] = x_s[pl.ds(pl.multiple_of(q * Q, Q), Q), :]
+
+    def gather_wait():
+        arrive(x_r.at[pl.ds(0, 3)], x_rs)
+        arrive(x_s.at[pl.ds(0, 3 * Q)], x_ss)
+        total = x_r[0].astype(F32)
+        for j in range(1, 4):
+            total = total + x_r[j].astype(F32)
+        return total
+
+    def message_back(t):
+        b2 = lax.rem(t, 2)
+        dm = dmb_r[...].astype(F32)
+        total = jnp.zeros((Q, D), F32)
+        for k in range(K):
+            rows = pl.ds(k * Q, Q)
+            d = (gp[t, rows, :].astype(F32) * dm).astype(BF16)
+            total = total + d.astype(F32)
+            dcat[b2, rows, pl.ds(0, D)] = d
+        row_s[:, pl.ds(0, D)] = total.astype(BF16)
+        x_s[:, pl.ds(0, D)] = mm(oht[...], dcat[b2, :, pl.ds(0, D)]).astype(BF16)
+
+    def node_backward():
+        @pl.when(me_s < S - 1)
+        def _():
+            arrive(dh1_r, dh_rs)
+            arrive(row_r, row_rs)
+            dn0 = mm_bt(row_r[:, pl.ds(0, 2 * D)], pwn[...])
+            dn3 = mm_bt(row_r[:, pl.ds(2 * D, 2 * EP)], ep[...])
+            for i in range(0, BN, RB):
+                rows = pl.ds(i, RB)
+                dn = dn3[i : i + RB]
+                dn3_s[rows, :] = dn
+                first = norm_back(dn0[i : i + RB], un0[rows, :], sc0[rows, :], parn[pl.ds(0, 1), :])
+                dh = (dh1_r[rows, :].astype(F32) + first).astype(BF16).astype(F32)
+                dh2_s[rows, :] = dh + norm_back(dn, un2[rows, :], sc2[rows, :], gains[2])
+
+        @pl.when(me_s == S - 1)
+        def _():
+            dh2_s[...] = cot[...].astype(F32)
+
+        dy = stacked([dh2_s[pl.ds(i, RB), :].astype(BF16) for i in range(0, BN, RB)])
+        bwd[:, pl.ds(D, D)] = dy
+        da2 = jnp.zeros((BN, D), F32)
+        for c in range(chunks):
+            cols = pl.ds(c * FC, FC)
+            dv = mm_bt(dy, fo[cols, :])
+            du = stacked(
+                [(slope_s[pl.ds(i, RB), cols].astype(F32) * dv[i : i + RB]).astype(BF16) for i in range(0, BN, RB)]
+            )
+            da2 = da2 + mm_bt(du, fi[:, cols])
+        for i in range(0, BN, RB):
+            rows = pl.ds(i, RB)
+            block = da2[i : i + RB]
+            da2_s[rows, :] = block
+            dh1 = dh2_s[rows, :] + norm_back(block, un1[rows, :], sc1[rows, :], gains[1])
+            dh1_f[rows, :] = dh1
+            bwd[rows, pl.ds(0, D)] = (dh1 * (1.0 / K)).astype(BF16)
+        dmb_s[...] = mm_bt(bwd[:, pl.ds(0, D)], mo[...]).astype(BF16)
+        rows_out(dmb_s, dmb_r, dmb_ss, dmb_rs)
+
+        @pl.when(me_s > 0)
+        def _():
+            dh1_s[...] = dh1_f[...].astype(BF16)
+            far(dh1_s, dh1_r, dh_ss, dh_rs, me_s - 1, me_d).start()
+
+        @pl.when(me_s < S - 1)
+        def _():
+            far(row_r.at[:, pl.ds(0, 2 * D)], dpqo_r, fw_ss, dpqo_rs, me_s + 1, me_d).start()
+            drs = row_r[:, pl.ds(2 * D, 2 * EP)]
+            bwd[:, pl.ds(2 * D, 2 * EP)] = drs
+            dn = dn3_s[...]
+            sg[pl.ds(11, 1), :] = col_sum(dn * un2[...])
+            sg[pl.ds(12, 1), :] = col_sum(dn)
+            sg[pl.ds(16, 1), pl.ds(0, EP)] = col_sum(drs[:, :EP].astype(F32))
+
+        @pl.when(me_s == S - 1)
+        def _():
+            bwd[:, pl.ds(2 * D, 2 * EP)] = jnp.zeros((B * N, 2 * EP), BF16)
+            sg[pl.ds(11, 1), :] = jnp.zeros((1, D), F32)
+            sg[pl.ds(12, 1), :] = jnp.zeros((1, D), F32)
+            sg[pl.ds(16, 1), pl.ds(0, EP)] = jnp.zeros((1, EP), F32)
+
+        share(1, bwd, g_bwd)
+        sg[pl.ds(13, 1), :] = col_sum(dh2_s[...])
+        sg[pl.ds(8, 1), :] = col_sum(da2_s[...] * un1[...])
+        sg[pl.ds(9, 1), :] = col_sum(da2_s[...])
+        sg[pl.ds(10, 1), :] = col_sum(dh1_f[...])
+
+    def node_backward_drain():
+        rows_drain(dmb_s, dmb_ss)
+
+        @pl.when(me_s > 0)
+        def _():
+            arrive(dh1_s, dh_ss)
+
+        @pl.when(me_s < S - 1)
+        def _():
+            arrive(row_r.at[:, pl.ds(0, 2 * D)], fw_ss)
+
+    dacc[...] = jnp.zeros_like(dacc)
+
+    def backward_step(step, carry):
+        t = S - 1 - step
+
+        @pl.when(me_s == t)
+        def _():
+            node_backward()
+
+        @pl.when(((t == S - 1) & (me_s >= S - 2)) | (me_s == t - 2))
+        def _():
+            prepare(me_s)
+
+        @pl.when(t < S - 1)
+        def _():
+            edge_pass(t)
+
+        @pl.when(t + 3 < S)
+        def _():
+            edge_grads_sum(t + 3)
+
+        arrive(dmb_r, dmb_rs)
+        message_back(t)
+
+        @pl.when(t > 0)
+        def _():
+            edge_back(t)
+
+        @pl.when(t == 0)
+        def _():
+            x_s[:, pl.ds(D, EP)] = jnp.zeros((N, EP), BF16)
+
+        gather_blocks()
+        other = gather_wait().astype(BF16)
+        row_s[:, pl.ds(D, D)] = other[:, :D]
+        row_s[:, pl.ds(2 * D + EP, EP)] = other[:, D:]
+        dpq = row_s.at[:, pl.ds(0, 2 * D)]
+
+        @pl.when(t > 0)
+        def _():
+            push(row_s, row_r.at[pl.ds(my_row, Q)], row_ss, row_rs, t - 1, owner_d)
+
+        @pl.when(t == 0)
+        def _():
+            push(dpq, dpqo_r.at[pl.ds(my_row, Q)], row_ss, dpqo_rs, t, owner_d)
+
+        edge_grads(t)
+
+        @pl.when(t > 0)
+        def _():
+            drain(row_s, row_ss, t - 1, owner_d)
+
+        @pl.when(t == 0)
+        def _():
+            drain(dpq, row_ss, t, owner_d)
+
+        @pl.when(me_s == t)
+        def _():
+            node_backward_drain()
+
+        return carry
+
+    lax.fori_loop(0, S, backward_step, 0)
+
+    arrive(dpqo_r, dpqo_rs)
+    share(2, dpqo_r, g_dpq)
+    dpq = dpqo_r[...]
+    sg[pl.ds(2, 1), :] = col_sum(dpq[:, :D].astype(F32))
+    dn = mm_bt(dpq, pw[...])
+    unit = hi_s[...]
+    sg[pl.ds(0, 1), :] = col_sum(dn * unit)
+    sg[pl.ds(1, 1), :] = col_sum(dn)
+    share(3, sg, g_small)
+    ig[...] = (dh1_f[...] + norm_back(dn, unit, sci[...], gains[0])).astype(BF16)
+    for t in range(min(2, S - 1), -1, -1):
+        edge_grads_sum(t)
+    for sec in range(S):
+        arrive(eg_o.at[sec], e2_rs.at[sec])
+    for half in range(2):
+        total = eg_o[half].astype(F32)
+        for sec in range(half + 2, S, 2):
+            total = total + eg_o[sec].astype(F32)
+        eg_f[half] = total.astype(BF16)
+    share(4, eg_f, g_edge)
+    for t in range(S):
+        drain(eg_b.at[t], e2_ss.at[t], t, me_d)
+    share_wait(0, fwd, g_fwd)
+    share_wait(1, bwd, g_bwd)
+    share_wait(2, dpqo_r, g_dpq)
+    share_wait(3, sg, g_small)
+    share_wait(4, eg_f, g_edge)
+
+
+def run_relay(dims, operands):
+    S, B, N, K, Q, D, DE, EP, FF, C = dims
+    R = K * Q
+    BN = B * N
+    tall = DE + N + Q
+    vm = pl.BlockSpec(memory_space=pltpu.VMEM)
+    hbm = pl.BlockSpec(memory_space=pl.ANY)
+    dma = pltpu.SemaphoreType.DMA
+    sds = jax.ShapeDtypeStruct
+    BW = (D + 2 * EP) // (2 * C)
+    tile = 32
+    held = -(-(DE + 16) // tile) * tile
+    scratch = [
+        pltpu.VMEM((BN, D), F32),
+        pltpu.VMEM((8, D), F32),
+        pltpu.VMEM((1, EP), F32),
+        pltpu.VMEM((S, held, D + 2 * EP), BF16),
+        pltpu.VMEM((BN, 4 * D), BF16),
+        pltpu.VMEM((BN, 2 * D + 2 * EP), BF16),
+        pltpu.VMEM((24, D), F32),
+        pltpu.VMEM((S, DE + 16, D + 2 * EP), BF16),
+        pltpu.VMEM((S, 2 * C, DE + 16, BW), BF16),
+        pltpu.VMEM((S, DE + 16, BW), BF16),
+        pltpu.VMEM((S, DE + 16, BW), BF16),
+        pltpu.VMEM((2, DE + 16, BW), BF16),
+        pltpu.VMEM((S, EP, EP), BF16),
+        pltpu.VMEM((S, 16, EP), BF16),
+        pltpu.VMEM((S, R, EP), BF16),
+        pltpu.VMEM((S, tall, D), BF16),
+        pltpu.VMEM((S, tall, EP), BF16),
+        pltpu.VMEM((D, 2 * D), BF16),
+        pltpu.VMEM((8, D), F32),
+        pltpu.VMEM((BN, D), BF16),
+        pltpu.VMEM((BN, D), BF16),
+        pltpu.VMEM((Q, D), BF16),
+        pltpu.VMEM((BN, D), BF16),
+        pltpu.VMEM((BN, 2 * D), BF16),
+        pltpu.VMEM((Q, 2 * D), BF16),
+        pltpu.VMEM((BN, 2 * EP), BF16),
+        pltpu.VMEM((Q, 2 * EP), BF16),
+        pltpu.VMEM((BN, D), F32),
+        pltpu.VMEM((BN, D), F32),
+        pltpu.VMEM((BN, D), F32),
+        pltpu.VMEM((BN, D), F32),
+        pltpu.VMEM((BN, 1), F32),
+        pltpu.VMEM((BN, 1), F32),
+        pltpu.VMEM((BN, 1), F32),
+        pltpu.VMEM((BN, 1), F32),
+        pltpu.VMEM((BN, FF), F32),
+        pltpu.VMEM((BN, FF), BF16),
+        pltpu.VMEM((2, R, EP), BF16),
+        pltpu.VMEM((R, EP), F32),
+        pltpu.VMEM((S, R, D), BF16),
+        pltpu.VMEM((S, R, EP), BF16),
+        pltpu.VMEM((2, R, D + EP), BF16),
+        pltpu.VMEM((S, EP, R), BF16),
+        pltpu.VMEM((S, EP, R), BF16),
+        pltpu.VMEM((N, D + EP), BF16),
+        pltpu.VMEM((4, Q, D + EP), BF16),
+        pltpu.VMEM((Q, 2 * D + 2 * EP), BF16),
+        pltpu.VMEM((BN, 2 * D + 2 * EP), BF16),
+        pltpu.VMEM((BN, 2 * D), BF16),
+        pltpu.VMEM((BN, D), BF16),
+        pltpu.VMEM((Q, D), BF16),
+        pltpu.VMEM((BN, D), BF16),
+        pltpu.VMEM((BN, D), BF16),
+        pltpu.VMEM((BN, D), F32),
+        pltpu.VMEM((BN, D), F32),
+        pltpu.VMEM((BN, D), F32),
+        pltpu.VMEM((BN, D), F32),
+        pltpu.VMEM((BN, D), F32),
+        pltpu.VMEM((BN, D), BF16),
+        dma, dma((2,)), dma((2,)), dma, dma,
+        dma, dma, dma, dma, dma, dma, dma, dma,
+        dma, dma, dma, dma, dma, dma, dma,
+        dma, dma, dma, dma, dma,
+        dma((S, 2 * C)), dma((S, 2 * C)), dma((S,)), dma((S,)), dma((5, C)), dma((5, C)),
+        dma((2, S // 2)), dma((S,)), dma((S,)), dma((S,)),
+    ]
+    return pl.pallas_call(
+        functools.partial(relay_kernel, dims),
+        out_shape=(
+            sds((BN, D), BF16),
+            sds((BN, D), BF16),
+            sds((C, BN, 4 * D), BF16),
+            sds((C, BN, 2 * D + 2 * EP), BF16),
+            sds((C, BN, 2 * D), BF16),
+            sds((C, 24, D), F32),
+            sds((C, 2, DE + 16, BW), BF16),
+        ),
+        in_specs=[hbm, vm, pl.BlockSpec(memory_space=pltpu.SMEM)] + [vm] * 16,
+        out_specs=(vm,) * 2 + (hbm,) * 5,
+        scratch_shapes=scratch,
+        compiler_params=pltpu.CompilerParams(
+            collective_id=0, has_side_effects=True, vmem_limit_bytes=62 * 1024 * 1024
+        ),
+    )(*operands)
+
+
+def gradient_kernel(
+    dims,
+    fwd, bwd, dpq, small, edge, fi, fo, fb, act, ig,
+    g_pair, g_edge, g_out, g_fi, g_fo, g_ep, g_self, g_eout, g_gain, g_shift, g_nb, g_fb, g_eb, act_out, ig_out,
+    fwd_v, bwd_v, dpq_v, fi_v, fo_v, gfi_v, gfo_v, pair_v, out_v, edge_v, in_sems, sems,
+):
+    S, B, N, K, Q, D, DE, EP, FF, C = dims
+    chunks = 4
+    FC = FF // chunks
+
+    def part(c, size=D):
+        return pl.ds(c * size, size)
+
+    loads = {}
+
+    def load(name, src, dst):
+        loads[name] = pltpu.make_async_copy(src, dst, in_sems.at[len(loads)])
+        loads[name].start()
+
+    load("a2", fwd.at[:, part(2)], fwd_v.at[2])
+    load("dy", bwd.at[:, part(1)], bwd_v.at[1])
+    for c in range(chunks):
+        load(("fi", c), fi.at[:, part(c, FC)], fi_v.at[c])
+        load(("fo", c), fo.at[part(c, FC)], fo_v.at[c])
+    load("a1", fwd.at[:, part(0)], fwd_v.at[0])
+    load("dpq0", dpq.at[:, part(0)], dpq_v.at[0])
+    load("dpq1", dpq.at[:, part(1)], dpq_v.at[1])
+    load("mbar", fwd.at[:, part(1)], fwd_v.at[1])
+    load("dmsg", bwd.at[:, part(0)], bwd_v.at[0])
+    load("a3", fwd.at[:, part(3)], fwd_v.at[3])
+    load("drs", bwd.at[:, part(2)], bwd_v.at[2])
+    load("edge", edge, edge_v)
+    stores = []
+
+    def out(src, dst):
+        copy = pltpu.make_async_copy(src, dst, sems.at[len(stores)])
+        copy.start()
+        stores.append(copy)
+
+    out(act, act_out)
+    out(ig, ig_out)
+    loads["a2"].wait()
+    loads["dy"].wait()
+    a2 = fwd_v[2]
+    dy = bwd_v[1]
+    for c in range(chunks):
+        cols = part(c, FC)
+        loads["fi", c].wait()
+        loads["fo", c].wait()
+        value, slope = gelu_both(mm(a2, fi_v[c]) + fb[:, cols])
+        du = (slope * mm_bt(dy, fo_v[c])).astype(BF16)
+        g_fb[:, cols] = col_sum(du.astype(F32))
+        gfi_v[c] = mm_at(a2, du)
+        out(gfi_v.at[c], g_fi.at[0, :, cols])
+        gfo_v[c] = mm_at(value.astype(BF16), dy)
+        out(gfo_v.at[c], g_fo.at[0, cols])
+    loads["a1"].wait()
+    for c in range(2):
+        loads["dpq%d" % c].wait()
+        pair_v[c] = mm_at(fwd_v[0], dpq_v[c])
+        out(pair_v.at[c], g_pair.at[0, :, part(c)])
+    loads["mbar"].wait()
+    loads["dmsg"].wait()
+    out_v[...] = mm_at(fwd_v[1], bwd_v[0]) * float(K)
+    out(out_v, g_out.at[0])
+    loads["a3"].wait()
+    loads["drs"].wait()
+    ends = mm_at(fwd_v[3], bwd_v[2])
+    g_ep[0] = jnp.concatenate([ends[:, :DE], ends[:, EP : EP + DE]], axis=1)
+    total = small[0]
+    for c in range(1, C):
+        total = total + small[c]
+    for i, rows in enumerate(((0, 1, 2), (8, 9, 10), (11, 12, 13))):
+        g_gain[i] = total[rows[0] : rows[0] + 1]
+        g_shift[i] = total[rows[1] : rows[1] + 1]
+        g_nb[i] = total[rows[2] : rows[2] + 1]
+    g_eb[0, pl.ds(0, 1), :] = total[16:17, :DE]
+    loads["edge"].wait()
+    BW = (D + 2 * EP) // (2 * C)
+    for k in range(2 * C):
+        block = edge_v[k % C, k // C].astype(F32)
+        first = k * BW
+        for array, begin, width in ((g_edge, 0, D), (g_self, D, DE), (g_eout, D + EP, DE)):
+            low, high = max(first, begin), min(first + BW, begin + width)
+            if low < high:
+                array[0, :, pl.ds(low - begin, high - low)] = block[:DE, low - first : high - first]
+        low, high = first, min(first + BW, DE)
+        if low < high:
+            g_eb[0, pl.ds(1, 1), pl.ds(low, high - low)] = block[DE : DE + 1, low - first : high - first]
+    for copy in stores:
+        copy.wait()
+
+
+def run_gradients(dims, operands):
+    S, B, N, K, Q, D, DE, EP, FF, C = dims
+    rows = C * B * N
+    BW = (D + 2 * EP) // (2 * C)
+    vm = pl.BlockSpec(memory_space=pltpu.VMEM)
+    hbm = pl.BlockSpec(memory_space=pl.ANY)
+    sds = jax.ShapeDtypeStruct
+    shapes = (
+        (1, D, 2 * D), (1, DE, D), (1, D, D), (1, D, FF), (1, FF, D), (1, D, 2 * DE), (1, DE, DE), (1, DE, DE),
+        (3, 1, D), (3, 1, D), (3, 1, D), (1, FF), (1, 2, DE),
+    )
+    return pl.pallas_call(
+        functools.partial(gradient_kernel, dims),
+        out_shape=tuple(sds(shape, F32) for shape in shapes) + (sds((1, B, N, D), BF16),) * 2,
+        in_specs=[hbm, hbm, hbm, vm, hbm, hbm, hbm, vm, hbm, hbm],
+        out_specs=(hbm, vm, hbm, hbm, hbm) + (vm,) * 8 + (hbm,) * 2,
+        scratch_shapes=[
+            pltpu.VMEM((4, rows, D), BF16),
+            pltpu.VMEM((3, rows, D), BF16),
+            pltpu.VMEM((2, rows, D), BF16),
+            pltpu.VMEM((4, D, FF // 4), BF16),
+            pltpu.VMEM((4, FF // 4, D), BF16),
+            pltpu.VMEM((4, D, FF // 4), F32),
+            pltpu.VMEM((4, FF // 4, D), F32),
+            pltpu.VMEM((2, D, D), F32),
+            pltpu.VMEM((D, D), F32),
+            pltpu.VMEM((C, 2, DE + 16, BW), BF16),
+            pltpu.SemaphoreType.DMA((18,)),
+            pltpu.SemaphoreType.DMA((13,)),
+        ],
+        compiler_params=pltpu.CompilerParams(vmem_limit_bytes=56 * 1024 * 1024),
+    )(*operands)
+
+
+def stationary(
+    clean_nodes, noise_nodes, edge_feats, neighbours, time_bins, cotangent,
+    pair_weight, message_edge, message_out, ffn_in, ffn_out, edge_pair, edge_self, edge_out,
+    norm_gain, norm_shift, node_bias, ffn_bias, edge_bias,
+):
+    S = lax.axis_size("section")
+    place = lax.axis_index("section")
+    column = lax.axis_index("dp")
+    B, N, D = clean_nodes.shape
+    K, DE = edge_feats.shape[2:]
+    FF = ffn_in.shape[2]
+    Q = N // 4
+    EP = DE + N
+    core = column % 2
+    w = place // 2
+    slab = (place % 2) * 2 * Q
+
+    node_ids = jnp.arange(N, dtype=jnp.int32)
+    both = [
+        lax.dynamic_slice(array, (w % B, slab) + (0,) * (array.ndim - 2), (1, 2 * Q) + array.shape[2:])[0]
+        for array in (edge_feats, neighbours)
+    ]
+    chosen = (both[1][:, :, None] == node_ids).astype(BF16)
+    both = jnp.concatenate([both[0], chosen], axis=2)
+    mine = lax.dynamic_slice_in_dim(both, core * Q, Q, 0)
+    theirs = lax.dynamic_slice_in_dim(both, (1 - core) * Q, Q, 0)
+    got = lax.ppermute(theirs, "dp", [(i, i ^ 1) for i in range(lax.axis_size("dp"))])
+    ecat0 = jnp.swapaxes(jnp.where(w // B == core, mine, got), 0, 1).reshape(K * Q, EP)
+    oht = jnp.transpose(ecat0[:, DE:])
+    phase = (time_bins.astype(F32) + 0.5) * (math.pi * 0.5 / TBINS)
+    mix = jnp.cos(phase[None] - jnp.array([[0.0], [math.pi * 0.5]], F32))
+
+    def by_rows(array):
+        return jnp.transpose(array, (1, 0, 2))
+
+    def widen(array, size, axis=-1):
+        extra = [(0, 0)] * array.ndim
+        extra[axis] = (0, size - array.shape[axis])
+        return jnp.pad(array, extra)
+
+    ep = jnp.concatenate([widen(edge_pair[0, :, :DE], EP), widen(edge_pair[0, :, DE:], EP)], axis=1)
+    C = lax.axis_size("dp")
+    dims = (S, B, N, K, Q, D, DE, EP, FF, C)
+    act, ig, g_fwd, g_bwd, g_dpq, g_small, g_edge = run_relay(
+        dims,
+        (
+            ecat0, oht, mix, clean_nodes.reshape(B * N, D), noise_nodes.reshape(B * N, D),
+            cotangent.reshape(B * N, D), pair_weight[0], message_out[0], ffn_in[0], ffn_out[0], ep,
+            by_rows(norm_gain), by_rows(norm_shift), by_rows(node_bias), ffn_bias, edge_bias[0],
+            message_edge[0], edge_self[0], edge_out[0],
+        ),
+    )
+    grads = run_gradients(
+        dims,
+        (
+            g_fwd.reshape(C * B * N, -1), g_bwd.reshape(C * B * N, -1), g_dpq.reshape(C * B * N, -1),
+            g_small, g_edge, ffn_in[0], ffn_out[0], ffn_bias, act.reshape(1, B, N, D), ig.reshape(1, B, N, D),
+        ),
+    )
+    grads, outs = list(grads[:-2]), tuple(grads[-2:])
+    grads[8:11] = [by_rows(array) for array in grads[8:11]]
+    return outs + tuple(grads)
+
+
 def solution(mesh):
+    sections, copies = mesh.shape["section"], mesh.shape["dp"]
+
+    def body(*args):
+        B, N = args[0].shape[:2]
+        fits = sections == 4 * B and copies % 2 == 0 and N % 64 == 0
+        return stationary(*args) if fits else on_device(*args)
+
     placed = (
         P("dp", None, None),
         P("dp", None, None),
@@ -417,7 +1443,7 @@
         P("section", None, None),
     )
     return jax.shard_map(
-        on_device,
+        body,
         mesh=mesh,
         in_specs=placed,
         out_specs=(

time: 4050 us -> 478 us (0.12)
  waiting for transfers between devices: 1880 us -> 0.01 us
  starting transfers between devices: 873 us -> 0.52 us
  local copies, waits for them, and re-layouts: 551 us -> 3.31 us
  Pallas kernels: 0 us -> 471 us
  other arithmetic: 436 us -> 2.31 us
  matrix products: 232 us -> 0 us
    ppermute x69 -> x1, waiting for transfers between devices: 1770 us -> 0.01 us  [stationary(): lax.ppermute(theirs, 'dp', [(i, i ^ 1) for i in range(lax.axis_size('dp'))])]
    ppermute x69 -> x1, starting transfers between devices: 873 us -> 0.52 us  [stationary(): lax.ppermute(theirs, 'dp', [(i, i ^ 1) for i in range(lax.axis_size('dp'))])]
    pallas_call x0 -> x2, Pallas kernels: none -> 471 us  [the longest x1 458 us: run_relay(): pl.pallas_call(functools.partial(relay_kernel, dims), out_shape=(sds((BN,...]
    dot_general x70 -> x0, matrix products: 232 us -> none  [the longest x6 55.6 us: forward_layer(): jnp.einsum('nkc,cd->nkd', message_act, msg_out, preferred_element_type=jn...]
    add x100 -> x0, other arithmetic: 221 us -> none  [the longest x99 219 us: backward_step(): grads = tuple((total + term for total, term in zip(grads, terms)))]
    gather x24 -> x0, local copies, waits for them, and re-layouts: 206 us -> none  [the longest x12 116 us: forward_layer(): jnp.take(pair_out[:, width:], nearest, axis=0)]
    broadcast_in_dim x113 -> x0, local copies, waits for them, and re-layouts: 133 us -> none  [the longest x56 74.3 us: on_device(): grads_zero = tuple((jnp.zeros(item.shape, jnp.float32) for item in weights))]
    dynamic_update_slice x60 -> x0, other arithmetic: 118 us -> none  [the longest x17 97 us: forward_step(): lax.dynamic_update_index_in_dim(kept_edges, jnp.where(second_pass, edges_...]
  transfers between devices with their start and end apart: 70 -> 1, of which waited for: 31 -> 0; matrix products, arithmetic and copies ran while one was open for 7% -> 0% of each run, Pallas kernels for 0% -> 0%
where the time goes in v1:
time: 478 us
  Pallas kernels  471 us (99%)
    pallas_call x1, Pallas kernels, run_relay(): pl.pallas_call(functools.partial(relay_kernel, dims), out_shape=(sds((BN,...  458 us
    pallas_call x1, Pallas kernels, run_gradients(): pl.pallas_call(functools.partial(gradient_kernel, dims), out_shape=tuple(...  12.9 us
  transfers between devices with their start and end apart: 1, of which 0 were waited for; matrix products, arithmetic and copies ran while one was open for 0% of the time, Pallas kernels for 0%

profile of v1, /device:TPU:0, one launch (start us, length us, event | category | flops | bytes accessed | tf_op | source)
XLA Modules:
  0.0 478.1 jit_solution(15478724193628199470)
XLA Ops:
  0.6 0.0 copy-start
  0.7 0.8 copy-done
  1.5 0.1 constant_dynamic-slice_fusion
  1.6 0.3 fusion.2
  1.9 0.0 copy-start.2
  2.0 1.3 dynamic-slice_bitcast_fusion
  3.3 0.0 copy-start.4
  3.3 0.0 copy-start.3
  3.3 0.2 fusion.4
  3.5 0.5 collective-permute-start
  4.0 0.0 copy-done.2
  4.0 0.1 slice_bitcast_fusion.1
  4.2 0.9 fusion.3.ep
  5.1 0.0 copy-done.4
  5.1 0.0 copy-done.3
  5.1 0.7 add_cosine_fusion.mix
  5.7 0.0 collective-permute-done
  5.8 0.3 fusion.6
  6.0 0.0 copy-start.1
  6.0 0.1 slice.12
  6.2 0.8 copy.40
  6.9 0.0 copy-done.1
  7.0 458.0 %shard_map.307 = (bf16[128,512]{1,0:T(8,128)(2,1)}, bf16[128,512]{1,0:T(8,128)(2,1)}, bf16[4,128,2048]{2,1,0:T(8,128)(2,1)}, bf16[4,128,1536]{2,1,0:T(8,128)(2,1...) custom-call(bf16[960,256]{1,0:T(8,128)(2,1)} %bitcast.41, ...), custom_call_target="tpu_custom_call" | custom-call | tf_op jit(solution)/shard_map/pallas_call | solution.py:1205
  465.0 12.9 %shard_map.308 = (f32[1,512,1024]{2,1,0:T(8,128)}, f32[1,192,512]{2,1,0:T(8,128)}, f32[1,512,512]{2,1,0:T(8,128)}, f32[1,512,2048]{2,1,0:T(8,128)}, f32[1,2048,5...) custom-call(bf16[512,2048]{1,0:T(8,128)(2,1)} %bitcast.42, ...), custom_call_target="tpu_custom_call" | custom-call | tf_op jit(solution)/shard_map/pallas_call | solution.py:1329
  (2 shorter events, 0.0 us)
Async XLA Ops:
  0.6 0.8 copy-start
  1.9 2.1 copy-start.2
  3.3 1.8 copy-start.4
  3.3 1.8 copy-start.3
  3.5 2.2 collective-permute-start
  6.0 0.9 copy-start.1

commit v2 on v1

--- a/solution.py
+++ b/solution.py
@@ -515,16 +515,19 @@
 
     works_here = lax.div(w, B) == core
 
-    pairs = [(p, j) for p in range(B) for j in range(4)]
+    def at(p, first=0, size=16):
+        return pl.ds(pl.multiple_of(p * N + first, size), size)
+
+    near = jnp.clip(w - core * B, 0, B - 1)
 
     load = pltpu.make_async_copy(ecat0, ecat.at[0], ld_sem)
     load.start()
     barrier = pltpu.get_barrier_semaphore()
     for sec in range(S):
         for c in range(C):
-            near = (c == pair) | (c == pair + 1) | (w == sec // 2)
-
-            @pl.when(near & jnp.logical_not(is_me(sec, c)))
+            greeted = (c == pair) | (c == pair + 1) | (w == sec // 2)
+
+            @pl.when(greeted & jnp.logical_not(is_me(sec, c)))
             def _():
                 pl.semaphore_signal(
                     barrier, inc=1, device_id={"section": sec, "dp": c}, device_id_type=MESH
@@ -604,10 +607,10 @@
         wo[t, pl.ds(DE, N), :] = jnp.zeros((N, EP), BF16)
         eb1[t] = wall[t, pl.ds(DE, 16), pl.ds(0, EP)]
 
-    def rows_out(src, dst, ssem, rsem):
-        for p, j in pairs:
+    def rows_out(p, src, dst, ssem, rsem):
+        for j in range(4):
             sec, dpi = worker_of(p, j)
-            push(src.at[pl.ds(p * N + j * Q, Q)], dst, ssem, rsem, sec, dpi)
+            push(src.at[at(p, j * Q, Q)], dst, ssem, rsem, sec, dpi)
 
     def rows_drain(src, ssem):
         lax.cond(
@@ -683,55 +686,69 @@
                 rows = pl.ds(i, RB)
                 hi_s[rows, :] = hin_r[rows, :].astype(F32) + first * start[rows, :]
 
-        arrive(mb_r, mb_rs)
-        mean = mm(mb_r[...], mo[...])
-        for i in range(0, BN, RB):
-            rows = pl.ds(i, RB)
-            h1 = hi_s[rows, :] + mean[i : i + RB] + node_b[1]
-            h1_s[rows, :] = h1
-            unit, scale = normed(h1)
-            un1[rows, :] = unit
-            sc1[rows, :] = scale
-            fwd[rows, pl.ds(2 * D, D)] = (unit * gains[1] + shifts[1]).astype(BF16)
-            fwd[rows, pl.ds(D, D)] = mb_r[rows, :]
-        a2 = fwd[:, pl.ds(2 * D, D)]
-        y = jnp.zeros((BN, D), F32)
-        for c in range(chunks):
-            cols = pl.ds(c * FC, FC)
-            u = mm(a2, fi[:, cols])
-            v = []
-            for i in range(0, BN, RB):
-                rows = pl.ds(i, RB)
-                block = u[i : i + RB] + fb[:, cols]
-                u_s[rows, cols] = block
-                v.append(gelu(block).astype(BF16))
-            y = y + mm(stacked(v), fo[cols, :])
-        last = jnp.where(me_s == S - 1, 1.0, 0.0)
-        for i in range(0, BN, RB):
-            rows = pl.ds(i, RB)
-            h2 = h1_s[rows, :] + y[i : i + RB] + node_b[2]
-            rounded = h2.astype(BF16)
-            hst[rows, :] = rounded
-            unit, scale = normed(h2)
-            un2[rows, :] = unit
-            sc2[rows, :] = scale
-            fwd[rows, pl.ds(3 * D, D)] = (unit * gains[2] + shifts[2]).astype(BF16)
-            pair_norm(rows, rounded.astype(F32) + last * start[rows, :], parn)
-        rq = mm(fwd[:, pl.ds(3 * D, D)], ep[...])
-        for i in range(0, BN, RB):
-            rows = pl.ds(i, RB)
-            rq_s[rows, pl.ds(0, EP)] = (rq[i : i + RB, :EP] + eb0[...]).astype(BF16)
-            rq_s[rows, pl.ds(EP, EP)] = rq[i : i + RB, EP:].astype(BF16)
-        pair_rows(pwn, parn)
         later = lax.rem(me_s + 1, S)
 
-        @pl.when(me_s < S - 1)
-        def _():
-            rows_out(rq_s, rq_r, rq_ss, rq_rs)
+        def turn(n, carry):
+            p = lax.rem(near + n, B)
+            whole = at(p, 0, N)
+            arrive(mb_r.at[whole], mb_rs.at[p])
+            mean = mm(mb_r[whole, :], mo[...])
+            for i in range(0, N, RB):
+                rows = at(p, i)
+                h1 = hi_s[rows, :] + mean[i : i + RB] + node_b[1]
+                h1_s[rows, :] = h1
+                unit, scale = normed(h1)
+                un1[rows, :] = unit
+                sc1[rows, :] = scale
+                fwd[rows, pl.ds(2 * D, D)] = (unit * gains[1] + shifts[1]).astype(BF16)
+                fwd[rows, pl.ds(D, D)] = mb_r[rows, :]
+            a2 = fwd[whole, pl.ds(2 * D, D)]
+            y = jnp.zeros((N, D), F32)
+            for c in range(chunks):
+                cols = pl.ds(c * FC, FC)
+                u = mm(a2, fi[:, cols])
+                v = []
+                for i in range(0, N, RB):
+                    block = u[i : i + RB] + fb[:, cols]
+                    u_s[at(p, i), cols] = block
+                    v.append(gelu(block).astype(BF16))
+                y = y + mm(stacked(v), fo[cols, :])
+            last = jnp.where(me_s == S - 1, 1.0, 0.0)
+            for i in range(0, N, RB):
+                rows = at(p, i)
+                h2 = h1_s[rows, :] + y[i : i + RB] + node_b[2]
+                rounded = h2.astype(BF16)
+                hst[rows, :] = rounded
+                unit, scale = normed(h2)
+                un2[rows, :] = unit
+                sc2[rows, :] = scale
+                fwd[rows, pl.ds(3 * D, D)] = (unit * gains[2] + shifts[2]).astype(BF16)
+                pair_norm(rows, rounded.astype(F32) + last * start[rows, :], parn)
+            rq = mm(fwd[whole, pl.ds(3 * D, D)], ep[...])
+            for i in range(0, N, RB):
+                rows = at(p, i)
+                rq_s[rows, pl.ds(0, EP)] = (rq[i : i + RB, :EP] + eb0[...]).astype(BF16)
+                rq_s[rows, pl.ds(EP, EP)] = rq[i : i + RB, EP:].astype(BF16)
+            pair_rows(p, pwn, parn)
+
+            @pl.when(me_s < S - 1)
+            def _():
+                rows_out(p, rq_s, rq_r, rq_ss, rq_rs)
+
+            @pl.when(step < 2 * S - 1)
+            def _():
+                rows_out(p, pq_s, pq_r, pq_ss, pq_rs)
+
+            @pl.when((n == 0) & works_here)
+            def _():
+                pass_on(step)
+
+            return carry
+
+        lax.fori_loop(0, B, turn, 0)
 
         @pl.when(step < 2 * S - 1)
         def _():
-            rows_out(pq_s, pq_r, pq_ss, pq_rs)
             far(hst, hin_r, hop_ss, hop_rs, later, me_d).start()
 
         @pl.when(step >= S)
@@ -754,13 +771,25 @@
         sc0[rows, :] = scale
         a1_s[rows, :] = (unit * first[pl.ds(0, 1), :] + first[pl.ds(1, 1), :]).astype(BF16)
 
-    def pair_rows(weight, first):
+    def pair_rows(p, weight, first):
+        whole = at(p, 0, N)
         for half in range(2):
             cols = pl.ds(half * D, D)
-            value = mm(a1_s[...], weight[:, cols])
+            value = mm(a1_s[whole, :], weight[:, cols])
             if half == 0:
                 value = value + first[pl.ds(2, 1), :]
-            pq_s[:, cols] = value.astype(BF16)
+            pq_s[whole, cols] = value.astype(BF16)
+
+    def pass_on(step):
+        t = lax.rem(step, S)
+
+        @pl.when(t < S - 1)
+        def _():
+            spread(rq_r, EP, scat, t, ag2_ss, ag2_rs, rq_rs)
+
+        @pl.when(step < 2 * S - 1)
+        def _():
+            spread(pq_r, D, wcat, lax.rem(step + 1, S), ag_ss, ag_rs, pq_rs)
 
     def node_forward_drain():
         arrive(hst, hop_ss)
@@ -775,8 +804,9 @@
         for i in range(0, BN, RB):
             rows = pl.ds(i, RB)
             pair_norm(rows, start[rows, :], par)
-        pair_rows(pw, par)
-        rows_out(pq_s, pq_r, pq_ss, pq_rs)
+        for p in range(B):
+            pair_rows(p, pw, par)
+            rows_out(p, pq_s, pq_r, pq_ss, pq_rs)
 
     def message_slope(t):
         own = wcat[t, own_rows, :].astype(F32)
@@ -814,7 +844,7 @@
         spread_wait(wcat, t, ag_rs)
         messages(t)
         spread_wait(wcat, t, ag_ss)
-        push(mb_s, mb_r.at[pl.ds(my_row, Q)], mb_ss, mb_rs, t, owner_d)
+        push(mb_s, mb_r.at[pl.ds(my_row, Q)], mb_ss, mb_rs.at[slot], t, owner_d)
 
         @pl.when((step == 0) & (me_s == 0))
         def _():
@@ -832,13 +862,9 @@
         def _():
             prepare(t)
 
-        @pl.when(t < S - 1)
-        def _():
-            spread(rq_r, EP, scat, t, ag2_ss, ag2_rs, rq_rs)
-
-        @pl.when(step < 2 * S - 1)
-        def _():
-            spread(pq_r, D, wcat, lax.rem(step + 1, S), ag_ss, ag_rs, pq_rs)
+        @pl.when(jnp.logical_not((me_s == t) & works_here))
+        def _():
+            pass_on(step)
 
         @pl.when(t < S - 1)
         def _():
@@ -956,40 +982,50 @@
         @pl.when(me_s < S - 1)
         def _():
             arrive(dh1_r, dh_rs)
-            arrive(row_r, row_rs)
-            dn0 = mm_bt(row_r[:, pl.ds(0, 2 * D)], pwn[...])
-            dn3 = mm_bt(row_r[:, pl.ds(2 * D, 2 * EP)], ep[...])
-            for i in range(0, BN, RB):
-                rows = pl.ds(i, RB)
-                dn = dn3[i : i + RB]
-                dn3_s[rows, :] = dn
-                first = norm_back(dn0[i : i + RB], un0[rows, :], sc0[rows, :], parn[pl.ds(0, 1), :])
-                dh = (dh1_r[rows, :].astype(F32) + first).astype(BF16).astype(F32)
-                dh2_s[rows, :] = dh + norm_back(dn, un2[rows, :], sc2[rows, :], gains[2])
-
-        @pl.when(me_s == S - 1)
-        def _():
-            dh2_s[...] = cot[...].astype(F32)
-
-        dy = stacked([dh2_s[pl.ds(i, RB), :].astype(BF16) for i in range(0, BN, RB)])
-        bwd[:, pl.ds(D, D)] = dy
-        da2 = jnp.zeros((BN, D), F32)
-        for c in range(chunks):
-            cols = pl.ds(c * FC, FC)
-            dv = mm_bt(dy, fo[cols, :])
-            du = stacked(
-                [(slope_s[pl.ds(i, RB), cols].astype(F32) * dv[i : i + RB]).astype(BF16) for i in range(0, BN, RB)]
-            )
-            da2 = da2 + mm_bt(du, fi[:, cols])
-        for i in range(0, BN, RB):
-            rows = pl.ds(i, RB)
-            block = da2[i : i + RB]
-            da2_s[rows, :] = block
-            dh1 = dh2_s[rows, :] + norm_back(block, un1[rows, :], sc1[rows, :], gains[1])
-            dh1_f[rows, :] = dh1
-            bwd[rows, pl.ds(0, D)] = (dh1 * (1.0 / K)).astype(BF16)
-        dmb_s[...] = mm_bt(bwd[:, pl.ds(0, D)], mo[...]).astype(BF16)
-        rows_out(dmb_s, dmb_r, dmb_ss, dmb_rs)
+
+        def turn(n, carry):
+            p = lax.rem(near + n, B)
+            whole = at(p, 0, N)
+
+            @pl.when(me_s < S - 1)
+            def _():
+                arrive(row_r.at[whole], row_rs.at[p])
+                dn0 = mm_bt(row_r[whole, pl.ds(0, 2 * D)], pwn[...])
+                dn3 = mm_bt(row_r[whole, pl.ds(2 * D, 2 * EP)], ep[...])
+                for i in range(0, N, RB):
+                    rows = at(p, i)
+                    dn = dn3[i : i + RB]
+                    dn3_s[rows, :] = dn
+                    first = norm_back(dn0[i : i + RB], un0[rows, :], sc0[rows, :], parn[pl.ds(0, 1), :])
+                    dh = (dh1_r[rows, :].astype(F32) + first).astype(BF16).astype(F32)
+                    dh2_s[rows, :] = dh + norm_back(dn, un2[rows, :], sc2[rows, :], gains[2])
+
+            @pl.when(me_s == S - 1)
+            def _():
+                dh2_s[whole, :] = cot[whole, :].astype(F32)
+
+            dy = dh2_s[whole, :].astype(BF16)
+            bwd[whole, pl.ds(D, D)] = dy
+            da2 = jnp.zeros((N, D), F32)
+            for c in range(chunks):
+                cols = pl.ds(c * FC, FC)
+                dv = mm_bt(dy, fo[cols, :])
+                du = stacked(
+                    [(slope_s[at(p, i), cols].astype(F32) * dv[i : i + RB]).astype(BF16) for i in range(0, N, RB)]
+                )
+                da2 = da2 + mm_bt(du, fi[:, cols])
+            for i in range(0, N, RB):
+                rows = at(p, i)
+                block = da2[i : i + RB]
+                da2_s[rows, :] = block
+                dh1 = dh2_s[rows, :] + norm_back(block, un1[rows, :], sc1[rows, :], gains[1])
+                dh1_f[rows, :] = dh1
+                bwd[rows, pl.ds(0, D)] = (dh1 * (1.0 / K)).astype(BF16)
+            dmb_s[whole, :] = mm_bt(bwd[whole, pl.ds(0, D)], mo[...]).astype(BF16)
+            rows_out(p, dmb_s, dmb_r, dmb_ss, dmb_rs)
+            return carry
+
+        lax.fori_loop(0, B, turn, 0)
 
         @pl.when(me_s > 0)
         def _():
@@ -1070,7 +1106,7 @@
 
         @pl.when(t > 0)
         def _():
-            push(row_s, row_r.at[pl.ds(my_row, Q)], row_ss, row_rs, t - 1, owner_d)
+            push(row_s, row_r.at[pl.ds(my_row, Q)], row_ss, row_rs.at[slot], t - 1, owner_d)
 
         @pl.when(t == 0)
         def _():
@@ -1197,7 +1233,7 @@
         pltpu.VMEM((BN, D), BF16),
         dma, dma((2,)), dma((2,)), dma, dma,
         dma, dma, dma, dma, dma, dma, dma, dma,
-        dma, dma, dma, dma, dma, dma, dma,
+        dma, dma((B,)), dma, dma, dma, dma((B,)), dma,
         dma, dma, dma, dma, dma,
         dma((S, 2 * C)), dma((S, 2 * C)), dma((S,)), dma((S,)), dma((5, C)), dma((5, C)),
         dma((2, S // 2)), dma((S,)), dma((S,)), dma((S,)),

time: 478 us -> 464 us (0.971)
  Pallas kernels: 471 us -> 456 us
    pallas_call x1, Pallas kernels: 458 us -> 443 us  [run_relay(): pl.pallas_call(functools.partial(relay_kernel, dims), out_shape=(sds((BN,...]
where the time goes in v2:
time: 464 us; the launch traced here: 463 us
  Pallas kernels  456 us (98%)
    pallas_call x1, Pallas kernels, run_relay(): pl.pallas_call(functools.partial(relay_kernel, dims), out_shape=(sds((BN,...  443 us
    pallas_call x1, Pallas kernels, run_gradients(): pl.pallas_call(functools.partial(gradient_kernel, dims), out_shape=tuple(...  12.9 us
  transfers between devices with their start and end apart: 1, of which 0 were waited for; matrix products, arithmetic and copies ran while one was open for 0% of the time, Pallas kernels for 0%

profile of v2, /device:TPU:0, one launch (start us, length us, event | category | flops | bytes accessed | tf_op | source)
XLA Modules:
  0.0 463.4 jit_solution(7011094587932959956)
XLA Ops:
  0.6 0.0 copy-start
  0.7 0.8 copy-done
  1.5 0.1 constant_dynamic-slice_fusion
  1.6 0.3 fusion.2
  1.9 0.0 copy-start.2
  2.0 1.3 dynamic-slice_bitcast_fusion
  3.3 0.0 copy-start.4
  3.3 0.0 copy-start.3
  3.3 0.2 fusion.4
  3.5 0.5 collective-permute-start
  4.0 0.0 copy-done.2
  4.0 0.1 slice_bitcast_fusion.1
  4.2 0.9 fusion.3.ep
  5.1 0.0 copy-done.4
  5.1 0.0 copy-done.3
  5.1 0.7 add_cosine_fusion.mix
  5.7 0.0 collective-permute-done
  5.8 0.3 fusion.6
  6.0 0.0 copy-start.1
  6.0 0.1 slice.12
  6.2 0.8 copy.40
  6.9 0.0 copy-done.1
  7.0 443.4 %shard_map.307 = (bf16[128,512]{1,0:T(8,128)(2,1)}, bf16[128,512]{1,0:T(8,128)(2,1)}, bf16[4,128,2048]{2,1,0:T(8,128)(2,1)}, bf16[4,128,1536]{2,1,0:T(8,128)(2,1...) custom-call(bf16[960,256]{1,0:T(8,128)(2,1)} %bitcast.41, ...), custom_call_target="tpu_custom_call" | custom-call | tf_op jit(solution)/shard_map/pallas_call | solution.py:1241
  450.3 12.9 %shard_map.308 = (f32[1,512,1024]{2,1,0:T(8,128)}, f32[1,192,512]{2,1,0:T(8,128)}, f32[1,512,512]{2,1,0:T(8,128)}, f32[1,512,2048]{2,1,0:T(8,128)}, f32[1,2048,5...) custom-call(bf16[512,2048]{1,0:T(8,128)(2,1)} %bitcast.42, ...), custom_call_target="tpu_custom_call" | custom-call | tf_op jit(solution)/shard_map/pallas_call | solution.py:1365
  (2 shorter events, 0.0 us)
Async XLA Ops:
  0.6 0.8 copy-start
  1.9 2.1 copy-start.2
  3.3 1.8 copy-start.4
  3.3 1.8 copy-start.3
  3.5 2.2 collective-permute-start
  6.0 0.9 copy-start.1

commit v3 on v2

--- a/solution.py
+++ b/solution.py
@@ -454,15 +454,16 @@
 def relay_kernel(
     dims,
     ecat0, oht, mix, clean, noise, cot, pw, mo, fi, fo, ep, gains, shifts, node_b, fb, edge_b, we_own, ws_own, wo_own,
-    act, ig, g_fwd, g_bwd, g_dpq, g_small, g_edge,
-    start, par, eb0, wall, fwd, bwd, sg, eg, eg_r, eg_b, eg_o, eg_f, wo, eb1,
+    act, ig, g_fwd, g_bwd, g_dpq, g_small, g_msg, g_upd,
+    start, par, eb0, wall_msg, wall_upd, fwd, bwd, sg,
+    msg_g, msg_r, msg_b, msg_o, msg_f, upd_g, upd_r, upd_b, upd_o, upd_f, wo, eb1,
     ecat, wcat, scat, pwn, parn, hin_r, hst, mb_s, mb_r, pq_s, pq_r, rq_s, rq_r,
     un0, un1, un2, hi_s, sc0, sc1, sc2, sci, u_s, slope_s, de, dacc, gp, gpe, dcat, act_t, edge_t,
     x_s, x_r, row_s, row_r, dpqo_r, dmb_s, dmb_r, dh1_s, dh1_r, dh1_f, dh2_s, dn3_s, da2_s, h1_s, a1_s,
     ld_sem, nx_ss, nx_rs, hop_ss, hop_rs,
     pq_ss, pq_rs, ag_ss, ag_rs, rq_ss, rq_rs, ag2_ss, ag2_rs,
     mb_ss, mb_rs, x_ss, x_rs, row_ss, row_rs, dpqo_rs, fw_ss, dmb_ss, dmb_rs, dh_ss, dh_rs,
-    e1_ss, e1_rs, e2_ss, e2_rs, g_ss, g_rs, ring_ss, ring_rs, sib_ss, sib_rs,
+    e1_ss, e1_rs, e2_ss, e2_rs, g_ss, g_rs, relay_ss, ring_ss, ring_rs, sib_ss, sib_rs,
 ):
     S, B, N, K, Q, D, DE, EP, FF, C = dims
     BN = B * N
@@ -532,16 +533,14 @@
                 pl.semaphore_signal(
                     barrier, inc=1, device_id={"section": sec, "dp": c}, device_id_type=MESH
                 )
-    W = D + 2 * EP
-    H = wall.shape[1] // 2
-    wall[me_s] = jnp.zeros((2 * H, W), BF16)
-    wall[me_s, pl.ds(0, DE), pl.ds(0, D)] = we_own[...]
-    wall[me_s, pl.ds(0, DE), pl.ds(D, DE)] = ws_own[...]
-    wall[me_s, pl.ds(0, DE), pl.ds(D + EP, DE)] = wo_own[...]
+    wall_msg[me_s] = we_own[...]
+    wall_upd[me_s] = jnp.zeros(wall_upd.shape[1:], BF16)
+    wall_upd[me_s, pl.ds(0, DE), pl.ds(0, DE)] = ws_own[...]
+    wall_upd[me_s, pl.ds(0, DE), pl.ds(EP, DE)] = wo_own[...]
     bias = edge_b[pl.ds(1, 1), :]
     high = bias.astype(BF16).astype(F32)
     row = lax.broadcasted_iota(jnp.int32, (16, DE), 0)
-    wall[me_s, pl.ds(DE, 16), pl.ds(0, DE)] = jnp.where(
+    wall_upd[me_s, pl.ds(DE, 16), pl.ds(0, DE)] = jnp.where(
         row == 0, high, jnp.where(row == 1, bias - high, 0.0)
     ).astype(BF16)
     eb0[...] = jnp.zeros_like(eb0)
@@ -557,18 +556,38 @@
         return jnp.where(i < S // 2, 2 * i, 2 * (S - i) - 1)
 
     place = jnp.where(lax.rem(me_s, 2) == 0, w, S - 1 - w)
-    mine = pl.ds(pl.multiple_of(core * H, H), H)
-    theirs = pl.ds(pl.multiple_of((1 - core) * H, H), H)
     sides = ((section_at(place + 1), S // 2), (section_at(place - 1), S // 2 - 1))
-
-    def ring_send(layer, side, hop):
+    walls = (wall_msg, wall_upd)
+
+    def half_of(which, layer, c):
+        size = walls[which].shape[1] // 2
+        return walls[which].at[layer, pl.ds(pl.multiple_of(c * size, size), size)]
+
+    def ring_send(which, layer, side, hop):
         sec, reach = sides[side]
         if hop < reach:
-            half = wall.at[layer, mine]
-            far(half, half, ring_ss.at[side, hop], ring_rs.at[layer], sec, me_d).start()
+            half = half_of(which, layer, core)
+            far(half, half, ring_ss.at[which, side, hop], ring_rs.at[which, layer], sec, me_d).start()
+
+    def ring_hop(which, side, hop):
+        layer = section_at(place - hop if side == 0 else place + hop)
+        half = half_of(which, layer, core)
+        arrive(half, ring_rs.at[which, layer])
+        ring_send(which, layer, side, hop)
+        far(half, half, sib_ss.at[which, layer], sib_rs.at[which, layer], me_s, pair + 1 - core).start()
+
+    hops = [(hop, side) for hop in range(1, S // 2 + 1) for side in range(2) if hop <= sides[side][1]]
+
+    def ring_later(second):
+        for hop, side in hops:
+            early = (place > 0) & ((place >= hop) if side == 0 else (place + hop <= S))
+
+            @pl.when(early != second)
+            def _():
+                ring_hop(1, side, hop)
 
     for side in range(2):
-        ring_send(me_s, side, 0)
+        ring_send(0, me_s, side, 0)
     before = lax.rem(me_s + S - 1, S)
     far(pw, pwn, nx_ss.at[0], nx_rs.at[0], before, me_d).start()
     far(par, parn, nx_ss.at[1], nx_rs.at[1], before, me_d).start()
@@ -577,35 +596,32 @@
         rows = pl.ds(p * N, N)
         start[rows, :] = mix[0, p] * clean[rows, :].astype(F32) + mix[1, p] * noise[rows, :].astype(F32)
 
-    def ring():
-        for hop in range(1, S // 2 + 1):
+    def ring_drain():
+        for which in range(2):
             for side in range(2):
-                if hop <= sides[side][1]:
-                    layer = section_at(place - hop if side == 0 else place + hop)
-                    half = wall.at[layer, mine]
-                    arrive(half, ring_rs.at[layer])
-                    ring_send(layer, side, hop)
-                    far(half, half, sib_ss.at[layer], sib_rs.at[layer], me_s, pair + 1 - core).start()
-
-    def ring_drain():
-        for side in range(2):
-            for hop in range(sides[side][1]):
-                arrive(wall.at[me_s, mine], ring_ss.at[side, hop])
-        for layer in range(S):
-            @pl.when(layer != me_s)
-            def _():
-                arrive(wall.at[layer, mine], sib_ss.at[layer])
-
-    def unpack(t):
+                for hop in range(sides[side][1]):
+                    arrive(half_of(which, me_s, core), ring_ss.at[which, side, hop])
+            for layer in range(S):
+                @pl.when(layer != me_s)
+                def _():
+                    arrive(half_of(which, layer, core), sib_ss.at[which, layer])
+
+    def unpack_messages(t):
         @pl.when(t != me_s)
         def _():
-            arrive(wall.at[t, theirs], sib_rs.at[t])
-
-        wcat[t, pl.ds(0, DE), :] = wall[t, pl.ds(0, DE), pl.ds(0, D)]
-        scat[t, pl.ds(0, DE), :] = wall[t, pl.ds(0, DE), pl.ds(D, EP)]
-        wo[t, pl.ds(0, DE), :] = wall[t, pl.ds(0, DE), pl.ds(D + EP, EP)]
+            arrive(half_of(0, t, 1 - core), sib_rs.at[0, t])
+
+        wcat[t, pl.ds(0, DE), :] = wall_msg[t]
+
+    def unpack_updates(t):
+        @pl.when(t != me_s)
+        def _():
+            arrive(half_of(1, t, 1 - core), sib_rs.at[1, t])
+
+        scat[t, pl.ds(0, DE), :] = wall_upd[t, pl.ds(0, DE), pl.ds(0, EP)]
+        wo[t, pl.ds(0, DE), :] = wall_upd[t, pl.ds(0, DE), pl.ds(EP, EP)]
         wo[t, pl.ds(DE, N), :] = jnp.zeros((N, EP), BF16)
-        eb1[t] = wall[t, pl.ds(DE, 16), pl.ds(0, EP)]
+        eb1[t] = wall_upd[t, pl.ds(DE, 16), pl.ds(0, EP)]
 
     def rows_out(p, src, dst, ssem, rsem):
         for j in range(4):
@@ -638,6 +654,33 @@
         for c in range(C):
             arrive(dst.at[c], g_rs.at[group, c])
             drain(src, g_ss.at[group, c], me_s, c)
+
+    def share_near(group, src, dst):
+        for c in range(C):
+            @pl.when((c == pair) | (c == pair + 1) | (core == c % 2))
+            def _():
+                push(src, dst(me_d), g_ss.at[group, c], g_rs.at[group, me_d], me_s, c)
+
+    def share_relay(group, src, dst):
+        for c in range(C):
+            @pl.when((c != me_d) & (core == c % 2))
+            def _():
+                arrive(dst(c), g_rs.at[group, c])
+                far(dst(c), dst(c), relay_ss.at[group - 2, c // 2], g_rs.at[group, c], me_s, pair + 1 - core).start()
+
+    def share_near_wait(group, src, dst):
+        for c in range(C):
+            @pl.when((c == me_d) | (core != c % 2))
+            def _():
+                arrive(dst(c), g_rs.at[group, c])
+
+            @pl.when((c != me_d) & ((c == pair) | (c == pair + 1) | (core == c % 2)))
+            def _():
+                arrive(src, g_ss.at[group, c])
+
+            @pl.when((c != me_d) & (core == c % 2))
+            def _():
+                arrive(dst(c), relay_ss.at[group - 2, c // 2])
 
     steps = 4
     KC = K // steps
@@ -839,13 +882,18 @@
 
         @pl.when(step < S)
         def _():
-            unpack(t)
+            unpack_messages(t)
 
         spread_wait(wcat, t, ag_rs)
         messages(t)
         spread_wait(wcat, t, ag_ss)
         push(mb_s, mb_r.at[pl.ds(my_row, Q)], mb_ss, mb_rs.at[slot], t, owner_d)
 
+        for second in range(2):
+            @pl.when(step == second)
+            def _():
+                ring_later(second == 1)
+
         @pl.when((step == 0) & (me_s == 0))
         def _():
             rows_drain(pq_s, pq_ss)
@@ -868,6 +916,10 @@
 
         @pl.when(t < S - 1)
         def _():
+            @pl.when(step < S)
+            def _():
+                unpack_updates(t)
+
             spread_wait(scat, t, ag2_rs)
             edge_update(t)
             spread_wait(scat, t, ag2_ss)
@@ -875,11 +927,18 @@
         drain(mb_s, mb_ss, t, owner_d)
         return carry
 
-    ring()
+    for hop, side in hops:
+        ring_hop(0, side, hop)
+    for side in range(2):
+        ring_send(1, me_s, side, 0)
     load.wait()
     spread(pq_r, D, wcat, 0, ag_ss, ag_rs, pq_rs)
     lax.fori_loop(0, 2 * S, forward_step, 0)
     ring_drain()
+
+    @pl.when(me_s != S - 1)
+    def _():
+        arrive(half_of(1, S - 1, 1 - core), sib_rs.at[1, S - 1])
 
     def edge_back(t):
         b2, n2 = lax.rem(t, 2), lax.rem(t + 1, 2)
@@ -909,47 +968,59 @@
             dacc[rows, :] = de[b3, rows, :].astype(F32) + mm_bt(d, scat[t, pl.ds(0, top), :])
 
     blocks = 2 * C
-    BW = (D + 2 * EP) // blocks
     my_block = lax.rem(me_s, 2) * C + me_d
-    my_cols = pl.ds(pl.multiple_of(my_block * BW, BW), BW)
-
-    def edge_grads(t):
-        b3 = lax.rem(t, 2)
-
-        @pl.when(t < S - 1)
-        def _():
-            eg[t, pl.ds(0, DE), pl.ds(0, D + EP)] = mm(edge_t[t, pl.ds(0, DE), :], dcat[b3]).astype(BF16)
-            eg[t, pl.ds(0, DE), pl.ds(D + EP, EP)] = mm(act_t[t, pl.ds(0, DE), :], de[b3]).astype(BF16)
-            bias = jnp.sum(de[b3].astype(F32), axis=0, keepdims=True)
-            eg[t, pl.ds(DE, 16), pl.ds(0, EP)] = jnp.broadcast_to(bias, (16, EP)).astype(BF16)
-
-        @pl.when(t == S - 1)
-        def _():
-            eg[t, pl.ds(0, DE), pl.ds(0, D)] = mm(edge_t[t, pl.ds(0, DE), :], dcat[b3, :, pl.ds(0, D)]).astype(BF16)
-            eg[t, pl.ds(0, DE), pl.ds(D, 2 * EP)] = jnp.zeros((DE, 2 * EP), BF16)
-            eg[t, pl.ds(DE, 16), pl.ds(0, EP)] = jnp.zeros((16, EP), BF16)
-
-        eg[t, pl.ds(DE, 16), pl.ds(EP, D + EP)] = jnp.zeros((16, D + EP), BF16)
+    kinds = ((msg_g, msg_r, msg_b, msg_o, msg_f, g_msg), (upd_g, upd_r, upd_b, upd_o, upd_f, g_upd))
+    BW = msg_r.shape[3]
+
+    def block_of(kind, t, half, c):
+        array, size = kinds[kind][0], kinds[kind][1].shape[2]
+        return array.at[t, pl.ds(pl.multiple_of(half * size, size), size), pl.ds(pl.multiple_of(c * BW, BW), BW)]
+
+    def blocks_out(kind, t):
         for k in range(blocks):
             @pl.when(k != my_block)
             def _():
                 far(
-                    eg.at[t, :, pl.ds(k * BW, BW)], eg_r.at[t, my_block], e1_ss.at[t, k], e1_rs.at[t, my_block],
-                    2 * w + k // C, k % C,
+                    block_of(kind, t, k // C, k % C), kinds[kind][1].at[t, my_block],
+                    e1_ss.at[kind, t, k], e1_rs.at[kind, t, my_block], 2 * w + k // C, k % C,
                 ).start()
 
-    def edge_grads_sum(t):
-        eg_r[t, my_block] = eg[t, :, my_cols]
+    def update_grads(t):
+        b2 = lax.rem(t, 2)
+
+        @pl.when(t < S - 1)
+        def _():
+            edges = mm(edge_t[t, pl.ds(0, DE), :], dcat[b2, :, pl.ds(D, EP)])
+            upd_g[t, pl.ds(0, DE), pl.ds(0, EP)] = edges.astype(BF16)
+            upd_g[t, pl.ds(0, DE), pl.ds(EP, EP)] = mm(act_t[t, pl.ds(0, DE), :], de[b2]).astype(BF16)
+            bias = jnp.sum(de[b2].astype(F32), axis=0, keepdims=True)
+            upd_g[t, pl.ds(DE, 16), pl.ds(0, EP)] = jnp.broadcast_to(bias, (16, EP)).astype(BF16)
+
+        @pl.when(t == S - 1)
+        def _():
+            upd_g[t, pl.ds(0, DE + 16), :] = jnp.zeros((DE + 16, 2 * EP), BF16)
+
+        upd_g[t, pl.ds(DE, 16), pl.ds(EP, EP)] = jnp.zeros((16, EP), BF16)
+        upd_g[t, pl.ds(DE + 16, 16), :] = jnp.zeros((16, 2 * EP), BF16)
+        blocks_out(1, t)
+
+    def message_grads(t):
+        msg_g[t] = mm(edge_t[t, pl.ds(0, DE), :], dcat[lax.rem(t, 2), :, pl.ds(0, D)]).astype(BF16)
+        blocks_out(0, t)
+
+    def blocks_sum(kind, t):
+        _, ref, low, dst, _, _ = kinds[kind]
+        ref[t, my_block] = block_of(kind, t, lax.rem(me_s, 2), me_d)[...]
         for k in range(blocks):
             @pl.when(k != my_block)
             def _():
-                arrive(eg_r.at[t, k], e1_rs.at[t, k])
-                arrive(eg.at[t, :, pl.ds(k * BW, BW)], e1_ss.at[t, k])
-        total = eg_r[t, 0].astype(F32)
+                arrive(ref.at[t, k], e1_rs.at[kind, t, k])
+                arrive(block_of(kind, t, k // C, k % C), e1_ss.at[kind, t, k])
+        total = ref[t, 0].astype(F32)
         for k in range(1, blocks):
-            total = total + eg_r[t, k].astype(F32)
-        eg_b[t] = total.astype(BF16)
-        push(eg_b.at[t], eg_o.at[me_s], e2_ss.at[t], e2_rs.at[me_s], t, me_d)
+            total = total + ref[t, k].astype(F32)
+        low[t] = total.astype(BF16)
+        push(low.at[t], dst.at[me_s], e2_ss.at[kind, t], e2_rs.at[kind, me_s], t, me_d)
 
     def gather_blocks():
         for k in range(1, 4):
@@ -1083,9 +1154,17 @@
         def _():
             edge_pass(t)
 
-        @pl.when(t + 3 < S)
-        def _():
-            edge_grads_sum(t + 3)
+        update_grads(t)
+
+        @pl.when(t + 2 < S)
+        def _():
+            for kind in range(2):
+                blocks_sum(kind, t + 2)
+
+        @pl.when(t == 0)
+        def _():
+            for kind in range(2):
+                blocks_sum(kind, 1)
 
         arrive(dmb_r, dmb_rs)
         message_back(t)
@@ -1112,7 +1191,7 @@
         def _():
             push(dpq, dpqo_r.at[pl.ds(my_row, Q)], row_ss, dpqo_rs, t, owner_d)
 
-        edge_grads(t)
+        message_grads(t)
 
         @pl.when(t > 0)
         def _():
@@ -1131,32 +1210,40 @@
     lax.fori_loop(0, S, backward_step, 0)
 
     arrive(dpqo_r, dpqo_rs)
-    share(2, dpqo_r, g_dpq)
+    across = [pl.ds(p * N, N) for p in range(B)]
+    for p in range(B):
+        share_near(2 + p, dpqo_r.at[across[p]], lambda c, p=p: g_dpq.at[c, across[p]])
     dpq = dpqo_r[...]
     sg[pl.ds(2, 1), :] = col_sum(dpq[:, :D].astype(F32))
     dn = mm_bt(dpq, pw[...])
     unit = hi_s[...]
     sg[pl.ds(0, 1), :] = col_sum(dn * unit)
     sg[pl.ds(1, 1), :] = col_sum(dn)
-    share(3, sg, g_small)
+    share(2 + B, sg, g_small)
     ig[...] = (dh1_f[...] + norm_back(dn, unit, sci[...], gains[0])).astype(BF16)
-    for t in range(min(2, S - 1), -1, -1):
-        edge_grads_sum(t)
-    for sec in range(S):
-        arrive(eg_o.at[sec], e2_rs.at[sec])
-    for half in range(2):
-        total = eg_o[half].astype(F32)
-        for sec in range(half + 2, S, 2):
-            total = total + eg_o[sec].astype(F32)
-        eg_f[half] = total.astype(BF16)
-    share(4, eg_f, g_edge)
-    for t in range(S):
-        drain(eg_b.at[t], e2_ss.at[t], t, me_d)
+    blocks_sum(1, 0)
+    blocks_sum(0, 0)
+    for p in range(B):
+        share_relay(2 + p, dpqo_r.at[across[p]], lambda c, p=p: g_dpq.at[c, across[p]])
+    for kind in range(1, -1, -1):
+        _, _, low, src, final, dst = kinds[kind]
+        for sec in range(S):
+            arrive(src.at[sec], e2_rs.at[kind, sec])
+        for half in range(2):
+            total = src[half].astype(F32)
+            for sec in range(half + 2, S, 2):
+                total = total + src[sec].astype(F32)
+            final[half] = total.astype(BF16)
+        share(3 + B + kind, final, dst)
+        for t in range(S):
+            drain(low.at[t], e2_ss.at[kind, t], t, me_d)
     share_wait(0, fwd, g_fwd)
     share_wait(1, bwd, g_bwd)
-    share_wait(2, dpqo_r, g_dpq)
-    share_wait(3, sg, g_small)
-    share_wait(4, eg_f, g_edge)
+    for p in range(B):
+        share_near_wait(2 + p, dpqo_r.at[across[p]], lambda c, p=p: g_dpq.at[c, across[p]])
+    share_wait(2 + B, sg, g_small)
+    for kind in range(2):
+        share_wait(3 + B + kind, kinds[kind][4], kinds[kind][5])
 
 
 def run_relay(dims, operands):
@@ -1168,22 +1255,28 @@
     hbm = pl.BlockSpec(memory_space=pl.ANY)
     dma = pltpu.SemaphoreType.DMA
     sds = jax.ShapeDtypeStruct
-    BW = (D + 2 * EP) // (2 * C)
+    BW = D // C
     tile = 32
     held = -(-(DE + 16) // tile) * tile
     scratch = [
         pltpu.VMEM((BN, D), F32),
         pltpu.VMEM((8, D), F32),
         pltpu.VMEM((1, EP), F32),
-        pltpu.VMEM((S, held, D + 2 * EP), BF16),
+        pltpu.VMEM((S, DE, D), BF16),
+        pltpu.VMEM((S, held, 2 * EP), BF16),
         pltpu.VMEM((BN, 4 * D), BF16),
         pltpu.VMEM((BN, 2 * D + 2 * EP), BF16),
         pltpu.VMEM((24, D), F32),
-        pltpu.VMEM((S, DE + 16, D + 2 * EP), BF16),
-        pltpu.VMEM((S, 2 * C, DE + 16, BW), BF16),
-        pltpu.VMEM((S, DE + 16, BW), BF16),
-        pltpu.VMEM((S, DE + 16, BW), BF16),
-        pltpu.VMEM((2, DE + 16, BW), BF16),
+        pltpu.VMEM((S, DE, D), BF16),
+        pltpu.VMEM((S, 2 * C, DE // 2, BW), BF16),
+        pltpu.VMEM((S, DE // 2, BW), BF16),
+        pltpu.VMEM((S, DE // 2, BW), BF16),
+        pltpu.VMEM((2, DE // 2, BW), BF16),
+        pltpu.VMEM((S, held, 2 * EP), BF16),
+        pltpu.VMEM((S, 2 * C, held // 2, BW), BF16),
+        pltpu.VMEM((S, held // 2, BW), BF16),
+        pltpu.VMEM((S, held // 2, BW), BF16),
+        pltpu.VMEM((2, held // 2, BW), BF16),
         pltpu.VMEM((S, EP, EP), BF16),
         pltpu.VMEM((S, 16, EP), BF16),
         pltpu.VMEM((S, R, EP), BF16),
@@ -1235,8 +1328,8 @@
         dma, dma, dma, dma, dma, dma, dma, dma,
         dma, dma((B,)), dma, dma, dma, dma((B,)), dma,
         dma, dma, dma, dma, dma,
-        dma((S, 2 * C)), dma((S, 2 * C)), dma((S,)), dma((S,)), dma((5, C)), dma((5, C)),
-        dma((2, S // 2)), dma((S,)), dma((S,)), dma((S,)),
+        dma((2, S, 2 * C)), dma((2, S, 2 * C)), dma((2, S)), dma((2, S)), dma((5 + B, C)), dma((5 + B, C)),
+        dma((B, C // 2)), dma((2, 2, S // 2)), dma((2, S)), dma((2, S)), dma((2, S)),
     ]
     return pl.pallas_call(
         functools.partial(relay_kernel, dims),
@@ -1247,10 +1340,11 @@
             sds((C, BN, 2 * D + 2 * EP), BF16),
             sds((C, BN, 2 * D), BF16),
             sds((C, 24, D), F32),
-            sds((C, 2, DE + 16, BW), BF16),
+            sds((C, 2, DE // 2, BW), BF16),
+            sds((C, 2, held // 2, BW), BF16),
         ),
         in_specs=[hbm, vm, pl.BlockSpec(memory_space=pltpu.SMEM)] + [vm] * 16,
-        out_specs=(vm,) * 2 + (hbm,) * 5,
+        out_specs=(vm,) * 2 + (hbm,) * 6,
         scratch_shapes=scratch,
         compiler_params=pltpu.CompilerParams(
             collective_id=0, has_side_effects=True, vmem_limit_bytes=62 * 1024 * 1024
@@ -1260,9 +1354,9 @@
 
 def gradient_kernel(
     dims,
-    fwd, bwd, dpq, small, edge, fi, fo, fb, act, ig,
+    fwd, bwd, dpq, small, edge, upd, fi, fo, fb, act, ig,
     g_pair, g_edge, g_out, g_fi, g_fo, g_ep, g_self, g_eout, g_gain, g_shift, g_nb, g_fb, g_eb, act_out, ig_out,
-    fwd_v, bwd_v, dpq_v, fi_v, fo_v, gfi_v, gfo_v, pair_v, out_v, edge_v, in_sems, sems,
+    fwd_v, bwd_v, dpq_v, fi_v, fo_v, gfi_v, gfo_v, pair_v, out_v, edge_v, upd_v, in_sems, sems,
 ):
     S, B, N, K, Q, D, DE, EP, FF, C = dims
     chunks = 4
@@ -1290,6 +1384,7 @@
     load("a3", fwd.at[:, part(3)], fwd_v.at[3])
     load("drs", bwd.at[:, part(2)], bwd_v.at[2])
     load("edge", edge, edge_v)
+    load("upd", upd, upd_v)
     stores = []
 
     def out(src, dst):
@@ -1336,12 +1431,16 @@
         g_nb[i] = total[rows[2] : rows[2] + 1]
     g_eb[0, pl.ds(0, 1), :] = total[16:17, :DE]
     loads["edge"].wait()
-    BW = (D + 2 * EP) // (2 * C)
-    for k in range(2 * C):
-        block = edge_v[k % C, k // C].astype(F32)
-        first = k * BW
-        for array, begin, width in ((g_edge, 0, D), (g_self, D, DE), (g_eout, D + EP, DE)):
-            low, high = max(first, begin), min(first + BW, begin + width)
+    loads["upd"].wait()
+    BW = edge_v.shape[3]
+    for c in range(C):
+        for half in range(2):
+            block = edge_v[c, half].astype(F32)
+            g_edge[0, pl.ds(half * (DE // 2), DE // 2), pl.ds(c * BW, BW)] = block
+        block = stacked([upd_v[c, 0], upd_v[c, 1]]).astype(F32)
+        first = c * BW
+        for array, begin in ((g_self, 0), (g_eout, EP)):
+            low, high = max(first, begin), min(first + BW, begin + DE)
             if low < high:
                 array[0, :, pl.ds(low - begin, high - low)] = block[:DE, low - first : high - first]
         low, high = first, min(first + BW, DE)
@@ -1354,7 +1453,8 @@
 def run_gradients(dims, operands):
     S, B, N, K, Q, D, DE, EP, FF, C = dims
     rows = C * B * N
-    BW = (D + 2 * EP) // (2 * C)
+    BW = D // C
+    held = operands[5].shape[2]
     vm = pl.BlockSpec(memory_space=pltpu.VMEM)
     hbm = pl.BlockSpec(memory_space=pl.ANY)
     sds = jax.ShapeDtypeStruct
@@ -1365,7 +1465,7 @@
     return pl.pallas_call(
         functools.partial(gradient_kernel, dims),
         out_shape=tuple(sds(shape, F32) for shape in shapes) + (sds((1, B, N, D), BF16),) * 2,
-        in_specs=[hbm, hbm, hbm, vm, hbm, hbm, hbm, vm, hbm, hbm],
+        in_specs=[hbm, hbm, hbm, vm, hbm, hbm, hbm, hbm, vm, hbm, hbm],
         out_specs=(hbm, vm, hbm, hbm, hbm) + (vm,) * 8 + (hbm,) * 2,
         scratch_shapes=[
             pltpu.VMEM((4, rows, D), BF16),
@@ -1377,8 +1477,9 @@
             pltpu.VMEM((4, FF // 4, D), F32),
             pltpu.VMEM((2, D, D), F32),
             pltpu.VMEM((D, D), F32),
-            pltpu.VMEM((C, 2, DE + 16, BW), BF16),
-            pltpu.SemaphoreType.DMA((18,)),
+            pltpu.VMEM((C, 2, DE // 2, BW), BF16),
+            pltpu.VMEM((C, 2, held, BW), BF16),
+            pltpu.SemaphoreType.DMA((19,)),
             pltpu.SemaphoreType.DMA((13,)),
         ],
         compiler_params=pltpu.CompilerParams(vmem_limit_bytes=56 * 1024 * 1024),
@@ -1428,7 +1529,7 @@
     ep = jnp.concatenate([widen(edge_pair[0, :, :DE], EP), widen(edge_pair[0, :, DE:], EP)], axis=1)
     C = lax.axis_size("dp")
     dims = (S, B, N, K, Q, D, DE, EP, FF, C)
-    act, ig, g_fwd, g_bwd, g_dpq, g_small, g_edge = run_relay(
+    act, ig, g_fwd, g_bwd, g_dpq, g_small, g_msg, g_upd = run_relay(
         dims,
         (
             ecat0, oht, mix, clean_nodes.reshape(B * N, D), noise_nodes.reshape(B * N, D),
@@ -1441,7 +1542,7 @@
         dims,
         (
             g_fwd.reshape(C * B * N, -1), g_bwd.reshape(C * B * N, -1), g_dpq.reshape(C * B * N, -1),
-            g_small, g_edge, ffn_in[0], ffn_out[0], ffn_bias, act.reshape(1, B, N, D), ig.reshape(1, B, N, D),
+            g_small, g_msg, g_upd, ffn_in[0], ffn_out[0], ffn_bias, act.reshape(1, B, N, D), ig.reshape(1, B, N, D),
         ),
     )
     grads, outs = list(grads[:-2]), tuple(grads[-2:])

time: 464 us -> 469 us (1.011)
  Pallas kernels: 456 us -> 462 us
    pallas_call x1, Pallas kernels: 443 us -> 449 us  [run_relay(): pl.pallas_call(functools.partial(relay_kernel, dims), out_shape=(sds((BN,...]
where the time goes in v3:
time: 469 us
  Pallas kernels  462 us (99%)
    pallas_call x1, Pallas kernels, run_relay(): pl.pallas_call(functools.partial(relay_kernel, dims), out_shape=(sds((BN,...  449 us
    pallas_call x1, Pallas kernels, run_gradients(): pl.pallas_call(functools.partial(gradient_kernel, dims), out_shape=tuple(...  12.9 us
  transfers between devices with their start and end apart: 1, of which 0 were waited for; matrix products, arithmetic and copies ran while one was open for 0% of the time, Pallas kernels for 0%

profile of v3, /device:TPU:0, one launch (start us, length us, event | category | flops | bytes accessed | tf_op | source)
XLA Modules:
  0.0 469.0 jit_solution(6578703686669741608)
XLA Ops:
  0.6 0.0 copy-start
  0.7 0.8 copy-done
  1.5 0.1 constant_dynamic-slice_fusion
  1.6 0.3 fusion.2
  1.9 0.0 copy-start.2
  2.0 1.3 dynamic-slice_bitcast_fusion
  3.3 0.0 copy-start.4
  3.3 0.0 copy-start.3
  3.3 0.2 fusion.4
  3.5 0.5 collective-permute-start
  4.0 0.0 copy-done.2
  4.0 0.1 slice_bitcast_fusion.1
  4.2 0.9 fusion.3.ep
  5.1 0.0 copy-done.4
  5.1 0.0 copy-done.3
  5.1 0.7 add_cosine_fusion.mix
  5.7 0.0 collective-permute-done
  5.8 0.3 fusion.6
  6.0 0.0 copy-start.1
  6.0 0.1 slice.12
  6.2 0.8 copy.40
  6.9 0.0 copy-done.1
  7.0 448.9 %shard_map.307 = (bf16[128,512]{1,0:T(8,128)(2,1)}, bf16[128,512]{1,0:T(8,128)(2,1)}, bf16[4,128,2048]{2,1,0:T(8,128)(2,1)}, bf16[4,128,1536]{2,1,0:T(8,128)(2,1...) custom-call(bf16[960,256]{1,0:T(8,128)(2,1)} %bitcast.41, ...), custom_call_target="tpu_custom_call" | custom-call | tf_op jit(solution)/shard_map/pallas_call | solution.py:1334
  455.9 12.9 %shard_map.308 = (f32[1,512,1024]{2,1,0:T(8,128)}, f32[1,192,512]{2,1,0:T(8,128)}, f32[1,512,512]{2,1,0:T(8,128)}, f32[1,512,2048]{2,1,0:T(8,128)}, f32[1,2048,5...) custom-call(bf16[512,2048]{1,0:T(8,128)(2,1)} %bitcast.42, ...), custom_call_target="tpu_custom_call" | custom-call | tf_op jit(solution)/shard_map/pallas_call | solution.py:1465
  (2 shorter events, 0.0 us)
Async XLA Ops:
  0.6 0.8 copy-start
  1.9 2.1 copy-start.2
  3.3 1.8 copy-start.4
  3.3 1.8 copy-start.3
  3.5 2.2 collective-permute-start
  6.0 0.9 copy-start.1

commit v4 on v3

--- a/solution.py
+++ b/solution.py
@@ -456,7 +456,7 @@
     ecat0, oht, mix, clean, noise, cot, pw, mo, fi, fo, ep, gains, shifts, node_b, fb, edge_b, we_own, ws_own, wo_own,
     act, ig, g_fwd, g_bwd, g_dpq, g_small, g_msg, g_upd,
     start, par, eb0, wall_msg, wall_upd, fwd, bwd, sg,
-    msg_g, msg_r, msg_b, msg_o, msg_f, upd_g, upd_r, upd_b, upd_o, upd_f, wo, eb1,
+    eg, eg_r, eg_b, msg_o, msg_f, upd_o, upd_f, wo, eb1,
     ecat, wcat, scat, pwn, parn, hin_r, hst, mb_s, mb_r, pq_s, pq_r, rq_s, rq_r,
     un0, un1, un2, hi_s, sc0, sc1, sc2, sci, u_s, slope_s, de, dacc, gp, gpe, dcat, act_t, edge_t,
     x_s, x_r, row_s, row_r, dpqo_r, dmb_s, dmb_r, dh1_s, dh1_r, dh1_f, dh2_s, dn3_s, da2_s, h1_s, a1_s,
@@ -969,58 +969,57 @@
 
     blocks = 2 * C
     my_block = lax.rem(me_s, 2) * C + me_d
-    kinds = ((msg_g, msg_r, msg_b, msg_o, msg_f, g_msg), (upd_g, upd_r, upd_b, upd_o, upd_f, g_upd))
-    BW = msg_r.shape[3]
-
-    def block_of(kind, t, half, c):
-        array, size = kinds[kind][0], kinds[kind][1].shape[2]
-        return array.at[t, pl.ds(pl.multiple_of(half * size, size), size), pl.ds(pl.multiple_of(c * BW, BW), BW)]
-
-    def blocks_out(kind, t):
+    BW, HM, HU = msg_o.shape[2], msg_o.shape[1], upd_o.shape[1]
+
+    def block_of(t, half, c, size):
+        return eg.at[t, half, pl.ds(0, size), pl.ds(pl.multiple_of(c * BW, BW), BW)]
+
+    def blocks_out(t, size):
         for k in range(blocks):
             @pl.when(k != my_block)
             def _():
                 far(
-                    block_of(kind, t, k // C, k % C), kinds[kind][1].at[t, my_block],
-                    e1_ss.at[kind, t, k], e1_rs.at[kind, t, my_block], 2 * w + k // C, k % C,
+                    block_of(t, k // C, k % C, size), eg_r.at[t, my_block, pl.ds(0, size)],
+                    e1_ss.at[t, k], e1_rs.at[t, my_block], 2 * w + k // C, k % C,
                 ).start()
 
-    def update_grads(t):
-        b2 = lax.rem(t, 2)
-
-        @pl.when(t < S - 1)
-        def _():
-            edges = mm(edge_t[t, pl.ds(0, DE), :], dcat[b2, :, pl.ds(D, EP)])
-            upd_g[t, pl.ds(0, DE), pl.ds(0, EP)] = edges.astype(BF16)
-            upd_g[t, pl.ds(0, DE), pl.ds(EP, EP)] = mm(act_t[t, pl.ds(0, DE), :], de[b2]).astype(BF16)
-            bias = jnp.sum(de[b2].astype(F32), axis=0, keepdims=True)
-            upd_g[t, pl.ds(DE, 16), pl.ds(0, EP)] = jnp.broadcast_to(bias, (16, EP)).astype(BF16)
-
-        @pl.when(t == S - 1)
-        def _():
-            upd_g[t, pl.ds(0, DE + 16), :] = jnp.zeros((DE + 16, 2 * EP), BF16)
-
-        upd_g[t, pl.ds(DE, 16), pl.ds(EP, EP)] = jnp.zeros((16, EP), BF16)
-        upd_g[t, pl.ds(DE + 16, 16), :] = jnp.zeros((16, 2 * EP), BF16)
-        blocks_out(1, t)
-
-    def message_grads(t):
-        msg_g[t] = mm(edge_t[t, pl.ds(0, DE), :], dcat[lax.rem(t, 2), :, pl.ds(0, D)]).astype(BF16)
-        blocks_out(0, t)
-
-    def blocks_sum(kind, t):
-        _, ref, low, dst, _, _ = kinds[kind]
-        ref[t, my_block] = block_of(kind, t, lax.rem(me_s, 2), me_d)[...]
+    def edge_grads(t):
+        grad = mm(edge_t[t, pl.ds(0, DE), :], dcat[lax.rem(t, 2), :, pl.ds(0, D)]).astype(BF16)
+        for half in range(2):
+            eg[t, half, pl.ds(0, HM), :] = grad[half * HM : (half + 1) * HM]
+
+        @pl.when(t > 0)
+        def _():
+            n2 = lax.rem(t + 1, 2)
+            edges = mm(edge_t[t - 1, pl.ds(0, DE), :], dcat[n2, :, pl.ds(D, EP)])
+            outs = mm(act_t[t - 1, pl.ds(0, DE), :], de[n2])
+            bias = jnp.sum(de[n2].astype(F32), axis=0, keepdims=True)
+            grad = jnp.concatenate([edges, outs], axis=1).astype(BF16)
+            eg[t, 0, pl.ds(HM, HU), :] = grad[:HU]
+            eg[t, 1, pl.ds(HM, DE - HU), :] = grad[HU:]
+            eg[t, 1, pl.ds(HM + DE - HU, 16), pl.ds(0, EP)] = jnp.broadcast_to(bias, (16, EP)).astype(BF16)
+            eg[t, 1, pl.ds(HM + DE - HU, 16), pl.ds(EP, EP)] = jnp.zeros((16, EP), BF16)
+            eg[t, 1, pl.ds(HM + DE - HU + 16, 2 * HU - DE - 16), :] = jnp.zeros((2 * HU - DE - 16, 2 * EP), BF16)
+            blocks_out(t, HM + HU)
+
+        @pl.when(t == 0)
+        def _():
+            blocks_out(t, HM)
+
+    def blocks_sum(t, size):
+        eg_r[t, my_block, pl.ds(0, size), :] = block_of(t, lax.rem(me_s, 2), me_d, size)[...]
         for k in range(blocks):
             @pl.when(k != my_block)
             def _():
-                arrive(ref.at[t, k], e1_rs.at[kind, t, k])
-                arrive(block_of(kind, t, k // C, k % C), e1_ss.at[kind, t, k])
-        total = ref[t, 0].astype(F32)
+                arrive(eg_r.at[t, k, pl.ds(0, size)], e1_rs.at[t, k])
+                arrive(block_of(t, k // C, k % C, size), e1_ss.at[t, k])
+        total = eg_r[t, 0, pl.ds(0, size), :].astype(F32)
         for k in range(1, blocks):
-            total = total + ref[t, k].astype(F32)
-        low[t] = total.astype(BF16)
-        push(low.at[t], dst.at[me_s], e2_ss.at[kind, t], e2_rs.at[kind, me_s], t, me_d)
+            total = total + eg_r[t, k, pl.ds(0, size), :].astype(F32)
+        eg_b[t, pl.ds(0, size), :] = total.astype(BF16)
+        push(eg_b.at[t, pl.ds(0, HM)], msg_o.at[me_s], e2_ss.at[0, t], e2_rs.at[0, me_s], t, me_d)
+        if size > HM:
+            push(eg_b.at[t, pl.ds(HM, HU)], upd_o.at[me_s], e2_ss.at[1, t], e2_rs.at[1, me_s], t - 1, me_d)
 
     def gather_blocks():
         for k in range(1, 4):
@@ -1154,17 +1153,13 @@
         def _():
             edge_pass(t)
 
-        update_grads(t)
-
         @pl.when(t + 2 < S)
         def _():
-            for kind in range(2):
-                blocks_sum(kind, t + 2)
+            blocks_sum(t + 2, HM + HU)
 
         @pl.when(t == 0)
         def _():
-            for kind in range(2):
-                blocks_sum(kind, 1)
+            blocks_sum(1, HM + HU)
 
         arrive(dmb_r, dmb_rs)
         message_back(t)
@@ -1191,7 +1186,7 @@
         def _():
             push(dpq, dpqo_r.at[pl.ds(my_row, Q)], row_ss, dpqo_rs, t, owner_d)
 
-        message_grads(t)
+        edge_grads(t)
 
         @pl.when(t > 0)
         def _():
@@ -1221,12 +1216,10 @@
     sg[pl.ds(1, 1), :] = col_sum(dn)
     share(2 + B, sg, g_small)
     ig[...] = (dh1_f[...] + norm_back(dn, unit, sci[...], gains[0])).astype(BF16)
-    blocks_sum(1, 0)
-    blocks_sum(0, 0)
+    blocks_sum(0, HM)
     for p in range(B):
         share_relay(2 + p, dpqo_r.at[across[p]], lambda c, p=p: g_dpq.at[c, across[p]])
-    for kind in range(1, -1, -1):
-        _, _, low, src, final, dst = kinds[kind]
+    def combine(kind, src, final):
         for sec in range(S):
             arrive(src.at[sec], e2_rs.at[kind, sec])
         for half in range(2):
@@ -1234,16 +1227,29 @@
             for sec in range(half + 2, S, 2):
                 total = total + src[sec].astype(F32)
             final[half] = total.astype(BF16)
-        share(3 + B + kind, final, dst)
-        for t in range(S):
-            drain(low.at[t], e2_ss.at[kind, t], t, me_d)
+
+    @pl.when(me_s < S - 1)
+    def _():
+        combine(1, upd_o, upd_f)
+
+    @pl.when(me_s == S - 1)
+    def _():
+        upd_f[...] = jnp.zeros_like(upd_f)
+
+    share(4 + B, upd_f, g_upd)
+    combine(0, msg_o, msg_f)
+    share(3 + B, msg_f, g_msg)
+    for t in range(S):
+        drain(eg_b.at[t, pl.ds(0, HM)], e2_ss.at[0, t], t, me_d)
+        if t > 0:
+            drain(eg_b.at[t, pl.ds(HM, HU)], e2_ss.at[1, t], t - 1, me_d)
     share_wait(0, fwd, g_fwd)
     share_wait(1, bwd, g_bwd)
     for p in range(B):
         share_near_wait(2 + p, dpqo_r.at[across[p]], lambda c, p=p: g_dpq.at[c, across[p]])
     share_wait(2 + B, sg, g_small)
-    for kind in range(2):
-        share_wait(3 + B + kind, kinds[kind][4], kinds[kind][5])
+    share_wait(3 + B, msg_f, g_msg)
+    share_wait(4 + B, upd_f, g_upd)
 
 
 def run_relay(dims, operands):
@@ -1267,14 +1273,11 @@
         pltpu.VMEM((BN, 4 * D), BF16),
         pltpu.VMEM((BN, 2 * D + 2 * EP), BF16),
         pltpu.VMEM((24, D), F32),
-        pltpu.VMEM((S, DE, D), BF16),
-        pltpu.VMEM((S, 2 * C, DE // 2, BW), BF16),
-        pltpu.VMEM((S, DE // 2, BW), BF16),
+        pltpu.VMEM((S, 2, (DE + held) // 2, D), BF16),
+        pltpu.VMEM((S, 2 * C, (DE + held) // 2, BW), BF16),
+        pltpu.VMEM((S, (DE + held) // 2, BW), BF16),
         pltpu.VMEM((S, DE // 2, BW), BF16),
         pltpu.VMEM((2, DE // 2, BW), BF16),
-        pltpu.VMEM((S, held, 2 * EP), BF16),
-        pltpu.VMEM((S, 2 * C, held // 2, BW), BF16),
-        pltpu.VMEM((S, held // 2, BW), BF16),
         pltpu.VMEM((S, held // 2, BW), BF16),
         pltpu.VMEM((2, held // 2, BW), BF16),
         pltpu.VMEM((S, EP, EP), BF16),
@@ -1328,7 +1331,7 @@
         dma, dma, dma, dma, dma, dma, dma, dma,
         dma, dma((B,)), dma, dma, dma, dma((B,)), dma,
         dma, dma, dma, dma, dma,
-        dma((2, S, 2 * C)), dma((2, S, 2 * C)), dma((2, S)), dma((2, S)), dma((5 + B, C)), dma((5 + B, C)),
+        dma((S, 2 * C)), dma((S, 2 * C)), dma((2, S)), dma((2, S)), dma((5 + B, C)), dma((5 + B, C)),
         dma((B, C // 2)), dma((2, 2, S // 2)), dma((2, S)), dma((2, S)), dma((2, S)),
     ]
     return pl.pallas_call(

time: 469 us -> 461 us (0.983)
  Pallas kernels: 462 us -> 454 us
    pallas_call x1, Pallas kernels: 449 us -> 441 us  [run_relay(): pl.pallas_call(functools.partial(relay_kernel, dims), out_shape=(sds((BN,...]
where the time goes in v4:
time: 461 us
  Pallas kernels  454 us (98%)
    pallas_call x1, Pallas kernels, run_relay(): pl.pallas_call(functools.partial(relay_kernel, dims), out_shape=(sds((BN,...  441 us
    pallas_call x1, Pallas kernels, run_gradients(): pl.pallas_call(functools.partial(gradient_kernel, dims), out_shape=tuple(...  12.9 us
  transfers between devices with their start and end apart: 1, of which 0 were waited for; matrix products, arithmetic and copies ran while one was open for 0% of the time, Pallas kernels for 0%

profile of v4, /device:TPU:0, one launch (start us, length us, event | category | flops | bytes accessed | tf_op | source)
XLA Modules:
  0.0 460.9 jit_solution(4873878980532292997)
XLA Ops:
  0.6 0.0 copy-start
  0.7 0.8 copy-done
  1.5 0.1 constant_dynamic-slice_fusion
  1.6 0.3 fusion.2
  1.9 0.0 copy-start.2
  2.0 1.3 dynamic-slice_bitcast_fusion
  3.3 0.0 copy-start.4
  3.3 0.0 copy-start.3
  3.3 0.2 fusion.4
  3.5 0.5 collective-permute-start
  4.0 0.0 copy-done.2
  4.0 0.1 slice_bitcast_fusion.1
  4.2 0.9 fusion.3.ep
  5.1 0.0 copy-done.4
  5.1 0.0 copy-done.3
  5.1 0.7 add_cosine_fusion.mix
  5.7 0.0 collective-permute-done
  5.8 0.3 fusion.6
  6.0 0.0 copy-start.1
  6.0 0.1 slice.12
  6.2 0.8 copy.40
  6.9 0.0 copy-done.1
  7.0 440.9 %shard_map.307 = (bf16[128,512]{1,0:T(8,128)(2,1)}, bf16[128,512]{1,0:T(8,128)(2,1)}, bf16[4,128,2048]{2,1,0:T(8,128)(2,1)}, bf16[4,128,1536]{2,1,0:T(8,128)(2,1...) custom-call(bf16[960,256]{1,0:T(8,128)(2,1)} %bitcast.41, ...), custom_call_target="tpu_custom_call" | custom-call | tf_op jit(solution)/shard_map/pallas_call | solution.py:1337
  447.9 12.9 %shard_map.308 = (f32[1,512,1024]{2,1,0:T(8,128)}, f32[1,192,512]{2,1,0:T(8,128)}, f32[1,512,512]{2,1,0:T(8,128)}, f32[1,512,2048]{2,1,0:T(8,128)}, f32[1,2048,5...) custom-call(bf16[512,2048]{1,0:T(8,128)(2,1)} %bitcast.42, ...), custom_call_target="tpu_custom_call" | custom-call | tf_op jit(solution)/shard_map/pallas_call | solution.py:1468
  (2 shorter events, 0.0 us)
Async XLA Ops:
  0.6 0.8 copy-start
  1.9 2.1 copy-start.2
  3.3 1.8 copy-start.4
  3.3 1.8 copy-start.3
  3.5 2.2 collective-permute-start
  6.0 0.9 copy-start.1

commit v5 on v4

--- a/solution.py
+++ b/solution.py
@@ -451,6 +451,18 @@
     return jnp.sum(x, axis=0, keepdims=True)
 
 
+def protein_on(plane, B):
+    if B != 2:
+        return plane
+    return jnp.where(plane == 0, 0, jnp.where(plane == 3, 1, plane + 1))
+
+
+def plane_of(protein, B):
+    if B != 2:
+        return protein
+    return jnp.where(protein == 0, 0, jnp.where(protein == 1, 3, protein - 1))
+
+
 def relay_kernel(
     dims,
     ecat0, oht, mix, clean, noise, cot, pw, mo, fi, fo, ep, gains, shifts, node_b, fb, edge_b, we_own, ws_own, wo_own,
@@ -475,8 +487,9 @@
     pair = me_d - core
     w = lax.div(me_s, 2)
     q = 2 * lax.rem(me_s, 2) + core
-    owner_d = pair + lax.div(w, B)
-    slot = lax.rem(w, B)
+    protein = protein_on(w, B)
+    owner_d = pair + lax.div(protein, B)
+    slot = lax.rem(protein, B)
     my_row = pl.multiple_of(slot * N + q * Q, Q)
     own_rows = pl.ds(top, Q)
 
@@ -508,18 +521,21 @@
             arrive(ref, sem)
 
     def worker_of(p, j):
-        return 2 * (core * B + p) + j // 2, pair + j % 2
+        return 2 * plane_of(core * B + p, B) + j // 2, pair + j % 2
 
     def peer(k):
         j = lax.rem(q + k, 4)
         return j, 2 * w + lax.div(j, 2), pair + lax.rem(j, 2)
 
-    works_here = lax.div(w, B) == core
+    works_here = lax.div(protein, B) == core
 
     def at(p, first=0, size=16):
         return pl.ds(pl.multiple_of(p * N + first, size), size)
 
-    near = jnp.clip(w - core * B, 0, B - 1)
+    away = [jnp.abs(plane_of(core * B + p, B) - w) for p in range(B)]
+    near = 0
+    for p in range(1, B):
+        near = jnp.where(away[p] < functools.reduce(jnp.minimum, away[:p]), p, near)
 
     load = pltpu.make_async_copy(ecat0, ecat.at[0], ld_sem)
     load.start()
@@ -1503,7 +1519,7 @@
     Q = N // 4
     EP = DE + N
     core = column % 2
-    w = place // 2
+    w = protein_on(place // 2, B)
     slab = (place % 2) * 2 * Q
 
     node_ids = jnp.arange(N, dtype=jnp.int32)

time: 461 us -> 472 us (1.024)
  Pallas kernels: 454 us -> 465 us
    pallas_call x1, Pallas kernels: 441 us -> 452 us  [run_relay(): pl.pallas_call(functools.partial(relay_kernel, dims), out_shape=(sds((BN,...]
where the time goes in v5:
time: 472 us
  Pallas kernels  465 us (99%)
    pallas_call x1, Pallas kernels, run_relay(): pl.pallas_call(functools.partial(relay_kernel, dims), out_shape=(sds((BN,...  452 us
    pallas_call x1, Pallas kernels, run_gradients(): pl.pallas_call(functools.partial(gradient_kernel, dims), out_shape=tuple(...  12.9 us
  transfers between devices with their start and end apart: 1, of which 0 were waited for; matrix products, arithmetic and copies ran while one was open for 0% of the time, Pallas kernels for 0%

profile of v5, /device:TPU:0, one launch (start us, length us, event | category | flops | bytes accessed | tf_op | source)
XLA Modules:
  0.0 472.0 jit_solution(528918656124045504)
XLA Ops:
  0.6 0.0 copy-start
  0.7 0.8 copy-done
  1.5 0.1 constant_dynamic-slice_fusion
  1.6 0.3 fusion.2
  1.9 0.0 copy-start.2
  2.0 1.3 dynamic-slice_bitcast_fusion
  3.3 0.0 copy-start.4
  3.3 0.0 copy-start.3
  3.3 0.2 fusion.4
  3.5 0.5 collective-permute-start
  4.0 0.0 copy-done.2
  4.0 0.1 slice_bitcast_fusion.1
  4.2 0.9 fusion.3.ep
  5.1 0.0 copy-done.4
  5.1 0.0 copy-done.3
  5.1 0.7 add_cosine_fusion.mix
  5.7 0.0 collective-permute-done
  5.8 0.3 fusion.6
  6.0 0.0 copy-start.1
  6.0 0.1 slice.12
  6.2 0.8 copy.40
  6.9 0.0 copy-done.1
  7.0 452.0 %shard_map.307 = (bf16[128,512]{1,0:T(8,128)(2,1)}, bf16[128,512]{1,0:T(8,128)(2,1)}, bf16[4,128,2048]{2,1,0:T(8,128)(2,1)}, bf16[4,128,1536]{2,1,0:T(8,128)(2,1...) custom-call(bf16[960,256]{1,0:T(8,128)(2,1)} %bitcast.41, ...), custom_call_target="tpu_custom_call" | custom-call | tf_op jit(solution)/shard_map/pallas_call | solution.py:1353
  458.9 12.9 %shard_map.308 = (f32[1,512,1024]{2,1,0:T(8,128)}, f32[1,192,512]{2,1,0:T(8,128)}, f32[1,512,512]{2,1,0:T(8,128)}, f32[1,512,2048]{2,1,0:T(8,128)}, f32[1,2048,5...) custom-call(bf16[512,2048]{1,0:T(8,128)(2,1)} %bitcast.42, ...), custom_call_target="tpu_custom_call" | custom-call | tf_op jit(solution)/shard_map/pallas_call | solution.py:1484
  (2 shorter events, 0.0 us)
Async XLA Ops:
  0.6 0.8 copy-start
  1.9 2.1 copy-start.2
  3.3 1.8 copy-start.4
  3.3 1.8 copy-start.3
  3.5 2.2 collective-permute-start
  6.0 0.9 copy-start.1

commit v6 on v4

--- a/solution.py
+++ b/solution.py
@@ -782,7 +782,7 @@
             def _():
                 rows_out(p, pq_s, pq_r, pq_ss, pq_rs)
 
-            @pl.when((n == 0) & works_here)
+            @pl.when(n == 0)
             def _():
                 pass_on(step)
 
@@ -910,7 +910,7 @@
         def _():
             prepare(t)
 
-        @pl.when(jnp.logical_not((me_s == t) & works_here))
+        @pl.when(me_s != t)
         def _():
             pass_on(step)
 

time: 461 us -> 466 us (1.011)
  Pallas kernels: 454 us -> 459 us
    pallas_call x1, Pallas kernels: 441 us -> 446 us  [run_relay(): pl.pallas_call(functools.partial(relay_kernel, dims), out_shape=(sds((BN,...]
where the time goes in v6:
time: 466 us
  Pallas kernels  459 us (98%)
    pallas_call x1, Pallas kernels, run_relay(): pl.pallas_call(functools.partial(relay_kernel, dims), out_shape=(sds((BN,...  446 us
    pallas_call x1, Pallas kernels, run_gradients(): pl.pallas_call(functools.partial(gradient_kernel, dims), out_shape=tuple(...  12.9 us
  transfers between devices with their start and end apart: 1, of which 0 were waited for; matrix products, arithmetic and copies ran while one was open for 0% of the time, Pallas kernels for 0%

profile of v6, /device:TPU:0, one launch (start us, length us, event | category | flops | bytes accessed | tf_op | source)
XLA Modules:
  0.0 465.9 jit_solution(5942849322044660170)
XLA Ops:
  0.6 0.0 copy-start
  0.7 0.8 copy-done
  1.5 0.1 constant_dynamic-slice_fusion
  1.6 0.3 fusion.2
  1.9 0.0 copy-start.2
  2.0 1.3 dynamic-slice_bitcast_fusion
  3.3 0.0 copy-start.4
  3.3 0.0 copy-start.3
  3.3 0.2 fusion.4
  3.5 0.5 collective-permute-start
  4.0 0.0 copy-done.2
  4.0 0.1 slice_bitcast_fusion.1
  4.2 0.9 fusion.3.ep
  5.1 0.0 copy-done.4
  5.1 0.0 copy-done.3
  5.1 0.7 add_cosine_fusion.mix
  5.7 0.0 collective-permute-done
  5.8 0.3 fusion.6
  6.0 0.0 copy-start.1
  6.0 0.1 slice.12
  6.2 0.8 copy.40
  6.9 0.0 copy-done.1
  7.0 445.9 %shard_map.307 = (bf16[128,512]{1,0:T(8,128)(2,1)}, bf16[128,512]{1,0:T(8,128)(2,1)}, bf16[4,128,2048]{2,1,0:T(8,128)(2,1)}, bf16[4,128,1536]{2,1,0:T(8,128)(2,1...) custom-call(bf16[960,256]{1,0:T(8,128)(2,1)} %bitcast.41, ...), custom_call_target="tpu_custom_call" | custom-call | tf_op jit(solution)/shard_map/pallas_call | solution.py:1337
  452.8 12.9 %shard_map.308 = (f32[1,512,1024]{2,1,0:T(8,128)}, f32[1,192,512]{2,1,0:T(8,128)}, f32[1,512,512]{2,1,0:T(8,128)}, f32[1,512,2048]{2,1,0:T(8,128)}, f32[1,2048,5...) custom-call(bf16[512,2048]{1,0:T(8,128)(2,1)} %bitcast.42, ...), custom_call_target="tpu_custom_call" | custom-call | tf_op jit(solution)/shard_map/pallas_call | solution.py:1468
  (2 shorter events, 0.0 us)
Async XLA Ops:
  0.6 0.8 copy-start
  1.9 2.1 copy-start.2
  3.3 1.8 copy-start.4
  3.3 1.8 copy-start.3
  3.5 2.2 collective-permute-start
  6.0 0.9 copy-start.1

commit v7 on v4

--- a/solution.py
+++ b/solution.py
@@ -520,6 +520,7 @@
         return pl.ds(pl.multiple_of(p * N + first, size), size)
 
     near = jnp.clip(w - core * B, 0, B - 1)
+    leading = jnp.where(works_here, near, B - 1 - near)
 
     load = pltpu.make_async_copy(ecat0, ecat.at[0], ld_sem)
     load.start()
@@ -732,7 +733,7 @@
         later = lax.rem(me_s + 1, S)
 
         def turn(n, carry):
-            p = lax.rem(near + n, B)
+            p = lax.rem(leading + n, B)
             whole = at(p, 0, N)
             arrive(mb_r.at[whole], mb_rs.at[p])
             mean = mm(mb_r[whole, :], mo[...])
@@ -1054,7 +1055,7 @@
             arrive(dh1_r, dh_rs)
 
         def turn(n, carry):
-            p = lax.rem(near + n, B)
+            p = lax.rem(leading + n, B)
             whole = at(p, 0, N)
 
             @pl.when(me_s < S - 1)

time: 461 us -> 465 us (level)
  no operation moved by 1% of the time
where the time goes in v7:
time: 465 us
  Pallas kernels  458 us (98%)
    pallas_call x1, Pallas kernels, run_relay(): pl.pallas_call(functools.partial(relay_kernel, dims), out_shape=(sds((BN,...  445 us
    pallas_call x1, Pallas kernels, run_gradients(): pl.pallas_call(functools.partial(gradient_kernel, dims), out_shape=tuple(...  12.9 us
  transfers between devices with their start and end apart: 1, of which 0 were waited for; matrix products, arithmetic and copies ran while one was open for 0% of the time, Pallas kernels for 0%

profile of v7, /device:TPU:0, one launch (start us, length us, event | category | flops | bytes accessed | tf_op | source)
XLA Modules:
  0.0 464.9 jit_solution(5610811707333204628)
XLA Ops:
  0.6 0.0 copy-start
  0.7 0.8 copy-done
  1.5 0.1 constant_dynamic-slice_fusion
  1.6 0.3 fusion.2
  1.9 0.0 copy-start.2
  2.0 1.3 dynamic-slice_bitcast_fusion
  3.3 0.0 copy-start.4
  3.3 0.0 copy-start.3
  3.3 0.2 fusion.4
  3.5 0.5 collective-permute-start
  4.0 0.0 copy-done.2
  4.0 0.1 slice_bitcast_fusion.1
  4.2 0.9 fusion.3.ep
  5.1 0.0 copy-done.4
  5.1 0.0 copy-done.3
  5.1 0.7 add_cosine_fusion.mix
  5.7 0.0 collective-permute-done
  5.8 0.3 fusion.6
  6.0 0.0 copy-start.1
  6.0 0.1 slice.12
  6.2 0.8 copy.40
  6.9 0.0 copy-done.1
  7.0 444.9 %shard_map.307 = (bf16[128,512]{1,0:T(8,128)(2,1)}, bf16[128,512]{1,0:T(8,128)(2,1)}, bf16[4,128,2048]{2,1,0:T(8,128)(2,1)}, bf16[4,128,1536]{2,1,0:T(8,128)(2,1...) custom-call(bf16[960,256]{1,0:T(8,128)(2,1)} %bitcast.41, ...), custom_call_target="tpu_custom_call" | custom-call | tf_op jit(solution)/shard_map/pallas_call | solution.py:1338
  451.8 12.9 %shard_map.308 = (f32[1,512,1024]{2,1,0:T(8,128)}, f32[1,192,512]{2,1,0:T(8,128)}, f32[1,512,512]{2,1,0:T(8,128)}, f32[1,512,2048]{2,1,0:T(8,128)}, f32[1,2048,5...) custom-call(bf16[512,2048]{1,0:T(8,128)(2,1)} %bitcast.42, ...), custom_call_target="tpu_custom_call" | custom-call | tf_op jit(solution)/shard_map/pallas_call | solution.py:1469
  (2 shorter events, 0.0 us)
Async XLA Ops:
  0.6 0.8 copy-start
  1.9 2.1 copy-start.2
  3.3 1.8 copy-start.4
  3.3 1.8 copy-start.3
  3.5 2.2 collective-permute-start
  6.0 0.9 copy-start.1

commit v8 on v4

--- a/solution.py
+++ b/solution.py
@@ -453,14 +453,14 @@
 
 def relay_kernel(
     dims,
-    ecat0, oht, mix, clean, noise, cot, pw, mo, fi, fo, ep, gains, shifts, node_b, fb, edge_b, we_own, ws_own, wo_own,
+    edges_in, near_in, mix, clean, noise, cot, pw, mo, fi, fo, ends, gains, shifts, node_b, fb, edge_b, we_own, ws_own, wo_own,
     act, ig, g_fwd, g_bwd, g_dpq, g_small, g_msg, g_upd,
-    start, par, eb0, wall_msg, wall_upd, fwd, bwd, sg,
+    ep, e0, nb0, oht, start, par, eb0, wall_msg, wall_upd, fwd, bwd, sg,
     eg, eg_r, eg_b, msg_o, msg_f, upd_o, upd_f, wo, eb1,
     ecat, wcat, scat, pwn, parn, hin_r, hst, mb_s, mb_r, pq_s, pq_r, rq_s, rq_r,
     un0, un1, un2, hi_s, sc0, sc1, sc2, sci, u_s, slope_s, de, dacc, gp, gpe, dcat, act_t, edge_t,
     x_s, x_r, row_s, row_r, dpqo_r, dmb_s, dmb_r, dh1_s, dh1_r, dh1_f, dh2_s, dn3_s, da2_s, h1_s, a1_s,
-    ld_sem, nx_ss, nx_rs, hop_ss, hop_rs,
+    ld_sem, ld_ss, nx_ss, nx_rs, hop_ss, hop_rs,
     pq_ss, pq_rs, ag_ss, ag_rs, rq_ss, rq_rs, ag2_ss, ag2_rs,
     mb_ss, mb_rs, x_ss, x_rs, row_ss, row_rs, dpqo_rs, fw_ss, dmb_ss, dmb_rs, dh_ss, dh_rs,
     e1_ss, e1_rs, e2_ss, e2_rs, g_ss, g_rs, relay_ss, ring_ss, ring_rs, sib_ss, sib_rs,
@@ -521,8 +521,6 @@
 
     near = jnp.clip(w - core * B, 0, B - 1)
 
-    load = pltpu.make_async_copy(ecat0, ecat.at[0], ld_sem)
-    load.start()
     barrier = pltpu.get_barrier_semaphore()
     for sec in range(S):
         for c in range(C):
@@ -588,6 +586,43 @@
 
     for side in range(2):
         ring_send(0, me_s, side, 0)
+
+    ep[...] = jnp.zeros_like(ep)
+    ep[:, pl.ds(0, DE)] = ends[:, pl.ds(0, DE)]
+    ep[:, pl.ds(EP, DE)] = ends[...].astype(F32)[:, DE:].astype(BF16)
+
+    arrays = ((edges_in, e0), (near_in, nb0))
+
+    def quarter_of(n, j):
+        rows = pl.ds(pl.multiple_of(j * Q, Q), Q)
+        return edges_in.at[slot, :, rows] if n == 0 else near_in.at[slot, rows]
+
+    @pl.when(works_here)
+    def _():
+        for n, (_, dst) in enumerate(arrays):
+            pltpu.make_async_copy(quarter_of(n, q), dst, ld_sem.at[n]).start()
+            other = q + 1 - 2 * core
+            far(quarter_of(n, other), dst, ld_ss.at[n], ld_sem.at[n], me_s, pair + 1 - core).start()
+
+    def edges_laid_out():
+        for n, (_, dst) in enumerate(arrays):
+            arrive(dst, ld_sem.at[n])
+        nearest = nb0[...]
+        lane = lax.broadcasted_iota(jnp.int32, (Q, EP), 1) - DE
+        for k in range(K):
+            rows = pl.ds(k * Q, Q)
+            ecat[0, rows, :] = jnp.where(lane == nearest[:, k : k + 1], 1.0, 0.0).astype(BF16)
+            ecat[0, rows, pl.ds(0, DE)] = e0[k]
+        node = lax.broadcasted_iota(jnp.int32, (N, EP), 0)
+        lane = lax.broadcasted_iota(jnp.int32, (N, EP), 1) - DE
+        chosen = jnp.where(lane == node, 1.0, 0.0).astype(BF16)
+        oht[...] = mm_bt(chosen, ecat[0]).astype(BF16)
+
+        @pl.when(works_here)
+        def _():
+            for n, (_, dst) in enumerate(arrays):
+                arrive(dst, ld_ss.at[n])
+
     before = lax.rem(me_s + S - 1, S)
     far(pw, pwn, nx_ss.at[0], nx_rs.at[0], before, me_d).start()
     far(par, parn, nx_ss.at[1], nx_rs.at[1], before, me_d).start()
@@ -928,10 +963,11 @@
         return carry
 
     for hop, side in hops:
+        if (hop, side) == (2, 0):
+            edges_laid_out()
         ring_hop(0, side, hop)
     for side in range(2):
         ring_send(1, me_s, side, 0)
-    load.wait()
     spread(pq_r, D, wcat, 0, ag_ss, ag_rs, pq_rs)
     lax.fori_loop(0, 2 * S, forward_step, 0)
     ring_drain()
@@ -1265,6 +1301,10 @@
     tile = 32
     held = -(-(DE + 16) // tile) * tile
     scratch = [
+        pltpu.VMEM((D, 2 * EP), BF16),
+        pltpu.VMEM((K, Q, DE), BF16),
+        pltpu.VMEM((Q, K), jnp.int32),
+        pltpu.VMEM((N, R), BF16),
         pltpu.VMEM((BN, D), F32),
         pltpu.VMEM((8, D), F32),
         pltpu.VMEM((1, EP), F32),
@@ -1327,7 +1367,7 @@
         pltpu.VMEM((BN, D), F32),
         pltpu.VMEM((BN, D), F32),
         pltpu.VMEM((BN, D), BF16),
-        dma, dma((2,)), dma((2,)), dma, dma,
+        dma((2,)), dma((2,)), dma((2,)), dma((2,)), dma, dma,
         dma, dma, dma, dma, dma, dma, dma, dma,
         dma, dma((B,)), dma, dma, dma, dma((B,)), dma,
         dma, dma, dma, dma, dma,
@@ -1346,7 +1386,7 @@
             sds((C, 2, DE // 2, BW), BF16),
             sds((C, 2, held // 2, BW), BF16),
         ),
-        in_specs=[hbm, vm, pl.BlockSpec(memory_space=pltpu.SMEM)] + [vm] * 16,
+        in_specs=[hbm, hbm, pl.BlockSpec(memory_space=pltpu.SMEM)] + [vm] * 16,
         out_specs=(vm,) * 2 + (hbm,) * 6,
         scratch_shapes=scratch,
         compiler_params=pltpu.CompilerParams(
@@ -1495,48 +1535,24 @@
     norm_gain, norm_shift, node_bias, ffn_bias, edge_bias,
 ):
     S = lax.axis_size("section")
-    place = lax.axis_index("section")
-    column = lax.axis_index("dp")
     B, N, D = clean_nodes.shape
     K, DE = edge_feats.shape[2:]
     FF = ffn_in.shape[2]
     Q = N // 4
     EP = DE + N
-    core = column % 2
-    w = place // 2
-    slab = (place % 2) * 2 * Q
-
-    node_ids = jnp.arange(N, dtype=jnp.int32)
-    both = [
-        lax.dynamic_slice(array, (w % B, slab) + (0,) * (array.ndim - 2), (1, 2 * Q) + array.shape[2:])[0]
-        for array in (edge_feats, neighbours)
-    ]
-    chosen = (both[1][:, :, None] == node_ids).astype(BF16)
-    both = jnp.concatenate([both[0], chosen], axis=2)
-    mine = lax.dynamic_slice_in_dim(both, core * Q, Q, 0)
-    theirs = lax.dynamic_slice_in_dim(both, (1 - core) * Q, Q, 0)
-    got = lax.ppermute(theirs, "dp", [(i, i ^ 1) for i in range(lax.axis_size("dp"))])
-    ecat0 = jnp.swapaxes(jnp.where(w // B == core, mine, got), 0, 1).reshape(K * Q, EP)
-    oht = jnp.transpose(ecat0[:, DE:])
     phase = (time_bins.astype(F32) + 0.5) * (math.pi * 0.5 / TBINS)
     mix = jnp.cos(phase[None] - jnp.array([[0.0], [math.pi * 0.5]], F32))
 
     def by_rows(array):
         return jnp.transpose(array, (1, 0, 2))
 
-    def widen(array, size, axis=-1):
-        extra = [(0, 0)] * array.ndim
-        extra[axis] = (0, size - array.shape[axis])
-        return jnp.pad(array, extra)
-
-    ep = jnp.concatenate([widen(edge_pair[0, :, :DE], EP), widen(edge_pair[0, :, DE:], EP)], axis=1)
     C = lax.axis_size("dp")
     dims = (S, B, N, K, Q, D, DE, EP, FF, C)
     act, ig, g_fwd, g_bwd, g_dpq, g_small, g_msg, g_upd = run_relay(
         dims,
         (
-            ecat0, oht, mix, clean_nodes.reshape(B * N, D), noise_nodes.reshape(B * N, D),
-            cotangent.reshape(B * N, D), pair_weight[0], message_out[0], ffn_in[0], ffn_out[0], ep,
+            jnp.transpose(edge_feats, (0, 2, 1, 3)), neighbours, mix, clean_nodes.reshape(B * N, D), noise_nodes.reshape(B * N, D),
+            cotangent.reshape(B * N, D), pair_weight[0], message_out[0], ffn_in[0], ffn_out[0], edge_pair[0],
             by_rows(norm_gain), by_rows(norm_shift), by_rows(node_bias), ffn_bias, edge_bias[0],
             message_edge[0], edge_self[0], edge_out[0],
         ),

time: 461 us -> 459 us (level)
  transfers between devices with their start and end apart: 1 -> 0, of which waited for: 0 -> 0; matrix products, arithmetic and copies ran while one was open for 0% -> 0% of each run, Pallas kernels for 0% -> 0%
where the time goes in v8:
time: 459 us; the launch traced here: 458 us
  Pallas kernels  454 us (99%)
    pallas_call x1, Pallas kernels, run_relay(): pl.pallas_call(functools.partial(relay_kernel, dims), out_shape=(sds((BN,...  441 us
    pallas_call x1, Pallas kernels, run_gradients(): pl.pallas_call(functools.partial(gradient_kernel, dims), out_shape=tuple(...  12.9 us

profile of v8, /device:TPU:0, one launch (start us, length us, event | category | flops | bytes accessed | tf_op | source)
XLA Modules:
  0.0 458.4 jit_solution(6433444236386552876)
XLA Ops:
  0.6 0.7 add_multiply_fusion
  1.3 1.3 add_cosine_fusion.mix
  2.6 1.5 copy.35.near_in
  4.2 441.1 %shard_map.307 = (bf16[128,512]{1,0:T(8,128)(2,1)}, bf16[128,512]{1,0:T(8,128)(2,1)}, bf16[4,128,2048]{2,1,0:T(8,128)(2,1)}, bf16[4,128,1536]{2,1,0:T(8,128)(2,1...) custom-call(bf16[2,60,64,192]{3,2,1,0:T(8,128)(2,1)} %bitcast.28, ...), custom_call_target="tpu_custom_call" | custom-call | tf_op jit(solution)/shard_map/pallas_call | solution.py:1377
  445.3 12.9 %shard_map.308 = (f32[1,512,1024]{2,1,0:T(8,128)}, f32[1,192,512]{2,1,0:T(8,128)}, f32[1,512,512]{2,1,0:T(8,128)}, f32[1,512,2048]{2,1,0:T(8,128)}, f32[1,2048,5...) custom-call(bf16[512,2048]{1,0:T(8,128)(2,1)} %bitcast.29, ...), custom_call_target="tpu_custom_call" | custom-call | tf_op jit(solution)/shard_map/pallas_call | solution.py:1508

commit v9 on v8

--- a/solution.py
+++ b/solution.py
@@ -453,14 +453,14 @@
 
 def relay_kernel(
     dims,
-    edges_in, near_in, mix, clean, noise, cot, pw, mo, fi, fo, ends, gains, shifts, node_b, fb, edge_b, we_own, ws_own, wo_own,
+    edges_in, near_in, mix, clean, noise, cot, pw_in, mo_in, fi_in, fo_in, ends, gains, shifts, node_b, fb, edge_b, we_own, ws_own, wo_own,
     act, ig, g_fwd, g_bwd, g_dpq, g_small, g_msg, g_upd,
-    ep, e0, nb0, oht, start, par, eb0, wall_msg, wall_upd, fwd, bwd, sg,
+    pw, mo, fi, fo, fwd_t, ep, e0, nb0, oht, start, par, eb0, wall_msg, wall_upd, fwd, bwd, sg,
     eg, eg_r, eg_b, msg_o, msg_f, upd_o, upd_f, wo, eb1,
     ecat, wcat, scat, pwn, parn, hin_r, hst, mb_s, mb_r, pq_s, pq_r, rq_s, rq_r,
     un0, un1, un2, hi_s, sc0, sc1, sc2, sci, u_s, slope_s, de, dacc, gp, gpe, dcat, act_t, edge_t,
     x_s, x_r, row_s, row_r, dpqo_r, dmb_s, dmb_r, dh1_s, dh1_r, dh1_f, dh2_s, dn3_s, da2_s, h1_s, a1_s,
-    ld_sem, ld_ss, nx_ss, nx_rs, hop_ss, hop_rs,
+    ld_sem, ld_ss, w_sem, nx_ss, nx_rs, hop_ss, hop_rs,
     pq_ss, pq_rs, ag_ss, ag_rs, rq_ss, rq_rs, ag2_ss, ag2_rs,
     mb_ss, mb_rs, x_ss, x_rs, row_ss, row_rs, dpqo_rs, fw_ss, dmb_ss, dmb_rs, dh_ss, dh_rs,
     e1_ss, e1_rs, e2_ss, e2_rs, g_ss, g_rs, relay_ss, ring_ss, ring_rs, sib_ss, sib_rs,
@@ -521,6 +521,12 @@
 
     near = jnp.clip(w - core * B, 0, B - 1)
 
+    weights = [
+        pltpu.make_async_copy(src, dst, w_sem.at[n])
+        for n, (src, dst) in enumerate(((pw_in, pw), (mo_in, mo), (fi_in, fi), (fo_in, fo)))
+    ]
+    for weight in weights:
+        weight.start()
     barrier = pltpu.get_barrier_semaphore()
     for sec in range(S):
         for c in range(C):
@@ -604,7 +610,12 @@
             other = q + 1 - 2 * core
             far(quarter_of(n, other), dst, ld_ss.at[n], ld_sem.at[n], me_s, pair + 1 - core).start()
 
+    weights[0].wait()
+
     def edges_laid_out():
+        for weight in weights[1:]:
+            weight.wait()
+
         for n, (_, dst) in enumerate(arrays):
             arrive(dst, ld_sem.at[n])
         nearest = nb0[...]
@@ -624,7 +635,7 @@
                 arrive(dst, ld_ss.at[n])
 
     before = lax.rem(me_s + S - 1, S)
-    far(pw, pwn, nx_ss.at[0], nx_rs.at[0], before, me_d).start()
+    far(pw_in, pwn, nx_ss.at[0], nx_rs.at[0], before, me_d).start()
     far(par, parn, nx_ss.at[1], nx_rs.at[1], before, me_d).start()
 
     for p in range(B):
@@ -841,7 +852,9 @@
                 for c in range(chunks):
                     cols = pl.ds(c * FC, FC)
                     slope_s[rows, cols] = gelu_both(u_s[rows, cols])[1].astype(BF16)
-            share(0, fwd, g_fwd)
+            for n in range(4):
+                fwd_t[pl.ds(n * D, D), :] = fwd[:, pl.ds(n * D, D)].T
+            share(0, fwd_t, g_fwd)
 
     def pair_norm(rows, hidden, first):
         unit, scale = normed(hidden)
@@ -1279,7 +1292,7 @@
         drain(eg_b.at[t, pl.ds(0, HM)], e2_ss.at[0, t], t, me_d)
         if t > 0:
             drain(eg_b.at[t, pl.ds(HM, HU)], e2_ss.at[1, t], t - 1, me_d)
-    share_wait(0, fwd, g_fwd)
+    share_wait(0, fwd_t, g_fwd)
     share_wait(1, bwd, g_bwd)
     for p in range(B):
         share_near_wait(2 + p, dpqo_r.at[across[p]], lambda c, p=p: g_dpq.at[c, across[p]])
@@ -1301,6 +1314,11 @@
     tile = 32
     held = -(-(DE + 16) // tile) * tile
     scratch = [
+        pltpu.VMEM((D, 2 * D), BF16),
+        pltpu.VMEM((D, D), BF16),
+        pltpu.VMEM((D, FF), BF16),
+        pltpu.VMEM((FF, D), BF16),
+        pltpu.VMEM((4 * D, BN), BF16),
         pltpu.VMEM((D, 2 * EP), BF16),
         pltpu.VMEM((K, Q, DE), BF16),
         pltpu.VMEM((Q, K), jnp.int32),
@@ -1367,7 +1385,7 @@
         pltpu.VMEM((BN, D), F32),
         pltpu.VMEM((BN, D), F32),
         pltpu.VMEM((BN, D), BF16),
-        dma((2,)), dma((2,)), dma((2,)), dma((2,)), dma, dma,
+        dma((2,)), dma((2,)), dma((4,)), dma((2,)), dma((2,)), dma, dma,
         dma, dma, dma, dma, dma, dma, dma, dma,
         dma, dma((B,)), dma, dma, dma, dma((B,)), dma,
         dma, dma, dma, dma, dma,
@@ -1379,14 +1397,14 @@
         out_shape=(
             sds((BN, D), BF16),
             sds((BN, D), BF16),
-            sds((C, BN, 4 * D), BF16),
+            sds((C, 4 * D, BN), BF16),
             sds((C, BN, 2 * D + 2 * EP), BF16),
             sds((C, BN, 2 * D), BF16),
             sds((C, 24, D), F32),
             sds((C, 2, DE // 2, BW), BF16),
             sds((C, 2, held // 2, BW), BF16),
         ),
-        in_specs=[hbm, hbm, pl.BlockSpec(memory_space=pltpu.SMEM)] + [vm] * 16,
+        in_specs=[hbm, hbm, pl.BlockSpec(memory_space=pltpu.SMEM)] + [vm] * 3 + [hbm] * 4 + [vm] * 9,
         out_specs=(vm,) * 2 + (hbm,) * 6,
         scratch_shapes=scratch,
         compiler_params=pltpu.CompilerParams(
@@ -1414,17 +1432,28 @@
         loads[name] = pltpu.make_async_copy(src, dst, in_sems.at[len(loads)])
         loads[name].start()
 
-    load("a2", fwd.at[:, part(2)], fwd_v.at[2])
+    BN = B * N
+
+    def load_kept(n):
+        for c in range(C):
+            load((n, c), fwd.at[c, part(n)], fwd_v.at[n, :, part(c, BN)])
+
+    def wait_kept(n):
+        for c in range(C):
+            loads[n, c].wait()
+        return fwd_v[n]
+
+    load_kept(2)
     load("dy", bwd.at[:, part(1)], bwd_v.at[1])
     for c in range(chunks):
         load(("fi", c), fi.at[:, part(c, FC)], fi_v.at[c])
         load(("fo", c), fo.at[part(c, FC)], fo_v.at[c])
-    load("a1", fwd.at[:, part(0)], fwd_v.at[0])
+    load_kept(0)
     load("dpq0", dpq.at[:, part(0)], dpq_v.at[0])
     load("dpq1", dpq.at[:, part(1)], dpq_v.at[1])
-    load("mbar", fwd.at[:, part(1)], fwd_v.at[1])
+    load_kept(1)
     load("dmsg", bwd.at[:, part(0)], bwd_v.at[0])
-    load("a3", fwd.at[:, part(3)], fwd_v.at[3])
+    load_kept(3)
     load("drs", bwd.at[:, part(2)], bwd_v.at[2])
     load("edge", edge, edge_v)
     load("upd", upd, upd_v)
@@ -1437,9 +1466,9 @@
 
     out(act, act_out)
     out(ig, ig_out)
-    loads["a2"].wait()
+    a2_t = wait_kept(2)
+    a2 = a2_t.T
     loads["dy"].wait()
-    a2 = fwd_v[2]
     dy = bwd_v[1]
     for c in range(chunks):
         cols = part(c, FC)
@@ -1448,22 +1477,20 @@
         value, slope = gelu_both(mm(a2, fi_v[c]) + fb[:, cols])
         du = (slope * mm_bt(dy, fo_v[c])).astype(BF16)
         g_fb[:, cols] = col_sum(du.astype(F32))
-        gfi_v[c] = mm_at(a2, du)
+        gfi_v[c] = mm(a2_t, du)
         out(gfi_v.at[c], g_fi.at[0, :, cols])
         gfo_v[c] = mm_at(value.astype(BF16), dy)
         out(gfo_v.at[c], g_fo.at[0, cols])
-    loads["a1"].wait()
+    a1_t = wait_kept(0)
     for c in range(2):
         loads["dpq%d" % c].wait()
-        pair_v[c] = mm_at(fwd_v[0], dpq_v[c])
+        pair_v[c] = mm(a1_t, dpq_v[c])
         out(pair_v.at[c], g_pair.at[0, :, part(c)])
-    loads["mbar"].wait()
     loads["dmsg"].wait()
-    out_v[...] = mm_at(fwd_v[1], bwd_v[0]) * float(K)
+    out_v[...] = mm(wait_kept(1), bwd_v[0]) * float(K)
     out(out_v, g_out.at[0])
-    loads["a3"].wait()
     loads["drs"].wait()
-    ends = mm_at(fwd_v[3], bwd_v[2])
+    ends = mm(wait_kept(3), bwd_v[2])
     g_ep[0] = jnp.concatenate([ends[:, :DE], ends[:, EP : EP + DE]], axis=1)
     total = small[0]
     for c in range(1, C):
@@ -1511,7 +1538,7 @@
         in_specs=[hbm, hbm, hbm, vm, hbm, hbm, hbm, hbm, vm, hbm, hbm],
         out_specs=(hbm, vm, hbm, hbm, hbm) + (vm,) * 8 + (hbm,) * 2,
         scratch_shapes=[
-            pltpu.VMEM((4, rows, D), BF16),
+            pltpu.VMEM((4, D, rows), BF16),
             pltpu.VMEM((3, rows, D), BF16),
             pltpu.VMEM((2, rows, D), BF16),
             pltpu.VMEM((4, D, FF // 4), BF16),
@@ -1522,7 +1549,7 @@
             pltpu.VMEM((D, D), F32),
             pltpu.VMEM((C, 2, DE // 2, BW), BF16),
             pltpu.VMEM((C, 2, held, BW), BF16),
-            pltpu.SemaphoreType.DMA((19,)),
+            pltpu.SemaphoreType.DMA((15 + 4 * C,)),
             pltpu.SemaphoreType.DMA((13,)),
         ],
         compiler_params=pltpu.CompilerParams(vmem_limit_bytes=56 * 1024 * 1024),
@@ -1560,7 +1587,7 @@
     grads = run_gradients(
         dims,
         (
-            g_fwd.reshape(C * B * N, -1), g_bwd.reshape(C * B * N, -1), g_dpq.reshape(C * B * N, -1),
+            g_fwd, g_bwd.reshape(C * B * N, -1), g_dpq.reshape(C * B * N, -1),
             g_small, g_msg, g_upd, ffn_in[0], ffn_out[0], ffn_bias, act.reshape(1, B, N, D), ig.reshape(1, B, N, D),
         ),
     )

time: 459 us -> 456 us (level)
  no operation moved by 1% of the time
where the time goes in v9:
time: 456 us
  Pallas kernels  452 us (99%)
    pallas_call x1, Pallas kernels, run_relay(): pl.pallas_call(functools.partial(relay_kernel, dims), out_shape=(sds((BN,...  439 us
    pallas_call x1, Pallas kernels, run_gradients(): pl.pallas_call(functools.partial(gradient_kernel, dims), out_shape=tuple(...  13.1 us

profile of v9, /device:TPU:0, one launch (start us, length us, event | category | flops | bytes accessed | tf_op | source)
XLA Modules:
  0.0 456.2 jit_solution(16030545896311004059)
XLA Ops:
  0.6 0.7 add_multiply_fusion
  1.3 1.3 add_cosine_fusion.mix
  2.6 1.5 copy.35.near_in
  4.2 438.7 %shard_map.307 = (bf16[128,512]{1,0:T(8,128)(2,1)}, bf16[128,512]{1,0:T(8,128)(2,1)}, bf16[4,2048,128]{2,1,0:T(8,128)(2,1)}, bf16[4,128,1536]{2,1,0:T(8,128)(2,1...) custom-call(bf16[2,60,64,192]{3,2,1,0:T(8,128)(2,1)} %bitcast.27, ...), custom_call_target="tpu_custom_call" | custom-call | tf_op jit(solution)/shard_map/pallas_call | solution.py:1395
  442.9 13.1 %shard_map.308 = (f32[1,512,1024]{2,1,0:T(8,128)}, f32[1,192,512]{2,1,0:T(8,128)}, f32[1,512,512]{2,1,0:T(8,128)}, f32[1,512,2048]{2,1,0:T(8,128)}, f32[1,2048,5...) custom-call(bf16[4,2048,128]{2,1,0:T(8,128)(2,1)} %get-tuple-element, ...), custom_call_target="tpu_custom_call" | custom-call | tf_op jit(solution)/shard_map/pallas_call | solution.py:1535

commit v10 on v9

--- a/solution.py
+++ b/solution.py
@@ -453,9 +453,9 @@
 
 def relay_kernel(
     dims,
-    edges_in, near_in, mix, clean, noise, cot, pw_in, mo_in, fi_in, fo_in, ends, gains, shifts, node_b, fb, edge_b, we_own, ws_own, wo_own,
+    edges_in, near_in, bins, clean, noise, cot, pw_in, mo_in, fi_in, fo_in, ends, gains, shifts, node_b, fb, edge_b, we_own, ws_own, wo_own,
     act, ig, g_fwd, g_bwd, g_dpq, g_small, g_msg, g_upd,
-    pw, mo, fi, fo, fwd_t, ep, e0, nb0, oht, start, par, eb0, wall_msg, wall_upd, fwd, bwd, sg,
+    pw, mo, fi, fo, fwd_t, ep, e0, nb0, nb1, nb2, oht, start, par, eb0, wall_msg, wall_upd, fwd, bwd, sg,
     eg, eg_r, eg_b, msg_o, msg_f, upd_o, upd_f, wo, eb1,
     ecat, wcat, scat, pwn, parn, hin_r, hst, mb_s, mb_r, pq_s, pq_r, rq_s, rq_r,
     un0, un1, un2, hi_s, sc0, sc1, sc2, sci, u_s, slope_s, de, dacc, gp, gpe, dcat, act_t, edge_t,
@@ -600,8 +600,7 @@
     arrays = ((edges_in, e0), (near_in, nb0))
 
     def quarter_of(n, j):
-        rows = pl.ds(pl.multiple_of(j * Q, Q), Q)
-        return edges_in.at[slot, :, rows] if n == 0 else near_in.at[slot, rows]
+        return edges_in.at[slot, :, pl.ds(pl.multiple_of(j * Q, Q), Q)] if n == 0 else near_in
 
     @pl.when(works_here)
     def _():
@@ -618,8 +617,14 @@
 
         for n, (_, dst) in enumerate(arrays):
             arrive(dst, ld_sem.at[n])
-        nearest = nb0[...]
-        lane = lax.broadcasted_iota(jnp.int32, (Q, EP), 1) - DE
+        by_step = nb0[:, 0, :]
+        for p in range(1, B):
+            by_step = jnp.where(slot == p, nb0[:, p, :], by_step)
+        nb1[...] = jnp.zeros_like(nb1)
+        nb1[pl.ds(0, K), pl.ds(0, N)] = by_step.astype(F32)
+        nb2[...] = nb1[...].T
+        nearest = nb2[pl.ds(pl.multiple_of(q * Q, Q), Q), :]
+        lane = (lax.broadcasted_iota(jnp.int32, (Q, EP), 1) - DE).astype(F32)
         for k in range(K):
             rows = pl.ds(k * Q, Q)
             ecat[0, rows, :] = jnp.where(lane == nearest[:, k : k + 1], 1.0, 0.0).astype(BF16)
@@ -640,7 +645,8 @@
 
     for p in range(B):
         rows = pl.ds(p * N, N)
-        start[rows, :] = mix[0, p] * clean[rows, :].astype(F32) + mix[1, p] * noise[rows, :].astype(F32)
+        phase = jnp.full((1, D), (bins[p].astype(F32) + 0.5) * (math.pi * 0.5 / TBINS), F32)
+        start[rows, :] = jnp.cos(phase) * clean[rows, :].astype(F32) + jnp.sin(phase) * noise[rows, :].astype(F32)
 
     def ring_drain():
         for which in range(2):
@@ -1321,7 +1327,9 @@
         pltpu.VMEM((4 * D, BN), BF16),
         pltpu.VMEM((D, 2 * EP), BF16),
         pltpu.VMEM((K, Q, DE), BF16),
-        pltpu.VMEM((Q, K), jnp.int32),
+        pltpu.VMEM((K, B, N), jnp.int32),
+        pltpu.VMEM((128, 128), F32),
+        pltpu.VMEM((128, 128), F32),
         pltpu.VMEM((N, R), BF16),
         pltpu.VMEM((BN, D), F32),
         pltpu.VMEM((8, D), F32),
@@ -1474,12 +1482,18 @@
         cols = part(c, FC)
         loads["fi", c].wait()
         loads["fo", c].wait()
-        value, slope = gelu_both(mm(a2, fi_v[c]) + fb[:, cols])
-        du = (slope * mm_bt(dy, fo_v[c])).astype(BF16)
+        u = mm(a2, fi_v[c])
+        dv = mm_bt(dy, fo_v[c])
+        v, du = [], []
+        for i in range(0, C * BN, 16):
+            value, slope = gelu_both(u[i : i + 16] + fb[:, cols])
+            v.append(value.astype(BF16))
+            du.append((slope * dv[i : i + 16]).astype(BF16))
+        v, du = stacked(v), stacked(du)
         g_fb[:, cols] = col_sum(du.astype(F32))
         gfi_v[c] = mm(a2_t, du)
         out(gfi_v.at[c], g_fi.at[0, :, cols])
-        gfo_v[c] = mm_at(value.astype(BF16), dy)
+        gfo_v[c] = mm_at(v, dy)
         out(gfo_v.at[c], g_fo.at[0, cols])
     a1_t = wait_kept(0)
     for c in range(2):
@@ -1567,9 +1581,6 @@
     FF = ffn_in.shape[2]
     Q = N // 4
     EP = DE + N
-    phase = (time_bins.astype(F32) + 0.5) * (math.pi * 0.5 / TBINS)
-    mix = jnp.cos(phase[None] - jnp.array([[0.0], [math.pi * 0.5]], F32))
-
     def by_rows(array):
         return jnp.transpose(array, (1, 0, 2))
 
@@ -1578,7 +1589,8 @@
     act, ig, g_fwd, g_bwd, g_dpq, g_small, g_msg, g_upd = run_relay(
         dims,
         (
-            jnp.transpose(edge_feats, (0, 2, 1, 3)), neighbours, mix, clean_nodes.reshape(B * N, D), noise_nodes.reshape(B * N, D),
+            jnp.transpose(edge_feats, (0, 2, 1, 3)), jnp.transpose(neighbours, (2, 0, 1)), time_bins,
+            clean_nodes.reshape(B * N, D), noise_nodes.reshape(B * N, D),
             cotangent.reshape(B * N, D), pair_weight[0], message_out[0], ffn_in[0], ffn_out[0], edge_pair[0],
             by_rows(norm_gain), by_rows(norm_shift), by_rows(node_bias), ffn_bias, edge_bias[0],
             message_edge[0], edge_self[0], edge_out[0],

time: 456 us -> 454 us (level)
  no operation moved by 1% of the time
where the time goes in v10:
time: 454 us
  Pallas kernels  453 us (100%)
    pallas_call x1, Pallas kernels, run_relay(): pl.pallas_call(functools.partial(relay_kernel, dims), out_shape=(sds((BN,...  440 us
    pallas_call x1, Pallas kernels, run_gradients(): pl.pallas_call(functools.partial(gradient_kernel, dims), out_shape=tuple(...  13.1 us

profile of v10, /device:TPU:0, one launch (start us, length us, event | category | flops | bytes accessed | tf_op | source)
XLA Modules:
  0.0 453.7 jit_solution(2837373314105746187)
XLA Ops:
  0.7 439.8 %shard_map.298 = (bf16[128,512]{1,0:T(8,128)(2,1)}, bf16[128,512]{1,0:T(8,128)(2,1)}, bf16[4,2048,128]{2,1,0:T(8,128)(2,1)}, bf16[4,128,1536]{2,1,0:T(8,128)(2,1...) custom-call(bf16[2,60,64,192]{3,2,1,0:T(8,128)(2,1)} %bitcast.28, ...), custom_call_target="tpu_custom_call" | custom-call | tf_op jit(solution)/shard_map/pallas_call | solution.py:1403
  440.5 13.1 %shard_map.299 = (f32[1,512,1024]{2,1,0:T(8,128)}, f32[1,192,512]{2,1,0:T(8,128)}, f32[1,512,512]{2,1,0:T(8,128)}, f32[1,512,2048]{2,1,0:T(8,128)}, f32[1,2048,5...) custom-call(bf16[4,2048,128]{2,1,0:T(8,128)(2,1)} %get-tuple-element, ...), custom_call_target="tpu_custom_call" | custom-call | tf_op jit(solution)/shard_map/pallas_call | solution.py:1549

commit v11 on v10

--- a/solution.py
+++ b/solution.py
@@ -520,6 +520,7 @@
         return pl.ds(pl.multiple_of(p * N + first, size), size)
 
     near = jnp.clip(w - core * B, 0, B - 1)
+    leading = jnp.where(lax.div(w, B) == core, near, B - 1 - near)
 
     weights = [
         pltpu.make_async_copy(src, dst, w_sem.at[n])
@@ -784,7 +785,7 @@
         later = lax.rem(me_s + 1, S)
 
         def turn(n, carry):
-            p = lax.rem(near + n, B)
+            p = lax.rem(leading + n, B)
             whole = at(p, 0, N)
             arrive(mb_r.at[whole], mb_rs.at[p])
             mean = mm(mb_r[whole, :], mo[...])

time: 454 us -> 459 us (1.011)
  Pallas kernels: 453 us -> 458 us
    pallas_call x1, Pallas kernels: 440 us -> 445 us  [run_relay(): pl.pallas_call(functools.partial(relay_kernel, dims), out_shape=(sds((BN,...]
where the time goes in v11:
time: 459 us; the launch traced here: 458 us
  Pallas kernels  458 us (100%)
    pallas_call x1, Pallas kernels, run_relay(): pl.pallas_call(functools.partial(relay_kernel, dims), out_shape=(sds((BN,...  445 us
    pallas_call x1, Pallas kernels, run_gradients(): pl.pallas_call(functools.partial(gradient_kernel, dims), out_shape=tuple(...  13.1 us

profile of v11, /device:TPU:0, one launch (start us, length us, event | category | flops | bytes accessed | tf_op | source)
XLA Modules:
  0.0 458.4 jit_solution(17541201190315560626)
XLA Ops:
  0.7 444.6 %shard_map.298 = (bf16[128,512]{1,0:T(8,128)(2,1)}, bf16[128,512]{1,0:T(8,128)(2,1)}, bf16[4,2048,128]{2,1,0:T(8,128)(2,1)}, bf16[4,128,1536]{2,1,0:T(8,128)(2,1...) custom-call(bf16[2,60,64,192]{3,2,1,0:T(8,128)(2,1)} %bitcast.28, ...), custom_call_target="tpu_custom_call" | custom-call | tf_op jit(solution)/shard_map/pallas_call | solution.py:1404
  445.2 13.1 %shard_map.299 = (f32[1,512,1024]{2,1,0:T(8,128)}, f32[1,192,512]{2,1,0:T(8,128)}, f32[1,512,512]{2,1,0:T(8,128)}, f32[1,512,2048]{2,1,0:T(8,128)}, f32[1,2048,5...) custom-call(bf16[4,2048,128]{2,1,0:T(8,128)(2,1)} %get-tuple-element, ...), custom_call_target="tpu_custom_call" | custom-call | tf_op jit(solution)/shard_map/pallas_call | solution.py:1550
